TPU v7x, 128 devices: a whole 4x4x4 slice. The times are simulated.
128 devices in a mesh: stream: 8 (over y, core), azim: 16 (over z, x).
Axes of the slice: x: 4, y: 4, z: 4, core: 2. Of those that a mesh axis runs over, the one named last changes fastest.
Arguments:
- fluid: float32 [4, 512, 512, 128], P(None, 'stream', 'azim'), may hold values from -4 to 4
- bubbles: float32 [65536, 5, 128], P(('stream', 'azim'))
- counts: int32 [128], P(('stream', 'azim')), may hold values from 128 to 512
- outgoing_block_order: int32 [65536], P(('stream', 'azim')), may hold values from 0 to 511, as said below
- tiles_first_update: int32 [65536], P(('stream', 'azim')), may hold values from 0 to 2047
- tiles_after: int32 [65536], P(('stream', 'azim')), may hold values from 0 to 2047
Outputs:
- fluid_out: float32 [4, 512, 512, 128], P(None, 'stream', 'azim')
- bubbles_out: float32 [65536, 5, 128], P(('stream', 'azim'))
- void_fraction: float32 [512, 512, 128], P('stream', 'azim')
Inputs may be any that keep to these rules, and one draw needn't show every extreme that they name: `outgoing_block_order`: for each device, its 512 entries are each of 0 to 511 once.
All inputs are finite; a program needn't handle non-finite values.
Results may differ from a plain program's by a relative error of at most 0.000076.
Values sent between devices are 32-bit elements; how exact they have to be, the bound alone decides.
No kernel may reach another device: no remote copies, remote signals or barrier semaphores. Data moves between devices by JAX's collectives and lax.ppermute only.
A program may use at most 128 MiB of HBM per device.

v0:
```python
import jax
import jax.numpy as jnp
from jax import lax
from jax.sharding import PartitionSpec as P

SUBSTEPS = 8


TIME_STEP = 0.25
MEAN_FLOW = 0.5
DIFFUSION = 0.1
KERNEL_WIDTH = 1.5
GAS_INDEX = 4.2
PRESSURE_COUPLING = 0.3
AMBIENT = 1.0
RELAX_TIME = 0.5
VISCOUS = 0.08
SOURCE_GAIN = 0.05
VOID_SCALE = 0.01
FOUR_PI = 12.566370614359172


def with_halo(cells, sides, width, closed):
    for axis, dim in sides:
        count = lax.axis_size(axis)
        ends = count if closed else count - 1
        head = lax.slice_in_dim(cells, 0, width, axis=dim)
        tail = lax.slice_in_dim(cells, cells.shape[dim] - width, cells.shape[dim], axis=dim)
        cells = jnp.concatenate(
            [
                lax.ppermute(tail, axis, [(i, (i + 1) % count) for i in range(ends)]),
                cells,
                lax.ppermute(head, axis, [((i + 1) % count, i) for i in range(ends)]),
            ],
            axis=dim,
        )
    return cells


def kernel_weights(position, cell_centres):
    offset = (position[:, :, None] - cell_centres) / KERNEL_WIDTH
    raw = jnp.exp(-0.5 * offset * offset)
    return raw / jnp.sum(raw, axis=-1, keepdims=True)


def advance_group(packed_blocks):
    bubble_state, tile_row_count, alive_flags = packed_blocks
    cell_centres = jnp.arange(tile_row_count.shape[-1], dtype=jnp.int32).astype(jnp.float32)
    weights = kernel_weights(bubble_state[:, 2], cell_centres)
    sampled = jnp.einsum("gbk,gck->gcb", weights, tile_row_count, precision=lax.Precision.HIGHEST)
    pressure = sampled[:, 0]
    velocity = sampled[:, 1]
    radius = bubble_state[:, 0]
    growth = bubble_state[:, 1]
    position = bubble_state[:, 2]
    bubble_speed = bubble_state[:, 3]
    rest_radius = bubble_state[:, 4]
    substep_size = TIME_STEP / SUBSTEPS
    for substep in range(SUBSTEPS):
        gas = jnp.exp(GAS_INDEX * jnp.log(rest_radius / radius))
        accel = (
            gas
            - AMBIENT
            - PRESSURE_COUPLING * pressure
            - 1.5 * growth * growth
            - VISCOUS * growth / radius
        ) / radius
        growth = growth + substep_size * accel
        radius = radius + substep_size * growth
        bubble_speed = bubble_speed + substep_size * (velocity - bubble_speed) / RELAX_TIME
        position = position + substep_size * bubble_speed
    new_state = jnp.stack([radius, growth, position, bubble_speed, rest_radius], axis=1)
    weights = kernel_weights(position, cell_centres)
    source_amounts = jnp.stack(
        [
            SOURCE_GAIN * FOUR_PI * radius * radius * growth,
            VOID_SCALE * FOUR_PI / 3.0 * radius * radius * radius,
        ],
        axis=1,
    )
    source_amounts = source_amounts * alive_flags[:, None, None]
    spread_sources = jnp.einsum(
        "gbk,gcb->gck", weights, source_amounts, precision=lax.Precision.HIGHEST
    )
    return (new_state, spread_sources)


def advance_every_group(bubble_state, tile_row_count, alive_flags):
    bubble_groups = bubble_state.shape[0] // 64
    new_state, spread_sources = lax.map(
        advance_group,
        (
            bubble_state.reshape((bubble_groups, 64) + bubble_state.shape[1:]),
            tile_row_count.reshape((bubble_groups, 64) + tile_row_count.shape[1:]),
            alive_flags.reshape(bubble_groups, 64),
        ),
    )
    return (new_state.reshape(bubble_state.shape), spread_sources.reshape(tile_row_count.shape))


def fluid_update(
    flow_field, stream_up, stream_down, azim_up, azim_down, radial_up, radial_down, source
):
    d_stream = 0.5 * (stream_up - stream_down)
    d_azim = 0.5 * (azim_up - azim_down)
    d_radial = 0.5 * (radial_up - radial_down)
    pressure_rate = -MEAN_FLOW * d_stream[0] - d_stream[1] - d_azim[2] - d_radial[3] - source
    stream_rate = -MEAN_FLOW * d_stream[1] - d_stream[0]
    azim_rate = -MEAN_FLOW * d_stream[2] - d_azim[0]
    radial_rate = -MEAN_FLOW * d_stream[3] - d_radial[0]
    change = jnp.stack([pressure_rate, stream_rate, azim_rate, radial_rate])
    laplace = (
        stream_up + stream_down + azim_up + azim_down + radial_up + radial_down - 6.0 * flow_field
    )
    return flow_field + TIME_STEP * change + DIFFUSION * laplace


def fluid_step(flow_field, source):
    stream_pad = with_halo(flow_field, (("stream", 1),), 1, False)
    azim_pad = with_halo(flow_field, (("azim", 2),), 1, True)
    radial_pad = jnp.pad(flow_field, ((0, 0), (0, 0), (0, 0), (1, 1)))
    return fluid_update(
        flow_field,
        stream_pad[:, 2:],
        stream_pad[:, :-2],
        azim_pad[:, :, 2:],
        azim_pad[:, :, :-2],
        radial_pad[..., 2:],
        radial_pad[..., :-2],
        source,
    )


def local_update(flow_field, bubble_state, tile_indices, alive_flags):
    selected = jnp.stack([flow_field[0], flow_field[3]]).reshape(2, -1, flow_field.shape[-1])
    tile_row_count = jnp.take(selected, tile_indices, axis=1).transpose(1, 0, 2)
    bubble_state, spread_sources = advance_every_group(bubble_state, tile_row_count, alive_flags)
    grid = jnp.zeros_like(selected).at[:, tile_indices].add(spread_sources.transpose(1, 0, 2))
    grid = grid.reshape((2,) + flow_field.shape[1:])
    return (fluid_step(flow_field, grid[0]), bubble_state, grid[1])


def on_device(fluid, bubbles, counts, outgoing_block_order, tiles_first_update, tiles_after):
    alive_flags = (jnp.arange(bubbles.shape[0], dtype=jnp.int32) < counts[0]).astype(jnp.float32)
    flow_field, bubble_state, void_before_update = local_update(
        fluid, bubbles, tiles_first_update, alive_flags
    )
    outgoing = jnp.take(bubble_state, outgoing_block_order, axis=0)
    outgoing_alive_flags = jnp.take(alive_flags, outgoing_block_order, axis=0)
    arrived, arrived_live = (
        lax.all_to_all(outgoing, ("stream", "azim"), split_axis=0, concat_axis=0, tiled=True),
        lax.all_to_all(
            outgoing_alive_flags, ("stream", "azim"), split_axis=0, concat_axis=0, tiled=True
        ),
    )
    flow_field, bubble_state, void_field = local_update(
        flow_field, arrived, tiles_after, arrived_live
    )
    return (flow_field, bubble_state * arrived_live[:, None, None], void_field)


def solution(mesh):
    return jax.shard_map(
        on_device,
        mesh=mesh,
        in_specs=(
            P(None, "stream", "azim", None),
            P(("stream", "azim"), None, None),
            P(("stream", "azim")),
            P(("stream", "azim")),
            P(("stream", "azim")),
            P(("stream", "azim")),
        ),
        out_specs=(
            P(None, "stream", "azim", None),
            P(("stream", "azim"), None, None),
            P("stream", "azim", None),
        ),
        check_vma=False,
    )
```

profile of v0, /device:TPU:1, one launch (start us, length us, event | category | flops | bytes accessed | tf_op | source)
XLA Modules:
  0.0 520.1 jit_solution(3948769978307189131)
XLA Ops:
  5.3 6.8 %collective-permute-start.2 = (f32[4,64,1,128]{3,1,2,0:T(8,128)S(1)}, f32[4,64,1,128]{3,1,2,0:T(8,128)S(1)}, u32[]{:S(2)}, u32[]{:S(2)}) collective-permute-start(f32[4,64,1,128]{3,1,2,0:T(8,128)S(1)} %get-tuple-element.382), channel_id=1, source_target_pairs={{1,0},{2,1},{3,2},{4,3},{5,4},{6,5},{7,6},{8,7},{9,8},{10,9},{11,1... | collective-permute-start | bytes 393224 | tf_op jit(solution)/shard_map/ppermute | solution.py:33
  24.0 8.9 %all-to-all-start.1 = ((f32[128,4,1]{1,2,0:T(1,128)}), f32[128,4,1]{1,2,0:T(1,128)S(1)}, u32[]{:S(2)}, u32[]{:S(2)}) async-start(f32[128,4,1]{1,2,0:T(1,128)} %bitcast.48), calls=%async_computation.1 | async-start | bytes 131072 | tf_op jit(solution)/shard_map/all_to_all | solution.py:152
  41.0 163.4 %while.30 = (s32[]{:T(128)}, f32[8,64,5,128]{3,1,0,2:T(8,128)S(1)}, f32[8,64,2,128]{3,2,1,0:T(2,128)S(1)}, f32[8,64,5,128]{3,1,0,2:T(8,128)}, f32[8,64,2,128]{3,...) while((s32[]{:T(128)}, f32[8,64,5,128]{3,1,0,2:T(8,128)S(1)}, f32[8,64,2,128]{3,2,1,0:T(2,128)S(1)}, ...), condition=%wide.region_3.5_spmd, body=%wide.region_0.4_spmd.sunk | while | flops 73212032 | bytes 2329953 | solution.py:90
  44.3 8.3 %fusion.208 = f32[64,2,128]{2,1,0:T(2,128)S(1)} fusion(f32[64,128]{1,0:T(8,128)S(1)} %fusion.207, f32[128]{0:T(128)S(1)} %iota_convert_fusion.4, f32[64,128]{1,0:T(8,128)S(1)} %slice_bitcast_fusion.4, f32[8,64,2,128]{3,2,1,0:T(2,128)S(1)} %get-tuple-element.507, s32[]{:T(128)} %get-tuple-element.496), kind=kOutput, calls=%fused_computation.19.clone.1 | convolution fusion | flops 30408704 | bytes 197124 | tf_op jit(solution)/shard_map/while/body/eval_jaxpr/gbk,gck->gcb/dot_general | solution.py:50
  64.7 8.3 %fusion.208 = f32[64,2,128]{2,1,0:T(2,128)S(1)} fusion(f32[64,128]{1,0:T(8,128)S(1)} %fusion.207, f32[128]{0:T(128)S(1)} %iota_convert_fusion.4, f32[64,128]{1,0:T(8,128)S(1)} %slice_bitcast_fusion.4, f32[8,64,2,128]{3,2,1,0:T(2,128)S(1)} %get-tuple-element.507, s32[]{:T(128)} %get-tuple-element.496), kind=kOutput, calls=%fused_computation.19.clone.1 | convolution fusion | flops 30408704 | bytes 197124 | tf_op jit(solution)/shard_map/while/body/eval_jaxpr/gbk,gck->gcb/dot_general | solution.py:50
  76.0 5.7 %fusion.214 = f32[8,64,2,128]{3,2,1,0:T(2,128)S(1)} fusion(f32[8,64,2,128]{3,2,1,0:T(2,128)S(1)} %get-tuple-element.498, s32[]{:T(128)} %get-tuple-element.496, f32[64,128]{1,0:T(8,128)S(1)} %fusion.212, f32[64,128]{1,0:T(8,128)S(1)} %multiply_add_fusion.38, f32[128]{0:T(128)S(1)} %iota_convert_fusion.4, f32[64,2,128]{2,0,1:T(8,128)S(1)} %maximum_multiply_fusion.6), kind=kOutput, calls=%fused_computation.31.clone.1 | convolution fusion | flops 30408704 | bytes 197124 | tf_op jit(solution)/shard_map/while/body/eval_jaxpr/gbk,gcb->gck/dot_general | solution.py:82
  85.2 8.3 %fusion.208 = f32[64,2,128]{2,1,0:T(2,128)S(1)} fusion(f32[64,128]{1,0:T(8,128)S(1)} %fusion.207, f32[128]{0:T(128)S(1)} %iota_convert_fusion.4, f32[64,128]{1,0:T(8,128)S(1)} %slice_bitcast_fusion.4, f32[8,64,2,128]{3,2,1,0:T(2,128)S(1)} %get-tuple-element.507, s32[]{:T(128)} %get-tuple-element.496), kind=kOutput, calls=%fused_computation.19.clone.1 | convolution fusion | flops 30408704 | bytes 197124 | tf_op jit(solution)/shard_map/while/body/eval_jaxpr/gbk,gck->gcb/dot_general | solution.py:50
  105.6 8.3 %fusion.208 = f32[64,2,128]{2,1,0:T(2,128)S(1)} fusion(f32[64,128]{1,0:T(8,128)S(1)} %fusion.207, f32[128]{0:T(128)S(1)} %iota_convert_fusion.4, f32[64,128]{1,0:T(8,128)S(1)} %slice_bitcast_fusion.4, f32[8,64,2,128]{3,2,1,0:T(2,128)S(1)} %get-tuple-element.507, s32[]{:T(128)} %get-tuple-element.496), kind=kOutput, calls=%fused_computation.19.clone.1 | convolution fusion | flops 30408704 | bytes 197124 | tf_op jit(solution)/shard_map/while/body/eval_jaxpr/gbk,gck->gcb/dot_general | solution.py:50
  116.8 5.7 %fusion.214 = f32[8,64,2,128]{3,2,1,0:T(2,128)S(1)} fusion(f32[8,64,2,128]{3,2,1,0:T(2,128)S(1)} %get-tuple-element.498, s32[]{:T(128)} %get-tuple-element.496, f32[64,128]{1,0:T(8,128)S(1)} %fusion.212, f32[64,128]{1,0:T(8,128)S(1)} %multiply_add_fusion.38, f32[128]{0:T(128)S(1)} %iota_convert_fusion.4, f32[64,2,128]{2,0,1:T(8,128)S(1)} %maximum_multiply_fusion.6), kind=kOutput, calls=%fused_computation.31.clone.1 | convolution fusion | flops 30408704 | bytes 197124 | tf_op jit(solution)/shard_map/while/body/eval_jaxpr/gbk,gcb->gck/dot_general | solution.py:82
  126.0 8.3 %fusion.208 = f32[64,2,128]{2,1,0:T(2,128)S(1)} fusion(f32[64,128]{1,0:T(8,128)S(1)} %fusion.207, f32[128]{0:T(128)S(1)} %iota_convert_fusion.4, f32[64,128]{1,0:T(8,128)S(1)} %slice_bitcast_fusion.4, f32[8,64,2,128]{3,2,1,0:T(2,128)S(1)} %get-tuple-element.507, s32[]{:T(128)} %get-tuple-element.496), kind=kOutput, calls=%fused_computation.19.clone.1 | convolution fusion | flops 30408704 | bytes 197124 | tf_op jit(solution)/shard_map/while/body/eval_jaxpr/gbk,gck->gcb/dot_general | solution.py:50
  137.2 5.7 %fusion.214 = f32[8,64,2,128]{3,2,1,0:T(2,128)S(1)} fusion(f32[8,64,2,128]{3,2,1,0:T(2,128)S(1)} %get-tuple-element.498, s32[]{:T(128)} %get-tuple-element.496, f32[64,128]{1,0:T(8,128)S(1)} %fusion.212, f32[64,128]{1,0:T(8,128)S(1)} %multiply_add_fusion.38, f32[128]{0:T(128)S(1)} %iota_convert_fusion.4, f32[64,2,128]{2,0,1:T(8,128)S(1)} %maximum_multiply_fusion.6), kind=kOutput, calls=%fused_computation.31.clone.1 | convolution fusion | flops 30408704 | bytes 197124 | tf_op jit(solution)/shard_map/while/body/eval_jaxpr/gbk,gcb->gck/dot_general | solution.py:82
  146.4 8.3 %fusion.208 = f32[64,2,128]{2,1,0:T(2,128)S(1)} fusion(f32[64,128]{1,0:T(8,128)S(1)} %fusion.207, f32[128]{0:T(128)S(1)} %iota_convert_fusion.4, f32[64,128]{1,0:T(8,128)S(1)} %slice_bitcast_fusion.4, f32[8,64,2,128]{3,2,1,0:T(2,128)S(1)} %get-tuple-element.507, s32[]{:T(128)} %get-tuple-element.496), kind=kOutput, calls=%fused_computation.19.clone.1 | convolution fusion | flops 30408704 | bytes 197124 | tf_op jit(solution)/shard_map/while/body/eval_jaxpr/gbk,gck->gcb/dot_general | solution.py:50
  166.8 8.3 %fusion.208 = f32[64,2,128]{2,1,0:T(2,128)S(1)} fusion(f32[64,128]{1,0:T(8,128)S(1)} %fusion.207, f32[128]{0:T(128)S(1)} %iota_convert_fusion.4, f32[64,128]{1,0:T(8,128)S(1)} %slice_bitcast_fusion.4, f32[8,64,2,128]{3,2,1,0:T(2,128)S(1)} %get-tuple-element.507, s32[]{:T(128)} %get-tuple-element.496), kind=kOutput, calls=%fused_computation.19.clone.1 | convolution fusion | flops 30408704 | bytes 197124 | tf_op jit(solution)/shard_map/while/body/eval_jaxpr/gbk,gck->gcb/dot_general | solution.py:50
  178.1 5.7 %fusion.214 = f32[8,64,2,128]{3,2,1,0:T(2,128)S(1)} fusion(f32[8,64,2,128]{3,2,1,0:T(2,128)S(1)} %get-tuple-element.498, s32[]{:T(128)} %get-tuple-element.496, f32[64,128]{1,0:T(8,128)S(1)} %fusion.212, f32[64,128]{1,0:T(8,128)S(1)} %multiply_add_fusion.38, f32[128]{0:T(128)S(1)} %iota_convert_fusion.4, f32[64,2,128]{2,0,1:T(8,128)S(1)} %maximum_multiply_fusion.6), kind=kOutput, calls=%fused_computation.31.clone.1 | convolution fusion | flops 30408704 | bytes 197124 | tf_op jit(solution)/shard_map/while/body/eval_jaxpr/gbk,gcb->gck/dot_general | solution.py:82
  187.2 8.3 %fusion.208 = f32[64,2,128]{2,1,0:T(2,128)S(1)} fusion(f32[64,128]{1,0:T(8,128)S(1)} %fusion.207, f32[128]{0:T(128)S(1)} %iota_convert_fusion.4, f32[64,128]{1,0:T(8,128)S(1)} %slice_bitcast_fusion.4, f32[8,64,2,128]{3,2,1,0:T(2,128)S(1)} %get-tuple-element.507, s32[]{:T(128)} %get-tuple-element.496), kind=kOutput, calls=%fused_computation.19.clone.1 | convolution fusion | flops 30408704 | bytes 197124 | tf_op jit(solution)/shard_map/while/body/eval_jaxpr/gbk,gck->gcb/dot_general | solution.py:50
  198.5 5.7 %fusion.214 = f32[8,64,2,128]{3,2,1,0:T(2,128)S(1)} fusion(f32[8,64,2,128]{3,2,1,0:T(2,128)S(1)} %get-tuple-element.498, s32[]{:T(128)} %get-tuple-element.496, f32[64,128]{1,0:T(8,128)S(1)} %fusion.212, f32[64,128]{1,0:T(8,128)S(1)} %multiply_add_fusion.38, f32[128]{0:T(128)S(1)} %iota_convert_fusion.4, f32[64,2,128]{2,0,1:T(8,128)S(1)} %maximum_multiply_fusion.6), kind=kOutput, calls=%fused_computation.31.clone.1 | convolution fusion | flops 30408704 | bytes 197124 | tf_op jit(solution)/shard_map/while/body/eval_jaxpr/gbk,gcb->gck/dot_general | solution.py:82
  213.1 16.7 %scatter_fusion = f32[2,2048,128]{2,0,1:T(2,128)S(1)} fusion(f32[2,2048,128]{2,0,1:T(2,128)S(1)} %broadcast.1542.clone, s32[512]{0:T(512)S(1)} %compare_select_fusion.2, f32[512,2,128]{2,1,0:T(2,128)S(1)} %bitcast.161), kind=kCustom, calls=%fused_computation.4 | custom fusion | flops 131072 | bytes 1574912 | tf_op jit(solution)/shard_map/scatter-add | solution.py:138
  231.6 10.2 %all-to-all-start = ((f32[512,5,128]{2,1,0:T(8,128)}), f32[512,5,128]{2,1,0:T(8,128)}, u32[]{:S(2)}, u32[]{:S(2)}) async-start(f32[512,5,128]{2,1,0:T(8,128)} %broadcast_select_fusion), calls=%async_computation | async-start | bytes 4194304 | tf_op jit(solution)/shard_map/all_to_all | solution.py:151
  244.0 13.0 %subtract_multiply_fusion.12 = (f32[4,64,32,128]{3,1,2,0:T(8,128)S(1)}, f32[4,64,32,128]{3,1,2,0:T(8,128)S(1)}, f32[4,64,32,128]{3,1,2,0:T(8,128)S(1)}) fusion(f32[4,64,1,128]{3,1,2,0:T(8,128)S(1)} %collective-permute-done.2, f32[4,64,32,128]{3,1,2,0:T(8,128)} %copy-done.2, f32[4,64,1,128]{3,1,2,0:T(8,128)S(1)} %collective-permute-done.3, ...), kind=kLoop, calls=%fused_computation.262 | loop fusion | flops 10485760 | bytes 17170432 | tf_op jit(solution)/shard_map/mul | solution.py:105
  285.0 15.8 %subtract_multiply_fusion.9 = (f32[4,64,32,128]{3,1,2,0:T(8,128)}, f32[4,64,32,128]{3,1,2,0:T(8,128)}, f32[4,64,32,128]{3,1,2,0:T(8,128)}) fusion(f32[4,64,1,128]{3,1,2,0:T(8,128)S(1)} %collective-permute-done.6, f32[4,64,32,128]{3,1,2,0:T(8,128)} %copy-done, f32[4,64,1,128]{3,1,2,0:T(8,128)S(1)} %collective-permute-done.7, ...), kind=kLoop, calls=%fused_computation.259 | loop fusion | flops 10485760 | bytes 17170432 | tf_op jit(solution)/shard_map/mul | solution.py:105
  303.0 167.2 %while.31 = (s32[]{:T(128)}, f32[8,64,5,128]{3,1,0,2:T(8,128)S(1)}, f32[8,64,2,128]{3,2,1,0:T(2,128)S(1)}, f32[8,64,5,128]{3,1,2,0:T(8,128)S(1)}, f32[8,64,2,128]{3,2,1,0:T(2,128)}, /*index=5*/f32[8,64]{1,0:T(8,128)}, s32[]{:T(128)}) while((s32[]{:T(128)}, f32[8,64,5,128]{3,1,0,2:T(8,128)S(1)}, f32[8,64,2,128]{3,2,1,0:T(2,128)S(1)}, ...), condition=%wide.region_8.10_spmd, body=%wide.region_5.9_spmd.sunk | while | flops 73212032 | bytes 2330461 | solution.py:90
  305.4 9.1 %fusion.220 = f32[64,2,128]{2,1,0:T(2,128)S(1)} fusion(f32[64,128]{1,0:T(8,128)S(1)} %fusion.219, f32[128]{0:T(128)S(1)} %iota_convert_fusion.5, f32[64,128]{1,0:T(8,128)S(1)} %slice_bitcast_fusion.5, f32[8,64,2,128]{3,2,1,0:T(2,128)} %get-tuple-element.528, s32[]{:T(128)} %get-tuple-element.517), kind=kOutput, calls=%fused_computation.136.clone.1 | convolution fusion | flops 30408704 | bytes 197632 | tf_op jit(solution)/shard_map/while/body/eval_jaxpr/gbk,gck->gcb/dot_general | solution.py:50
  326.3 9.1 %fusion.220 = f32[64,2,128]{2,1,0:T(2,128)S(1)} fusion(f32[64,128]{1,0:T(8,128)S(1)} %fusion.219, f32[128]{0:T(128)S(1)} %iota_convert_fusion.5, f32[64,128]{1,0:T(8,128)S(1)} %slice_bitcast_fusion.5, f32[8,64,2,128]{3,2,1,0:T(2,128)} %get-tuple-element.528, s32[]{:T(128)} %get-tuple-element.517), kind=kOutput, calls=%fused_computation.136.clone.1 | convolution fusion | flops 30408704 | bytes 197632 | tf_op jit(solution)/shard_map/while/body/eval_jaxpr/gbk,gck->gcb/dot_general | solution.py:50
  338.9 5.7 %fusion.226 = f32[8,64,2,128]{3,2,1,0:T(2,128)S(1)} fusion(f32[8,64,2,128]{3,2,1,0:T(2,128)S(1)} %get-tuple-element.519, s32[]{:T(128)} %get-tuple-element.517, f32[64,128]{1,0:T(8,128)S(1)} %fusion.224, f32[64,128]{1,0:T(8,128)S(1)} %multiply_add_fusion.39, f32[128]{0:T(128)S(1)} %iota_convert_fusion.5, f32[64,2,128]{2,0,1:T(8,128)S(1)} %maximum_multiply_fusion.7), kind=kOutput, calls=%fused_computation.148.clone.1 | convolution fusion | flops 30408704 | bytes 197124 | tf_op jit(solution)/shard_map/while/body/eval_jaxpr/gbk,gcb->gck/dot_general | solution.py:82
  347.2 9.1 %fusion.220 = f32[64,2,128]{2,1,0:T(2,128)S(1)} fusion(f32[64,128]{1,0:T(8,128)S(1)} %fusion.219, f32[128]{0:T(128)S(1)} %iota_convert_fusion.5, f32[64,128]{1,0:T(8,128)S(1)} %slice_bitcast_fusion.5, f32[8,64,2,128]{3,2,1,0:T(2,128)} %get-tuple-element.528, s32[]{:T(128)} %get-tuple-element.517), kind=kOutput, calls=%fused_computation.136.clone.1 | convolution fusion | flops 30408704 | bytes 197632 | tf_op jit(solution)/shard_map/while/body/eval_jaxpr/gbk,gck->gcb/dot_general | solution.py:50
  359.8 5.7 %fusion.226 = f32[8,64,2,128]{3,2,1,0:T(2,128)S(1)} fusion(f32[8,64,2,128]{3,2,1,0:T(2,128)S(1)} %get-tuple-element.519, s32[]{:T(128)} %get-tuple-element.517, f32[64,128]{1,0:T(8,128)S(1)} %fusion.224, f32[64,128]{1,0:T(8,128)S(1)} %multiply_add_fusion.39, f32[128]{0:T(128)S(1)} %iota_convert_fusion.5, f32[64,2,128]{2,0,1:T(8,128)S(1)} %maximum_multiply_fusion.7), kind=kOutput, calls=%fused_computation.148.clone.1 | convolution fusion | flops 30408704 | bytes 197124 | tf_op jit(solution)/shard_map/while/body/eval_jaxpr/gbk,gcb->gck/dot_general | solution.py:82
  368.1 9.1 %fusion.220 = f32[64,2,128]{2,1,0:T(2,128)S(1)} fusion(f32[64,128]{1,0:T(8,128)S(1)} %fusion.219, f32[128]{0:T(128)S(1)} %iota_convert_fusion.5, f32[64,128]{1,0:T(8,128)S(1)} %slice_bitcast_fusion.5, f32[8,64,2,128]{3,2,1,0:T(2,128)} %get-tuple-element.528, s32[]{:T(128)} %get-tuple-element.517), kind=kOutput, calls=%fused_computation.136.clone.1 | convolution fusion | flops 30408704 | bytes 197632 | tf_op jit(solution)/shard_map/while/body/eval_jaxpr/gbk,gck->gcb/dot_general | solution.py:50
  389.0 9.1 %fusion.220 = f32[64,2,128]{2,1,0:T(2,128)S(1)} fusion(f32[64,128]{1,0:T(8,128)S(1)} %fusion.219, f32[128]{0:T(128)S(1)} %iota_convert_fusion.5, f32[64,128]{1,0:T(8,128)S(1)} %slice_bitcast_fusion.5, f32[8,64,2,128]{3,2,1,0:T(2,128)} %get-tuple-element.528, s32[]{:T(128)} %get-tuple-element.517), kind=kOutput, calls=%fused_computation.136.clone.1 | convolution fusion | flops 30408704 | bytes 197632 | tf_op jit(solution)/shard_map/while/body/eval_jaxpr/gbk,gck->gcb/dot_general | solution.py:50
  409.9 9.1 %fusion.220 = f32[64,2,128]{2,1,0:T(2,128)S(1)} fusion(f32[64,128]{1,0:T(8,128)S(1)} %fusion.219, f32[128]{0:T(128)S(1)} %iota_convert_fusion.5, f32[64,128]{1,0:T(8,128)S(1)} %slice_bitcast_fusion.5, f32[8,64,2,128]{3,2,1,0:T(2,128)} %get-tuple-element.528, s32[]{:T(128)} %get-tuple-element.517), kind=kOutput, calls=%fused_computation.136.clone.1 | convolution fusion | flops 30408704 | bytes 197632 | tf_op jit(solution)/shard_map/while/body/eval_jaxpr/gbk,gck->gcb/dot_general | solution.py:50
  430.8 9.1 %fusion.220 = f32[64,2,128]{2,1,0:T(2,128)S(1)} fusion(f32[64,128]{1,0:T(8,128)S(1)} %fusion.219, f32[128]{0:T(128)S(1)} %iota_convert_fusion.5, f32[64,128]{1,0:T(8,128)S(1)} %slice_bitcast_fusion.5, f32[8,64,2,128]{3,2,1,0:T(2,128)} %get-tuple-element.528, s32[]{:T(128)} %get-tuple-element.517), kind=kOutput, calls=%fused_computation.136.clone.1 | convolution fusion | flops 30408704 | bytes 197632 | tf_op jit(solution)/shard_map/while/body/eval_jaxpr/gbk,gck->gcb/dot_general | solution.py:50
  451.7 9.1 %fusion.220 = f32[64,2,128]{2,1,0:T(2,128)S(1)} fusion(f32[64,128]{1,0:T(8,128)S(1)} %fusion.219, f32[128]{0:T(128)S(1)} %iota_convert_fusion.5, f32[64,128]{1,0:T(8,128)S(1)} %slice_bitcast_fusion.5, f32[8,64,2,128]{3,2,1,0:T(2,128)} %get-tuple-element.528, s32[]{:T(128)} %get-tuple-element.517), kind=kOutput, calls=%fused_computation.136.clone.1 | convolution fusion | flops 30408704 | bytes 197632 | tf_op jit(solution)/shard_map/while/body/eval_jaxpr/gbk,gck->gcb/dot_general | solution.py:50
  471.6 32.1 %scatter_fusion.1 = f32[2,2048,128]{2,0,1:T(2,128)S(1)} fusion(f32[2,2048,128]{2,0,1:T(2,128)S(1)} %broadcast.1542, s32[512]{0:T(512)S(1)} %compare_select_fusion.1, f32[512,2,128]{2,1,0:T(2,128)} %bitcast.162), kind=kCustom, calls=%fused_computation.5 | custom fusion | flops 131072 | bytes 1574912 | tf_op jit(solution)/shard_map/scatter-add | solution.py:138
  (372 shorter events, 233.3 us)
Async XLA Ops:
  0.6 19.1 %copy-start.18 = (s32[512]{0:T(512)S(1)}, s32[512]{0:T(512)}, u32[]{:S(2)}) copy-start(s32[512]{0:T(512)} %param.15) | copy-start | bytes 6148
  5.3 14.5 %copy-start.2 = (f32[4,64,32,128]{3,1,2,0:T(8,128)}, f32[4,64,32,128]{3,1,2,0:T(8,128)S(1)}, u32[]{:S(2)}) copy-start(f32[4,64,32,128]{3,1,2,0:T(8,128)S(1)} %copy.117) | copy-start | bytes 12582916
  5.3 29.4 %copy-start.16 = (s32[512]{0:T(512)S(1)}, s32[512]{0:T(512)}, u32[]{:S(2)}) copy-start(s32[512]{0:T(512)} %param.16) | copy-start | bytes 6148
  5.3 238.6 %collective-permute-start.2 = (f32[4,64,1,128]{3,1,2,0:T(8,128)S(1)}, f32[4,64,1,128]{3,1,2,0:T(8,128)S(1)}, u32[]{:S(2)}, u32[]{:S(2)}) collective-permute-start(f32[4,64,1,128]{3,1,2,0:T(8,128)S(1)} %get-tuple-element.382), channel_id=1, source_target_pairs={{1,0},{2,1},{3,2},{4,3},{5,4},{6,5},{7,6},{8,7},{9,8},{10,9},{11,1... | collective-permute-start | bytes 393224 | tf_op jit(solution)/shard_map/ppermute | solution.py:33
  12.2 231.8 %collective-permute-start.3 = (f32[4,64,1,128]{3,1,2,0:T(8,128)S(1)}, f32[4,64,1,128]{3,1,2,0:T(8,128)S(1)}, u32[]{:S(2)}, u32[]{:S(2)}) collective-permute-start(f32[4,64,1,128]{3,1,2,0:T(8,128)S(1)} %get-tuple-element.381), channel_id=1, source_target_pairs={{0,1},{1,2},{2,3},{3,4},{4,5},{5,6},{6,7},{7,8},{8,9},{9,10},{10,1... | collective-permute-start | bytes 393224 | tf_op jit(solution)/shard_map/ppermute | solution.py:31
  13.1 230.9 %collective-permute-start = (f32[4,1,32,128]{3,1,2,0:T(1,128)S(1)}, f32[4,1,32,128]{3,1,2,0:T(1,128)S(1)}, u32[]{:S(2)}, u32[]{:S(2)}) collective-permute-start(f32[4,1,32,128]{3,1,2,0:T(1,128)S(1)} %bitcast.171), channel_id=1, source_target_pairs={{16,0},{32,16},{48,32},{64,48},{80,64},{96,80},{112,96},{17,1},{33... | collective-permute-start | bytes 196616 | tf_op jit(solution)/shard_map/ppermute | solution.py:33
  15.9 228.0 %collective-permute-start.1 = (f32[4,1,32,128]{3,1,2,0:T(1,128)S(1)}, f32[4,1,32,128]{3,1,2,0:T(1,128)S(1)}, u32[]{:S(2)}, u32[]{:S(2)}) collective-permute-start(f32[4,1,32,128]{3,1,2,0:T(1,128)S(1)} %bitcast.170), channel_id=1, source_target_pairs={{0,16},{16,32},{32,48},{48,64},{64,80},{80,96},{96,112},{1,17},{17... | collective-permute-start | bytes 196616 | tf_op jit(solution)/shard_map/ppermute | solution.py:31
  24.0 207.6 %all-to-all-start.1 = ((f32[128,4,1]{1,2,0:T(1,128)}), f32[128,4,1]{1,2,0:T(1,128)S(1)}, u32[]{:S(2)}, u32[]{:S(2)}) async-start(f32[128,4,1]{1,2,0:T(1,128)} %bitcast.48), calls=%async_computation.1 | async-start | bytes 131072 | tf_op jit(solution)/shard_map/all_to_all | solution.py:152
  41.0 163.4 %copy-start.17 = (s32[512]{0:T(512)S(1)}, s32[512]{0:T(512)}, u32[]{:S(2)}) copy-start(s32[512]{0:T(512)} %param.17) | copy-start | bytes 6148
  231.6 69.3 %all-to-all-start = ((f32[512,5,128]{2,1,0:T(8,128)}), f32[512,5,128]{2,1,0:T(8,128)}, u32[]{:S(2)}, u32[]{:S(2)}) async-start(f32[512,5,128]{2,1,0:T(8,128)} %broadcast_select_fusion), calls=%async_computation | async-start | bytes 4194304 | tf_op jit(solution)/shard_map/all_to_all | solution.py:151
  243.9 13.1 %copy-start.10 = (f32[4,1,32,128]{3,1,2,0:T(1,128)}, f32[4,1,32,128]{3,1,2,0:T(1,128)S(1)}, u32[]{:S(2)}) copy-start(f32[4,1,32,128]{3,1,2,0:T(1,128)S(1)} %collective-permute-done) | copy-start | bytes 196612
  243.9 13.1 %copy-start.11 = (f32[4,1,32,128]{3,1,2,0:T(1,128)}, f32[4,1,32,128]{3,1,2,0:T(1,128)S(1)}, u32[]{:S(2)}) copy-start(f32[4,1,32,128]{3,1,2,0:T(1,128)S(1)} %collective-permute-done.1) | copy-start | bytes 196612
  244.0 13.1 %copy-start.6 = (f32[4,64,1,128]{3,1,2,0:T(8,128)}, f32[4,64,1,128]{3,1,2,0:T(8,128)S(1)}, u32[]{:S(2)}) copy-start(f32[4,64,1,128]{3,1,2,0:T(8,128)S(1)} %collective-permute-done.2) | copy-start | bytes 393220
  244.0 13.1 %copy-start.7 = (f32[4,64,1,128]{3,1,2,0:T(8,128)}, f32[4,64,1,128]{3,1,2,0:T(8,128)S(1)}, u32[]{:S(2)}) copy-start(f32[4,64,1,128]{3,1,2,0:T(8,128)S(1)} %collective-permute-done.3) | copy-start | bytes 393220
  257.1 4.1 copy-start.3
  266.7 7.6 %copy-start = (f32[4,64,32,128]{3,1,2,0:T(8,128)}, f32[4,64,32,128]{3,1,2,0:T(8,128)S(1)}, u32[]{:S(2)}) copy-start(f32[4,64,32,128]{3,1,2,0:T(8,128)S(1)} %fusion.161) | copy-start | bytes 12582916
  266.9 15.6 %copy-start.19 = (pred[512]{0:T(512)(128)(4,1)S(1)}, pred[512]{0:T(512)(128)(4,1)}, u32[]{:S(2)}) copy-start(pred[512]{0:T(512)(128)(4,1)} %compare_and_fusion) | copy-start | bytes 1540
  268.8 16.2 %collective-permute-start.6 = (f32[4,64,1,128]{3,1,2,0:T(8,128)S(1)}, f32[4,64,1,128]{3,1,2,0:T(8,128)S(1)}, u32[]{:S(2)}, u32[]{:S(2)}) collective-permute-start(f32[4,64,1,128]{3,1,2,0:T(8,128)S(1)} %get-tuple-element.372), channel_id=1, source_target_pairs={{1,0},{2,1},{3,2},{4,3},{5,4},{6,5},{7,6},{8,7},{9,8},{10,9},{11,1... | collective-permute-start | bytes 393224 | tf_op jit(solution)/shard_map/ppermute | solution.py:33
  274.3 10.8 %collective-permute-start.7 = (f32[4,64,1,128]{3,1,2,0:T(8,128)S(1)}, f32[4,64,1,128]{3,1,2,0:T(8,128)S(1)}, u32[]{:S(2)}, u32[]{:S(2)}) collective-permute-start(f32[4,64,1,128]{3,1,2,0:T(8,128)S(1)} %get-tuple-element.371), channel_id=1, source_target_pairs={{0,1},{1,2},{2,3},{3,4},{4,5},{5,6},{6,7},{7,8},{8,9},{9,10},{10,1... | collective-permute-start | bytes 393224 | tf_op jit(solution)/shard_map/ppermute | solution.py:31
  274.4 10.6 %collective-permute-start.4 = (f32[4,1,32,128]{3,1,2,0:T(1,128)S(1)}, f32[4,1,32,128]{3,1,2,0:T(1,128)S(1)}, u32[]{:S(2)}, u32[]{:S(2)}) collective-permute-start(f32[4,1,32,128]{3,1,2,0:T(1,128)S(1)} %get-tuple-element.374), channel_id=1, source_target_pairs={{16,0},{32,16},{48,32},{64,48},{80,64},{96,80},{112,96},{17,1},{33... | collective-permute-start | bytes 196616 | tf_op jit(solution)/shard_map/ppermute | solution.py:33
  276.9 8.1 %collective-permute-start.5 = (f32[4,1,32,128]{3,1,2,0:T(1,128)S(1)}, f32[4,1,32,128]{3,1,2,0:T(1,128)S(1)}, u32[]{:S(2)}, u32[]{:S(2)}) collective-permute-start(f32[4,1,32,128]{3,1,2,0:T(1,128)S(1)} %get-tuple-element.373), channel_id=1, source_target_pairs={{0,16},{16,32},{32,48},{48,64},{64,80},{80,96},{96,112},{1,17},{17... | collective-permute-start | bytes 196616 | tf_op jit(solution)/shard_map/ppermute | solution.py:31
  285.0 15.8 %copy-start.12 = (f32[4,1,32,128]{3,1,2,0:T(1,128)}, f32[4,1,32,128]{3,1,2,0:T(1,128)S(1)}, u32[]{:S(2)}) copy-start(f32[4,1,32,128]{3,1,2,0:T(1,128)S(1)} %collective-permute-done.4) | copy-start | bytes 196612
  285.0 15.8 %copy-start.14 = (f32[4,1,32,128]{3,1,2,0:T(1,128)}, f32[4,1,32,128]{3,1,2,0:T(1,128)S(1)}, u32[]{:S(2)}) copy-start(f32[4,1,32,128]{3,1,2,0:T(1,128)S(1)} %collective-permute-done.5) | copy-start | bytes 196612
  285.0 15.8 %copy-start.8 = (f32[4,64,1,128]{3,1,2,0:T(8,128)}, f32[4,64,1,128]{3,1,2,0:T(8,128)S(1)}, u32[]{:S(2)}) copy-start(f32[4,64,1,128]{3,1,2,0:T(8,128)S(1)} %collective-permute-done.7) | copy-start | bytes 393220
  470.2 0.8 copy-start.5
  503.7 2.6 copy-start.4
  506.3 3.7 copy-start.1
  506.3 3.7 copy-start.9
  506.3 3.7 copy-start.13
  506.4 3.7 copy-start.15
where the time goes:
time: 528 us; the launch traced here: 520 us
  matrix products  230 us (44%)
  other arithmetic  189 us (36%)
  local copies, waits for them, and re-layouts  53.8 us (10%)
  starting transfers between devices  43.1 us (8%)
    dot_general x16, matrix products, advance_group(): jnp.einsum('gbk,gck->gcb', weights, tile_row_count, precision=lax.Precisi...  139 us
    dot_general x16, matrix products, advance_group(): jnp.einsum('gbk,gcb->gck', weights, source_amounts, precision=lax.Precisi...  90.8 us
    reduce_sum x32, other arithmetic, kernel_weights(): return raw / jnp.sum(raw, axis=-1, keepdims=True)  75.5 us
    scatter-add x2, other arithmetic, local_update(): jnp.zeros_like(selected).at[:, tile_indices]  48.8 us
    mul x2, other arithmetic, fluid_update(): d_azim = 0.5 * (azim_up - azim_down)  28.8 us
    ppermute x4, starting transfers between devices, with_halo(): lax.ppermute(head, axis, [((i + 1) % count, i) for i in range(ends)])  17.7 us
  transfers between devices with their start and end apart: 10, of which 0 were waited for; matrix products, arithmetic and copies ran while one was open for 48% of the time, Pallas kernels for 0%

commit v1 on v0

v1 whole, which is shorter than its diff:
```python
import functools

import jax
import jax.numpy as jnp
from jax import lax
from jax.experimental import pallas as pl
from jax.experimental.pallas import tpu as pltpu
from jax.sharding import PartitionSpec as P

SUBSTEPS = 8
TIME_STEP = 0.25
MEAN_FLOW = 0.5
DIFFUSION = 0.1
KERNEL_WIDTH = 1.5
GAS_INDEX = 4.2
PRESSURE_COUPLING = 0.3
AMBIENT = 1.0
RELAX_TIME = 0.5
VISCOUS = 0.08
SOURCE_GAIN = 0.05
VOID_SCALE = 0.01
FOUR_PI = 12.566370614359172
LOG2_E = 1.4426950408889634

CR = 128
BB = 128
NBLK = 512
COMPS = 5
CAP = 4
PACK = 24
GROUP = 8
CHUNK = 64
SHARP = 0.5 / (KERNEL_WIDTH * KERNEL_WIDTH) * LOG2_E
VMEM = pltpu.VMEM
SMEM = pltpu.SMEM


def split(values):
    high = values.astype(jnp.bfloat16)
    low = (values - high.astype(jnp.float32)).astype(jnp.bfloat16)
    return high, low


def centre_terms(position):
    centre = jnp.clip(jnp.floor(position + 0.5), 0.0, CR - 1.0)
    return centre * SHARP, 2.0 * position - centre


def raw_weights(cells, scaled_cells, near, far):
    return jnp.exp2((scaled_cells[...] - near) * (far - cells[...]))


def fill_cells(cells, scaled_cells):
    index = lax.broadcasted_iota(jnp.int32, (CR, BB), 0).astype(jnp.float32)
    cells[...] = index
    scaled_cells[...] = index * SHARP


def sample_phase(groups, state, rows_p, rows_v, cells, scaled_cells, sampled_p, sampled_v):
    sublane = lax.broadcasted_iota(jnp.int32, (GROUP, BB), 0)
    ones = jnp.ones((16, CR), jnp.bfloat16)

    def body(group, carry):
        base = pl.multiple_of(group * GROUP, GROUP)
        here = pl.ds(base, GROUP)
        near, far = centre_terms(state[here, 2, :])
        rows = jnp.concatenate([rows_p[here, :], rows_v[here, :]], axis=0)
        high, low = split(rows)
        left = jnp.concatenate([high, low, ones], axis=0)
        left = jnp.concatenate([left, left], axis=1)
        acc_p = jnp.zeros((GROUP, BB), jnp.float32)
        acc_v = acc_p
        acc_n = acc_p
        for i in range(GROUP):
            w = raw_weights(cells, scaled_cells, near[i : i + 1], far[i : i + 1])
            right = jnp.concatenate(split(w), axis=0)
            out = jnp.dot(left, right, preferred_element_type=jnp.float32)
            mine = sublane == i
            acc_p = jnp.where(mine, out[0:8] + out[16:24], acc_p)
            acc_v = jnp.where(mine, out[8:16] + out[24:32], acc_v)
            acc_n = jnp.where(mine, out[32:40], acc_n)
        sampled_p[here, :] = acc_p / acc_n
        sampled_v[here, :] = acc_v / acc_n
        return carry

    lax.fori_loop(0, groups, body, 0)


def bubble_phase(chunks, state, sampled_p, sampled_v, source, void):
    h = TIME_STEP / SUBSTEPS

    def body(chunk, carry):
        here = pl.ds(pl.multiple_of(chunk * CHUNK, CHUNK), CHUNK)
        radius = state[here, 0, :]
        growth = state[here, 1, :]
        position = state[here, 2, :]
        speed = state[here, 3, :]
        rest_log = jnp.log2(state[here, 4, :])
        drive = AMBIENT + PRESSURE_COUPLING * sampled_p[here, :]
        velocity = sampled_v[here, :]
        for _ in range(SUBSTEPS):
            inverse = 1.0 / radius
            gas = jnp.exp2(GAS_INDEX * (rest_log - jnp.log2(radius)))
            accel = (gas - drive - growth * (1.5 * growth + VISCOUS * inverse)) * inverse
            growth = growth + h * accel
            radius = radius + h * growth
            speed = speed + (h / RELAX_TIME) * (velocity - speed)
            position = position + h * speed
        state[here, 0, :] = radius
        state[here, 1, :] = growth
        state[here, 2, :] = position
        state[here, 3, :] = speed
        area = radius * radius
        source[here, :] = (SOURCE_GAIN * FOUR_PI) * area * growth
        if void is not None:
            void[here, :] = (VOID_SCALE * FOUR_PI / 3.0) * area * radius
        return carry

    lax.fori_loop(0, chunks, body, 0)


def spread_phase(groups, live_blocks, tile_of, state, amounts, cells, scaled_cells, grids):
    sublane = lax.broadcasted_iota(jnp.int32, (GROUP, BB), 0)
    kinds = len(amounts)

    def body(group, carry):
        base = pl.multiple_of(group * GROUP, GROUP)
        here = pl.ds(base, GROUP)
        near, far = centre_terms(state[here, 2, :])
        whole = jnp.concatenate([a[here, :] for a in amounts], axis=0)
        accs = [jnp.zeros((GROUP, CR), jnp.float32) for _ in amounts]
        for i in range(GROUP):
            w = raw_weights(cells, scaled_cells, near[i : i + 1], far[i : i + 1])
            total = jnp.sum(w, axis=0, keepdims=True)
            high, low = split(w)
            right = jnp.concatenate([high, low], axis=1)
            top, rest = split(whole * (1.0 / total))
            left = jnp.concatenate([top, rest], axis=0)
            left = jnp.concatenate([left, left], axis=1)
            out = lax.dot_general(
                left, right, (((1,), (1,)), ((), ())), preferred_element_type=jnp.float32
            )
            mine = sublane == i
            for kind in range(kinds):
                lo = GROUP * kind
                hi = GROUP * (kinds + kind)
                accs[kind] = jnp.where(mine, out[lo : lo + GROUP] + out[hi : hi + GROUP], accs[kind])
        alive = sublane + base < live_blocks
        accs = [jnp.where(alive, acc, 0.0) for acc in accs]
        for i in range(GROUP):
            tile = tile_of(base + i)
            for grid, acc in zip(grids, accs):
                grid[pl.ds(tile, 1), :] = grid[pl.ds(tile, 1), :] + acc[i : i + 1]
        return carry

    lax.fori_loop(0, groups, body, 0)


def first_bubbles_kernel(
    counts, order, tiles, bubbles, flow_p, flow_v, packed, source_grid,
    state, rows_p, rows_v, sampled_p, sampled_v, source, cells, scaled_cells,
):
    live = counts[0]
    groups = (live + GROUP - 1) // GROUP
    chunks = (live + CHUNK - 1) // CHUNK
    fill_cells(cells, scaled_cells)
    source_grid[...] = jnp.zeros_like(source_grid)

    def gather(group, carry):
        base = pl.multiple_of(group * GROUP, GROUP)
        for i in range(GROUP):
            tile = tiles[base + i]
            rows_p[pl.ds(base + i, 1), :] = flow_p[0, pl.ds(tile, 1), :]
            rows_v[pl.ds(base + i, 1), :] = flow_v[0, pl.ds(tile, 1), :]
            state[base + i, 0:COMPS, :] = bubbles[base + i]
        return carry

    lax.fori_loop(0, groups, gather, 0)
    sample_phase(groups, state, rows_p, rows_v, cells, scaled_cells, sampled_p, sampled_v)
    bubble_phase(chunks, state, sampled_p, sampled_v, source, None)
    spread_phase(
        groups, live, lambda j: tiles[j], state, [source], cells, scaled_cells, [source_grid]
    )

    def pack(peer, carry):
        for k in range(CAP):
            block = order[peer * CAP + k]
            alive = block < live
            packed[peer, COMPS * k : COMPS * (k + 1), :] = jnp.where(
                alive, state[block, 0:COMPS, :], 0.0
            )
            packed[peer, COMPS * CAP + k : COMPS * CAP + k + 1, :] = jnp.where(
                alive, jnp.ones((1, BB), jnp.float32), 0.0
            )
        return carry

    lax.fori_loop(0, NBLK // CAP, pack, 0)


def second_bubbles_kernel(
    alive, tiles, packed, flow_p, flow_v, bubbles_out, source_grid, void_grid,
    slots, arrived, state, rows_p, rows_v, sampled_p, sampled_v, source, void, cells, scaled_cells,
):
    fill_cells(cells, scaled_cells)
    source_grid[...] = jnp.zeros_like(source_grid)
    void_grid[...] = jnp.zeros_like(void_grid)
    bubbles_out[...] = jnp.zeros_like(bubbles_out)

    def unpack(peer, live):
        for k in range(CAP):
            slot = peer * CAP + k
            arrived[slot, 0:COMPS, :] = packed[peer, COMPS * k : COMPS * (k + 1), :]
            slots[live] = slot
            live = live + alive[slot]
        return live

    live = lax.fori_loop(0, NBLK // CAP, unpack, jnp.int32(0))
    last = slots[jnp.maximum(live - 1, 0)]
    for i in range(GROUP):
        slots[live + i] = last
    groups = (live + GROUP - 1) // GROUP
    chunks = (live + CHUNK - 1) // CHUNK

    def gather(group, carry):
        base = pl.multiple_of(group * GROUP, GROUP)
        for i in range(GROUP):
            slot = slots[base + i]
            tile = tiles[slot]
            rows_p[pl.ds(base + i, 1), :] = flow_p[0, pl.ds(tile, 1), :]
            rows_v[pl.ds(base + i, 1), :] = flow_v[0, pl.ds(tile, 1), :]
            state[base + i, 0:COMPS, :] = arrived[slot, 0:COMPS, :]
        return carry

    lax.fori_loop(0, groups, gather, 0)
    sample_phase(groups, state, rows_p, rows_v, cells, scaled_cells, sampled_p, sampled_v)
    bubble_phase(chunks, state, sampled_p, sampled_v, source, void)

    def put(group, carry):
        base = pl.multiple_of(group * GROUP, GROUP)
        for i in range(GROUP):
            bubbles_out[slots[base + i]] = state[base + i, 0:COMPS, :]
        return carry

    lax.fori_loop(0, groups, put, 0)
    spread_phase(
        groups, live, lambda j: tiles[slots[j]], state, [source, void], cells, scaled_cells,
        [source_grid, void_grid],
    )


def fluid_kernel(
    flow, source, stream_before, stream_after, azim_before, azim_after, new, *faces
):
    streams = flow.shape[1]
    azims = flow.shape[2]
    shape = (azims, CR)
    lane = lax.broadcasted_iota(jnp.int32, shape, 1)
    row = lax.broadcasted_iota(jnp.int32, shape, 0)
    first_lane, last_lane = lane == 0, lane == CR - 1
    first_row, last_row = row == 0, row == azims - 1
    a = 0.5 * TIME_STEP

    def plane(s, down, up):
        sums = []
        values = []
        advected = []
        stream_slope = []
        azim_slope = {}
        radial_slope = {}
        for c in range(4):
            f = flow[c, s]
            before = down(c)
            after = up(c)
            left = jnp.where(first_row, azim_before[c, pl.ds(s, 1), :], pltpu.roll(f, 1, 0))
            right = jnp.where(last_row, azim_after[c, pl.ds(s, 1), :], pltpu.roll(f, azims - 1, 0))
            inner = jnp.where(first_lane, 0.0, pltpu.roll(f, 1, 1))
            outer = jnp.where(last_lane, 0.0, pltpu.roll(f, CR - 1, 1))
            slope = after - before
            values.append(f)
            sums.append(((before + after) + (left + right)) + (inner + outer))
            stream_slope.append(slope)
            if c in (0, 2):
                azim_slope[c] = right - left
            if c in (0, 3):
                radial_slope[c] = outer - inner
        rates = [
            MEAN_FLOW * stream_slope[0] + stream_slope[1] + azim_slope[2] + radial_slope[3],
            MEAN_FLOW * stream_slope[1] + stream_slope[0],
            MEAN_FLOW * stream_slope[2] + azim_slope[0],
            MEAN_FLOW * stream_slope[3] + radial_slope[0],
        ]
        for c in range(4):
            value = (1.0 - 6.0 * DIFFUSION) * values[c] + DIFFUSION * sums[c] - a * rates[c]
            if c == 0:
                value = value - TIME_STEP * source[s]
            new[c, s] = value
            if faces:
                faces[2][c, pl.ds(s, 1), :] = value[0:1]
                faces[3][c, pl.ds(s, 1), :] = value[azims - 1 : azims]

    plane(0, lambda c: stream_before[c], lambda c: flow[c, 1])

    def body(s, carry):
        plane(s, lambda c: flow[c, s - 1], lambda c: flow[c, s + 1])
        return carry

    lax.fori_loop(1, streams - 1, body, 0)
    plane(streams - 1, lambda c: flow[c, streams - 2], lambda c: stream_after[c])
    if faces:
        faces[0][...] = new[:, 0]
        faces[1][...] = new[:, streams - 1]


F32 = jnp.float32
SHAPE = jax.ShapeDtypeStruct


def whole(shape):
    return pl.BlockSpec(shape, lambda *_: (0,) * len(shape), memory_space=VMEM)


def component(c, tiles):
    return pl.BlockSpec((1, tiles, CR), lambda *_: (c, 0, 0), memory_space=VMEM)


def params(mib):
    return pltpu.CompilerParams(vmem_limit_bytes=mib << 20)


def bubble_scratch(amounts):
    wide = [VMEM((NBLK, BB), F32)] * (4 + amounts)
    return [VMEM((NBLK, 8, BB), F32)] + wide + [VMEM((CR, BB), F32)] * 2


def first_bubbles(counts, order, tiles, bubbles, flow_rows):
    ntile = flow_rows.shape[1]
    peers = NBLK // CAP
    return pl.pallas_call(
        first_bubbles_kernel,
        grid=(1,),
        in_specs=[pl.BlockSpec(memory_space=SMEM)] * 3
        + [whole((NBLK, COMPS, BB)), component(0, ntile), component(3, ntile)],
        out_specs=[whole((peers, PACK, BB)), whole((ntile, CR))],
        out_shape=[SHAPE((peers, PACK, BB), F32), SHAPE((ntile, CR), F32)],
        scratch_shapes=bubble_scratch(1),
        compiler_params=params(24),
        cost_estimate=pl.CostEstimate(flops=10**9, bytes_accessed=40 * 10**6, transcendentals=10**7),
        name="first_bubbles",
    )(counts, order, tiles, bubbles, flow_rows, flow_rows)


def second_bubbles(alive, tiles, packed, flow_rows):
    ntile = flow_rows.shape[1]
    peers = NBLK // CAP
    return pl.pallas_call(
        second_bubbles_kernel,
        grid=(1,),
        in_specs=[pl.BlockSpec(memory_space=SMEM)] * 2
        + [whole((peers, PACK, BB)), component(0, ntile), component(3, ntile)],
        out_specs=[whole((NBLK, COMPS, BB)), whole((ntile, CR)), whole((ntile, CR))],
        out_shape=[SHAPE((NBLK, COMPS, BB), F32), SHAPE((ntile, CR), F32), SHAPE((ntile, CR), F32)],
        scratch_shapes=[SMEM((NBLK + 2 * GROUP,), jnp.int32), VMEM((NBLK, 8, BB), F32)]
        + bubble_scratch(2),
        compiler_params=params(24),
        cost_estimate=pl.CostEstimate(flops=10**9, bytes_accessed=40 * 10**6, transcendentals=10**7),
        name="second_bubbles",
    )(alive, tiles, packed, flow_rows, flow_rows)


def fluid_update(flow, source, halos, with_faces):
    streams, azims = flow.shape[1:3]
    out_shape = [SHAPE(flow.shape, F32)]
    if with_faces:
        out_shape += [SHAPE((4, azims, CR), F32)] * 2 + [SHAPE((4, streams, CR), F32)] * 2
    return pl.pallas_call(
        fluid_kernel,
        grid=(1,),
        in_specs=[whole(flow.shape), whole((streams, azims, CR))]
        + [whole((4, azims, CR))] * 2
        + [whole((4, streams, CR))] * 2,
        out_specs=[whole(s.shape) for s in out_shape],
        out_shape=out_shape,
        compiler_params=params(28),
        cost_estimate=pl.CostEstimate(flops=10**8, bytes_accessed=10**7, transcendentals=0),
        name="fluid",
    )(flow, source.reshape(streams, azims, CR), *halos)


def exchange(head_stream, tail_stream, head_azim, tail_azim):
    streams = lax.axis_size("stream")
    azims = lax.axis_size("azim")
    return (
        lax.ppermute(tail_stream, "stream", [(i, i + 1) for i in range(streams - 1)]),
        lax.ppermute(head_stream, "stream", [(i + 1, i) for i in range(streams - 1)]),
        lax.ppermute(tail_azim, "azim", [(i, (i + 1) % azims) for i in range(azims)]),
        lax.ppermute(head_azim, "azim", [((i + 1) % azims, i) for i in range(azims)]),
    )


def on_device(fluid, bubbles, counts, outgoing_block_order, tiles_first_update, tiles_after):
    halos = exchange(fluid[:, 0], fluid[:, -1], fluid[:, :, 0], fluid[:, :, -1])
    rows = fluid.reshape(4, -1, CR)
    packed, source = first_bubbles(
        counts, outgoing_block_order, tiles_first_update, bubbles, rows
    )
    arrived = lax.all_to_all(packed, ("stream", "azim"), split_axis=0, concat_axis=0, tiled=True)
    flow, *faces = fluid_update(fluid, source, halos, True)
    halos = exchange(*faces)
    alive = (arrived[:, COMPS * CAP :, 0] > 0.5).astype(jnp.int32).reshape(-1)
    moved, source, void = second_bubbles(alive, tiles_after, arrived, flow.reshape(4, -1, CR))
    (flow,) = fluid_update(flow, source, halos, False)
    return flow, moved, void.reshape(fluid.shape[1:])


def solution(mesh):
    return jax.shard_map(
        on_device,
        mesh=mesh,
        in_specs=(
            P(None, "stream", "azim", None),
            P(("stream", "azim"), None, None),
            P(("stream", "azim")),
            P(("stream", "azim")),
            P(("stream", "azim")),
            P(("stream", "azim")),
        ),
        out_specs=(
            P(None, "stream", "azim", None),
            P(("stream", "azim"), None, None),
            P("stream", "azim", None),
        ),
        check_vma=False,
    )
```

time: 528 us -> 160 us (0.30); the launches traced: 520 us -> 159 us
  matrix products: 230 us -> 0 us
  other arithmetic: 189 us -> 2.23 us
  Pallas kernels: 0 us -> 96.5 us
  local copies, waits for them, and re-layouts: 53.8 us -> 14.7 us
  waiting for transfers between devices: 0.03 us -> 11.6 us
  starting transfers between devices: 43.1 us -> 32.8 us
    dot_general x32 -> x0, matrix products: 230 us -> none  [the longest x16 139 us: advance_group(): jnp.einsum('gbk,gck->gcb', weights, tile_row_count, precision=lax.Precisi...]
    pallas_call x0 -> x4, Pallas kernels: none -> 96.5 us  [the longest x1 48.5 us: first_bubbles(): pl.pallas_call(first_bubbles_kernel, grid=(1,), in_specs=[pl.BlockSpec(me...]
    reduce_sum x32 -> x0, other arithmetic: 75.5 us -> none  [kernel_weights(): return raw / jnp.sum(raw, axis=-1, keepdims=True)]
    scatter-add x2 -> x0, other arithmetic: 48.8 us -> none  [local_update(): jnp.zeros_like(selected).at[:, tile_indices]]
    mul x51 -> x0, other arithmetic: 35.8 us -> none  [the longest x2 28.8 us: fluid_update(): d_azim = 0.5 * (azim_up - azim_down)]
    ppermute x8, waiting for transfers between devices: 0.02 us -> 11.6 us  [the longest x2 9 us: exchange(): lax.ppermute(tail_azim, 'azim', [(i, (i + 1) % azims) for i in range(azim...]
    gather x4 -> x0, local copies, waits for them, and re-layouts: 10.6 us -> none  [the longest x2 4.55 us: local_update(): tile_row_count = jnp.take(selected, tile_indices, axis=1).transpose(1, 0, 2)]
    add x18 -> x0, other arithmetic: 10.5 us -> none  [the longest x2 9.64 us: fluid_update(): return flow_field + TIME_STEP * change + DIFFUSION * laplace]
  transfers between devices with their start and end apart: 10 -> 9, of which waited for: 0 -> 2; matrix products, arithmetic and copies ran while one was open for 48% -> 4% of each run, Pallas kernels for 0% -> 25%
where the time goes in v1:
time: 160 us; the launch traced here: 159 us
  Pallas kernels  96.5 us (60%)
  starting transfers between devices  32.8 us (20%)
  local copies, waits for them, and re-layouts  14.7 us (9%)
  waiting for transfers between devices  11.6 us (7%)
  other arithmetic  2.23 us (1%)
    pallas_call x1, Pallas kernels, first_bubbles(): pl.pallas_call(first_bubbles_kernel, grid=(1,), in_specs=[pl.BlockSpec(me...  48.5 us
    pallas_call x1, Pallas kernels, second_bubbles(): pl.pallas_call(second_bubbles_kernel, grid=(1,), in_specs=[pl.BlockSpec(m...  32.1 us
    pallas_call x2, Pallas kernels, fluid_update(): pl.pallas_call(fluid_kernel, grid=(1,), in_specs=[whole(flow.shape), whol...  15.9 us
    unnamed x18, local copies, waits for them, and re-layouts  12 us
    all_to_all x1, starting transfers between devices, on_device(): lax.all_to_all(packed, ('stream', 'azim'), split_axis=0, concat_axis=0, t...  10.8 us
    ppermute x2, waiting for transfers between devices, exchange(): lax.ppermute(tail_azim, 'azim', [(i, (i + 1) % azims) for i in range(azim...  9 us
    ppermute x2, starting transfers between devices, exchange(): lax.ppermute(head_azim, 'azim', [((i + 1) % azims, i) for i in range(azim...  8.88 us
    ppermute x2, starting transfers between devices, exchange(): lax.ppermute(tail_stream, 'stream', [(i, i + 1) for i in range(streams -...  6.83 us
  transfers between devices with their start and end apart: 9, of which 2 were waited for; matrix products, arithmetic and copies ran while one was open for 4% of the time, Pallas kernels for 25%

profile of v1, /device:TPU:1, one launch (start us, length us, event | category | flops | bytes accessed | tf_op | source)
XLA Modules:
  0.0 159.3 jit_solution(14553213951976308517)
XLA Ops:
  1.3 2.1 %copy.15.bubbles = f32[512,5,128]{2,1,0:T(8,128)S(1)} copy(f32[512,5,128]{2,0,1:T(8,128)} %param.7) | data formatting | bytes 2621440 | tf_op args[1]
  3.5 0.0 copy-start
  3.5 2.2 %copy-done = f32[4,64,32,128]{3,2,1,0:T(8,128)S(1)} copy-done((f32[4,64,32,128]{3,2,1,0:T(8,128)S(1)}, f32[4,64,32,128]{3,2,1,0:T(8,128)}, u32[]{:S(2)}) %copy-start) | copy-done | bytes 4194328
  5.7 48.5 %first_bubbles.1 = (f32[128,24,128]{2,1,0:T(8,128)}, f32[2048,128]{1,0:T(8,128)S(1)}) custom-call(s32[1]{0:T(128)S(6)} %copy.25.counts, s32[512]{0:T(512)S(1)} %copy-done.5, s32[512]{0:T(512)S(1)} %copy-done.6, f32[512,5,128]{2,1,0:T(8,128)S(1)} %copy.15.bubbles, f32[4,2048,128]{2,1,0:T(8,128)S(1)} %bitcast.19, f32[4,2048,128]{2,1,0:T(8,128)S(1)} %bitcast.20), custom_call_target="tpu_custom_call" | custom-call | flops 1000000000 | bytes 40000000 | tf_op jit(solution)/shard_map/first_bubbles/pallas_call | solution.py:338
  54.2 10.8 %all-to-all-start = ((f32[128,24,128]{2,1,0:T(8,128)}), f32[128,24,128]{2,1,0:T(8,128)S(1)}, u32[]{:S(2)}, u32[]{:S(2)}) async-start(f32[128,24,128]{2,1,0:T(8,128)} %get-tuple-element.15), calls=%async_computation | async-start | bytes 3145728 | tf_op jit(solution)/shard_map/all_to_all | solution.py:406
  65.0 1.7 %fusion = (f32[4,64,1,128]{3,2,1,0:T(1,128)S(1)}, f32[4,64,1,128]{3,2,1,0:T(1,128)S(1)}) fusion(f32[4,64,32,128]{3,2,1,0:T(8,128)} %flow.1), kind=kLoop, calls=%fused_computation.4 | loop fusion | bytes 524288 | tf_op jit(solution)/shard_map/slice | solution.py:401
  66.7 1.5 collective-permute-start.2
  68.2 4.1 %collective-permute-start.3 = (f32[4,64,128]{2,1,0:T(8,128)S(1)}, f32[4,64,128]{2,1,0:T(8,128)S(1)}, u32[]{:S(2)}, u32[]{:S(2)}) collective-permute-start(f32[4,64,128]{2,1,0:T(8,128)S(1)} %bitcast.25), channel_id=1, source_target_pairs={{1,0},{2,1},{3,2},{4,3},{5,4},{6,5},{7,6},{8,7},{9,8},{10,9},{11,1... | collective-permute-start | bytes 393224 | tf_op jit(solution)/shard_map/ppermute | solution.py:396
  72.3 0.9 slice_bitcast_fusion
  73.2 2.8 %collective-permute-start.1 = (f32[4,32,128]{2,1,0:T(8,128)S(1)}, f32[4,32,128]{2,1,0:T(8,128)S(1)}, u32[]{:S(2)}, u32[]{:S(2)}) collective-permute-start(f32[4,32,128]{2,1,0:T(8,128)S(1)} %get-tuple-element.31), channel_id=1, source_target_pairs={{16,0},{32,16},{48,32},{64,48},{80,64},{96,80},{112,96},{17,1},{33... | collective-permute-start | bytes 196616 | tf_op jit(solution)/shard_map/ppermute | solution.py:394
  76.0 2.8 %collective-permute-start = (f32[4,32,128]{2,1,0:T(8,128)S(1)}, f32[4,32,128]{2,1,0:T(8,128)S(1)}, u32[]{:S(2)}, u32[]{:S(2)}) collective-permute-start(f32[4,32,128]{2,1,0:T(8,128)S(1)} %get-tuple-element.32), channel_id=1, source_target_pairs={{0,16},{16,32},{32,48},{48,64},{64,80},{80,96},{96,112},{1,17},{17... | collective-permute-start | bytes 196616 | tf_op jit(solution)/shard_map/ppermute | solution.py:393
  78.8 2.6 %collective-permute-done.1.stream_after = f32[4,32,128]{2,1,0:T(8,128)S(1)} collective-permute-done((f32[4,32,128]{2,1,0:T(8,128)S(1)}, f32[4,32,128]{2,1,0:T(8,128)S(1)}, u32[]{:S(2)}, u32[]{:S(2)}) %collective-permute-start.1) | collective-permute-done | bytes 65568 | tf_op jit(solution)/shard_map/ppermute | solution.py:394
  81.4 9.0 %collective-permute-done.2.azim_before = f32[4,64,128]{2,1,0:T(8,128)S(1)} collective-permute-done((f32[4,64,128]{2,1,0:T(8,128)S(1)}, f32[4,64,128]{2,1,0:T(8,128)S(1)}, u32[]{:S(2)}, u32[]{:S(2)}) %collective-permute-start.2) | collective-permute-done | bytes 131104 | tf_op jit(solution)/shard_map/ppermute | solution.py:395
  90.4 0.0 collective-permute-done.3.azim_after
  90.4 2.2 %copy-done.1 = f32[4,64,32,128]{3,2,1,0:T(8,128)S(1)} copy-done((f32[4,64,32,128]{3,2,1,0:T(8,128)S(1)}, f32[4,64,32,128]{3,2,1,0:T(8,128)}, u32[]{:S(2)}) %copy-start.1) | copy-done | bytes 4194328
  92.6 6.9 %fluid.2 = (f32[4,64,32,128]{3,2,1,0:T(8,128)S(1)}, f32[4,32,128]{2,1,0:T(8,128)S(1)}, f32[4,32,128]{2,1,0:T(8,128)S(1)}, f32[4,64,128]{2,1,0:T(8,128)S(1)}, f32[4,64,128]{2,1,0:T(8,128)S(1)}) custom-call(f32[4,64,32,128]{3,2,1,0:T(8,128)S(1)} %copy-done.1, f32[64,32,128]{2,1,0:T(8,128)S(1)} %bitcast.24, ...), custom_call_target="tpu_custom_call" | custom-call | flops 100000000 | bytes 10000000 | tf_op jit(solution)/shard_map/fluid/pallas_call | solution.py:375
  99.5 0.0 copy-start.2
  99.5 2.0 %copy-done.2 = f32[4,64,32,128]{3,2,1,0:T(8,128)} copy-done((f32[4,64,32,128]{3,2,1,0:T(8,128)}, f32[4,64,32,128]{3,2,1,0:T(8,128)S(1)}, u32[]{:S(2)}) %copy-start.2) | copy-done | bytes 4194328
  101.5 4.0 %collective-permute-start.4 = (f32[4,32,128]{2,1,0:T(8,128)S(1)}, f32[4,32,128]{2,1,0:T(8,128)S(1)}, u32[]{:S(2)}, u32[]{:S(2)}) collective-permute-start(f32[4,32,128]{2,1,0:T(8,128)S(1)} %get-tuple-element.17), channel_id=1, source_target_pairs={{0,16},{16,32},{32,48},{48,64},{64,80},{80,96},{96,112},{1,17},{17... | collective-permute-start | bytes 196616 | tf_op jit(solution)/shard_map/ppermute | solution.py:393
  105.6 1.9 %collective-permute-start.5 = (f32[4,32,128]{2,1,0:T(8,128)S(1)}, f32[4,32,128]{2,1,0:T(8,128)S(1)}, u32[]{:S(2)}, u32[]{:S(2)}) collective-permute-start(f32[4,32,128]{2,1,0:T(8,128)S(1)} %get-tuple-element.18), channel_id=1, source_target_pairs={{16,0},{32,16},{48,32},{64,48},{80,64},{96,80},{112,96},{17,1},{33... | collective-permute-start | bytes 196616 | tf_op jit(solution)/shard_map/ppermute | solution.py:394
  107.5 0.1 collective-permute-start.6
  107.6 4.8 %collective-permute-start.7 = (f32[4,64,128]{2,1,0:T(8,128)S(1)}, f32[4,64,128]{2,1,0:T(8,128)S(1)}, u32[]{:S(2)}, u32[]{:S(2)}) collective-permute-start(f32[4,64,128]{2,1,0:T(8,128)S(1)} %get-tuple-element.20), channel_id=1, source_target_pairs={{1,0},{2,1},{3,2},{4,3},{5,4},{6,5},{7,6},{8,7},{9,8},{10,9},{11,1... | collective-permute-start | bytes 393224 | tf_op jit(solution)/shard_map/ppermute | solution.py:396
  112.4 2.2 %convert_reduce_fusion = s32[128,4]{1,0:T(8,128)S(1)} fusion(f32[128,24,128]{2,1,0:T(8,128)S(1)} %all-to-all-done.packed), kind=kLoop, calls=%fused_computation.1 | loop fusion | flops 1024 | bytes 4096 | tf_op jit(solution)/shard_map/convert_element_type | solution.py:409
  114.6 0.1 reshape.32.alive
  114.7 0.0 copy-start.3
  114.7 2.2 %copy-done.3 = f32[4,64,32,128]{3,2,1,0:T(8,128)S(1)} copy-done((f32[4,64,32,128]{3,2,1,0:T(8,128)S(1)}, f32[4,64,32,128]{3,2,1,0:T(8,128)}, u32[]{:S(2)}) %copy-start.3) | copy-done | bytes 4194328
  116.9 32.1 %second_bubbles.1 = (f32[512,5,128]{2,1,0:T(8,128)S(1)}, f32[2048,128]{1,0:T(8,128)S(1)}, f32[2048,128]{1,0:T(8,128)}) custom-call(s32[512]{0:T(512)S(1)} %reshape.32.alive, s32[512]{0:T(512)S(1)} %copy-done.7, f32[128,24,128]{2,1,0:T(8,128)S(1)} %all-to-all-done.packed, f32[4,2048,128]{2,1,0:T(8,128)S(1)} %bitcast.21, f32[4,2048,128]{2,1,0:T(8,128)S(1)} %bitcast.22), custom_call_target="tpu_custom_call" | custom-call | flops 1000000000 | bytes 40000000 | tf_op jit(solution)/shard_map/second_bubbles/pallas_call | solution.py:355
  149.0 1.3 copy.20
  150.3 0.0 collective-permute-done.4.stream_before
  150.3 0.0 collective-permute-done.5.stream_after
  150.3 0.0 collective-permute-done.7.azim_after
  150.4 8.9 %fluid.3 = f32[4,64,32,128]{3,2,1,0:T(8,128)} custom-call(f32[4,64,32,128]{3,2,1,0:T(8,128)S(1)} %copy-done.4, f32[64,32,128]{2,1,0:T(8,128)S(1)} %bitcast.23, f32[4,32,128]{2,1,0:T(8,128)S(1)} %collective-permute-done.4.stream_before, f32[4,32,128]{2,1,0:T(8,128)S(1)} %collective-permute-done.5.stream_after, ...), custom_call_target="tpu_custom_call" | custom-call | flops 100000000 | bytes 10000000 | tf_op jit(solution)/shard_map/fluid/pallas_call | solution.py:375
  (12 shorter events, 0.0 us)
Async XLA Ops:
  0.6 2.8 %copy-start.6 = (s32[512]{0:T(512)S(1)}, s32[512]{0:T(512)}, u32[]{:S(2)}) copy-start(s32[512]{0:T(512)} %tiles.2) | copy-start | bytes 6148
  0.6 2.8 %copy-start.5 = (s32[512]{0:T(512)S(1)}, s32[512]{0:T(512)}, u32[]{:S(2)}) copy-start(s32[512]{0:T(512)} %order.1) | copy-start | bytes 6148
  3.5 2.2 %copy-start = (f32[4,64,32,128]{3,2,1,0:T(8,128)S(1)}, f32[4,64,32,128]{3,2,1,0:T(8,128)}, u32[]{:S(2)}) copy-start(f32[4,64,32,128]{3,2,1,0:T(8,128)} %flow.1) | copy-start | bytes 12582916
  54.2 58.2 %all-to-all-start = ((f32[128,24,128]{2,1,0:T(8,128)}), f32[128,24,128]{2,1,0:T(8,128)S(1)}, u32[]{:S(2)}, u32[]{:S(2)}) async-start(f32[128,24,128]{2,1,0:T(8,128)} %get-tuple-element.15), calls=%async_computation | async-start | bytes 3145728 | tf_op jit(solution)/shard_map/all_to_all | solution.py:406
  66.7 23.7 %collective-permute-start.2 = (f32[4,64,128]{2,1,0:T(8,128)S(1)}, f32[4,64,128]{2,1,0:T(8,128)S(1)}, u32[]{:S(2)}, u32[]{:S(2)}) collective-permute-start(f32[4,64,128]{2,1,0:T(8,128)S(1)} %bitcast.26), channel_id=1, source_target_pairs={{0,1},{1,2},{2,3},{3,4},{4,5},{5,6},{6,7},{7,8},{8,9},{9,10},{10,1... | collective-permute-start | bytes 393224 | tf_op jit(solution)/shard_map/ppermute | solution.py:395
  68.2 22.2 %collective-permute-start.3 = (f32[4,64,128]{2,1,0:T(8,128)S(1)}, f32[4,64,128]{2,1,0:T(8,128)S(1)}, u32[]{:S(2)}, u32[]{:S(2)}) collective-permute-start(f32[4,64,128]{2,1,0:T(8,128)S(1)} %bitcast.25), channel_id=1, source_target_pairs={{1,0},{2,1},{3,2},{4,3},{5,4},{6,5},{7,6},{8,7},{9,8},{10,9},{11,1... | collective-permute-start | bytes 393224 | tf_op jit(solution)/shard_map/ppermute | solution.py:396
  73.2 8.2 %collective-permute-start.1 = (f32[4,32,128]{2,1,0:T(8,128)S(1)}, f32[4,32,128]{2,1,0:T(8,128)S(1)}, u32[]{:S(2)}, u32[]{:S(2)}) collective-permute-start(f32[4,32,128]{2,1,0:T(8,128)S(1)} %get-tuple-element.31), channel_id=1, source_target_pairs={{16,0},{32,16},{48,32},{64,48},{80,64},{96,80},{112,96},{17,1},{33... | collective-permute-start | bytes 196616 | tf_op jit(solution)/shard_map/ppermute | solution.py:394
  76.0 5.4 %collective-permute-start = (f32[4,32,128]{2,1,0:T(8,128)S(1)}, f32[4,32,128]{2,1,0:T(8,128)S(1)}, u32[]{:S(2)}, u32[]{:S(2)}) collective-permute-start(f32[4,32,128]{2,1,0:T(8,128)S(1)} %get-tuple-element.32), channel_id=1, source_target_pairs={{0,16},{16,32},{32,48},{48,64},{64,80},{80,96},{96,112},{1,17},{17... | collective-permute-start | bytes 196616 | tf_op jit(solution)/shard_map/ppermute | solution.py:393
  90.4 2.2 %copy-start.1 = (f32[4,64,32,128]{3,2,1,0:T(8,128)S(1)}, f32[4,64,32,128]{3,2,1,0:T(8,128)}, u32[]{:S(2)}) copy-start(f32[4,64,32,128]{3,2,1,0:T(8,128)} %flow.1) | copy-start | bytes 12582916
  92.6 22.1 %copy-start.7 = (s32[512]{0:T(512)S(1)}, s32[512]{0:T(512)}, u32[]{:S(2)}) copy-start(s32[512]{0:T(512)} %tiles.3) | copy-start | bytes 6148
  99.5 2.0 %copy-start.2 = (f32[4,64,32,128]{3,2,1,0:T(8,128)}, f32[4,64,32,128]{3,2,1,0:T(8,128)S(1)}, u32[]{:S(2)}) copy-start(f32[4,64,32,128]{3,2,1,0:T(8,128)S(1)} %get-tuple-element.14.flow) | copy-start | bytes 12582916
  101.5 48.8 %collective-permute-start.4 = (f32[4,32,128]{2,1,0:T(8,128)S(1)}, f32[4,32,128]{2,1,0:T(8,128)S(1)}, u32[]{:S(2)}, u32[]{:S(2)}) collective-permute-start(f32[4,32,128]{2,1,0:T(8,128)S(1)} %get-tuple-element.17), channel_id=1, source_target_pairs={{0,16},{16,32},{32,48},{48,64},{64,80},{80,96},{96,112},{1,17},{17... | collective-permute-start | bytes 196616 | tf_op jit(solution)/shard_map/ppermute | solution.py:393
  105.6 44.8 %collective-permute-start.5 = (f32[4,32,128]{2,1,0:T(8,128)S(1)}, f32[4,32,128]{2,1,0:T(8,128)S(1)}, u32[]{:S(2)}, u32[]{:S(2)}) collective-permute-start(f32[4,32,128]{2,1,0:T(8,128)S(1)} %get-tuple-element.18), channel_id=1, source_target_pairs={{16,0},{32,16},{48,32},{64,48},{80,64},{96,80},{112,96},{17,1},{33... | collective-permute-start | bytes 196616 | tf_op jit(solution)/shard_map/ppermute | solution.py:394
  107.5 42.8 %collective-permute-start.6 = (f32[4,64,128]{2,1,0:T(8,128)S(1)}, f32[4,64,128]{2,1,0:T(8,128)S(1)}, u32[]{:S(2)}, u32[]{:S(2)}) collective-permute-start(f32[4,64,128]{2,1,0:T(8,128)S(1)} %get-tuple-element.19), channel_id=1, source_target_pairs={{0,1},{1,2},{2,3},{3,4},{4,5},{5,6},{6,7},{7,8},{8,9},{9,10},{10,1... | collective-permute-start | bytes 393224 | tf_op jit(solution)/shard_map/ppermute | solution.py:395
  107.6 42.8 %collective-permute-start.7 = (f32[4,64,128]{2,1,0:T(8,128)S(1)}, f32[4,64,128]{2,1,0:T(8,128)S(1)}, u32[]{:S(2)}, u32[]{:S(2)}) collective-permute-start(f32[4,64,128]{2,1,0:T(8,128)S(1)} %get-tuple-element.20), channel_id=1, source_target_pairs={{1,0},{2,1},{3,2},{4,3},{5,4},{6,5},{7,6},{8,7},{9,8},{10,9},{11,1... | collective-permute-start | bytes 393224 | tf_op jit(solution)/shard_map/ppermute | solution.py:396
  114.7 2.2 %copy-start.3 = (f32[4,64,32,128]{3,2,1,0:T(8,128)S(1)}, f32[4,64,32,128]{3,2,1,0:T(8,128)}, u32[]{:S(2)}) copy-start(f32[4,64,32,128]{3,2,1,0:T(8,128)} %copy-done.2) | copy-start | bytes 12582916
  116.9 33.4 %copy-start.4 = (f32[4,64,32,128]{3,2,1,0:T(8,128)S(1)}, f32[4,64,32,128]{3,2,1,0:T(8,128)}, u32[]{:S(2)}) copy-start(f32[4,64,32,128]{3,2,1,0:T(8,128)} %copy-done.2) | copy-start | bytes 12582916

commit v2 on v1

--- a/solution.py
+++ b/solution.py
@@ -29,6 +29,8 @@
 CAP = 4
 PACK = 24
 GROUP = 8
+STREAM_BLOCK = 8
+VMEM_MIB = 58
 CHUNK = 64
 SHARP = 0.5 / (KERNEL_WIDTH * KERNEL_WIDTH) * LOG2_E
 VMEM = pltpu.VMEM
@@ -56,14 +58,14 @@
     scaled_cells[...] = index * SHARP
 
 
-def sample_phase(groups, state, rows_p, rows_v, cells, scaled_cells, sampled_p, sampled_v):
+def sample_phase(groups, positions, rows_p, rows_v, cells, scaled_cells, sampled_p, sampled_v):
     sublane = lax.broadcasted_iota(jnp.int32, (GROUP, BB), 0)
     ones = jnp.ones((16, CR), jnp.bfloat16)
 
     def body(group, carry):
         base = pl.multiple_of(group * GROUP, GROUP)
         here = pl.ds(base, GROUP)
-        near, far = centre_terms(state[here, 2, :])
+        near, far = centre_terms(positions(here))
         rows = jnp.concatenate([rows_p[here, :], rows_v[here, :]], axis=0)
         high, low = split(rows)
         left = jnp.concatenate([high, low, ones], axis=0)
@@ -71,14 +73,22 @@
         acc_p = jnp.zeros((GROUP, BB), jnp.float32)
         acc_v = acc_p
         acc_n = acc_p
-        for i in range(GROUP):
-            w = raw_weights(cells, scaled_cells, near[i : i + 1], far[i : i + 1])
-            right = jnp.concatenate(split(w), axis=0)
-            out = jnp.dot(left, right, preferred_element_type=jnp.float32)
-            mine = sublane == i
-            acc_p = jnp.where(mine, out[0:8] + out[16:24], acc_p)
-            acc_v = jnp.where(mine, out[8:16] + out[24:32], acc_v)
-            acc_n = jnp.where(mine, out[32:40], acc_n)
+        for i in range(0, GROUP, 2):
+            right = jnp.concatenate(
+                [
+                    jnp.concatenate(
+                        split(raw_weights(cells, scaled_cells, near[b : b + 1], far[b : b + 1])), axis=0
+                    )
+                    for b in (i, i + 1)
+                ],
+                axis=1,
+            )
+            both = jnp.dot(left, right, preferred_element_type=jnp.float32)
+            for b, out in ((i, both[:, :BB]), (i + 1, both[:, BB:])):
+                mine = sublane == b
+                acc_p = jnp.where(mine, out[0:8] + out[16:24], acc_p)
+                acc_v = jnp.where(mine, out[8:16] + out[24:32], acc_v)
+                acc_n = jnp.where(mine, out[32:40], acc_n)
         sampled_p[here, :] = acc_p / acc_n
         sampled_v[here, :] = acc_v / acc_n
         return carry
@@ -86,16 +96,16 @@
     lax.fori_loop(0, groups, body, 0)
 
 
-def bubble_phase(chunks, state, sampled_p, sampled_v, source, void):
+def bubble_phase(chunks, component, state, sampled_p, sampled_v, source, void):
     h = TIME_STEP / SUBSTEPS
 
     def body(chunk, carry):
         here = pl.ds(pl.multiple_of(chunk * CHUNK, CHUNK), CHUNK)
-        radius = state[here, 0, :]
-        growth = state[here, 1, :]
-        position = state[here, 2, :]
-        speed = state[here, 3, :]
-        rest_log = jnp.log2(state[here, 4, :])
+        radius = component(0, here)
+        growth = component(1, here)
+        position = component(2, here)
+        speed = component(3, here)
+        rest_log = jnp.log2(component(4, here))
         drive = AMBIENT + PRESSURE_COUPLING * sampled_p[here, :]
         velocity = sampled_v[here, :]
         for _ in range(SUBSTEPS):
@@ -110,6 +120,7 @@
         state[here, 1, :] = growth
         state[here, 2, :] = position
         state[here, 3, :] = speed
+        state[here, 4, :] = component(4, here)
         area = radius * radius
         source[here, :] = (SOURCE_GAIN * FOUR_PI) * area * growth
         if void is not None:
@@ -129,22 +140,29 @@
         near, far = centre_terms(state[here, 2, :])
         whole = jnp.concatenate([a[here, :] for a in amounts], axis=0)
         accs = [jnp.zeros((GROUP, CR), jnp.float32) for _ in amounts]
-        for i in range(GROUP):
-            w = raw_weights(cells, scaled_cells, near[i : i + 1], far[i : i + 1])
-            total = jnp.sum(w, axis=0, keepdims=True)
-            high, low = split(w)
-            right = jnp.concatenate([high, low], axis=1)
-            top, rest = split(whole * (1.0 / total))
-            left = jnp.concatenate([top, rest], axis=0)
-            left = jnp.concatenate([left, left], axis=1)
-            out = lax.dot_general(
+        for i in range(0, GROUP, 2):
+            lefts = []
+            rights = []
+            for b in (i, i + 1):
+                w = raw_weights(cells, scaled_cells, near[b : b + 1], far[b : b + 1])
+                total = jnp.sum(w, axis=0, keepdims=True)
+                rights.append(jnp.concatenate(split(w), axis=1))
+                left = jnp.concatenate(split(whole * (1.0 / total)), axis=0)
+                lefts.append(jnp.concatenate([left, left], axis=1))
+            left = jnp.concatenate(lefts, axis=0)
+            right = jnp.concatenate(rights, axis=0)
+            both = lax.dot_general(
                 left, right, (((1,), (1,)), ((), ())), preferred_element_type=jnp.float32
             )
-            mine = sublane == i
-            for kind in range(kinds):
-                lo = GROUP * kind
-                hi = GROUP * (kinds + kind)
-                accs[kind] = jnp.where(mine, out[lo : lo + GROUP] + out[hi : hi + GROUP], accs[kind])
+            for b in (0, 1):
+                out = both[2 * GROUP * kinds * b :, CR * b : CR * (b + 1)]
+                mine = sublane == i + b
+                for kind in range(kinds):
+                    lo = GROUP * kind
+                    hi = GROUP * (kinds + kind)
+                    accs[kind] = jnp.where(
+                        mine, out[lo : lo + GROUP] + out[hi : hi + GROUP], accs[kind]
+                    )
         alive = sublane + base < live_blocks
         accs = [jnp.where(alive, acc, 0.0) for acc in accs]
         for i in range(GROUP):
@@ -172,49 +190,61 @@
             tile = tiles[base + i]
             rows_p[pl.ds(base + i, 1), :] = flow_p[0, pl.ds(tile, 1), :]
             rows_v[pl.ds(base + i, 1), :] = flow_v[0, pl.ds(tile, 1), :]
-            state[base + i, 0:COMPS, :] = bubbles[base + i]
         return carry
 
     lax.fori_loop(0, groups, gather, 0)
-    sample_phase(groups, state, rows_p, rows_v, cells, scaled_cells, sampled_p, sampled_v)
-    bubble_phase(chunks, state, sampled_p, sampled_v, source, None)
+    sample_phase(
+        groups, lambda here: bubbles[2, here, :], rows_p, rows_v, cells, scaled_cells, sampled_p, sampled_v
+    )
+    bubble_phase(
+        chunks, lambda c, here: bubbles[c, here, :], state, sampled_p, sampled_v, source, None
+    )
     spread_phase(
         groups, live, lambda j: tiles[j], state, [source], cells, scaled_cells, [source_grid]
     )
 
+    lane = lax.broadcasted_iota(jnp.int32, (PACK - COMPS * CAP, BB), 1)
+
     def pack(peer, carry):
+        flags = jnp.zeros((PACK - COMPS * CAP, BB), jnp.float32)
         for k in range(CAP):
             block = order[peer * CAP + k]
             alive = block < live
             packed[peer, COMPS * k : COMPS * (k + 1), :] = jnp.where(
                 alive, state[block, 0:COMPS, :], 0.0
             )
-            packed[peer, COMPS * CAP + k : COMPS * CAP + k + 1, :] = jnp.where(
-                alive, jnp.ones((1, BB), jnp.float32), 0.0
-            )
+            flags = jnp.where((lane == k) & alive, 1.0, flags)
+        packed[peer, COMPS * CAP : PACK, :] = flags
         return carry
 
     lax.fori_loop(0, NBLK // CAP, pack, 0)
 
 
 def second_bubbles_kernel(
-    alive, tiles, packed, flow_p, flow_v, bubbles_out, source_grid, void_grid,
-    slots, arrived, state, rows_p, rows_v, sampled_p, sampled_v, source, void, cells, scaled_cells,
+    tiles, packed, flow_p, flow_v, bubbles_out, source_grid, void_grid,
+    slots, flags, flag_sem, arrived, state, rows_p, rows_v, sampled_p, sampled_v, source, void, cells, scaled_cells,
 ):
+    copy = pltpu.make_async_copy(packed.at[:, COMPS * CAP, :], flags, flag_sem)
+    copy.start()
     fill_cells(cells, scaled_cells)
     source_grid[...] = jnp.zeros_like(source_grid)
     void_grid[...] = jnp.zeros_like(void_grid)
-    bubbles_out[...] = jnp.zeros_like(bubbles_out)
-
-    def unpack(peer, live):
+
+    def unpack(peer, carry):
         for k in range(CAP):
-            slot = peer * CAP + k
-            arrived[slot, 0:COMPS, :] = packed[peer, COMPS * k : COMPS * (k + 1), :]
-            slots[live] = slot
-            live = live + alive[slot]
+            arrived[peer * CAP + k, 0:COMPS, :] = packed[peer, COMPS * k : COMPS * (k + 1), :]
+        return carry
+
+    lax.fori_loop(0, NBLK // CAP, unpack, 0, unroll=4)
+    copy.wait()
+
+    def compact(peer, live):
+        for k in range(CAP):
+            slots[live] = peer * CAP + k
+            live = live + jnp.where(flags[peer, k] > 0.5, 1, 0)
         return live
 
-    live = lax.fori_loop(0, NBLK // CAP, unpack, jnp.int32(0))
+    live = lax.fori_loop(0, NBLK // CAP, compact, jnp.int32(0), unroll=4)
     last = slots[jnp.maximum(live - 1, 0)]
     for i in range(GROUP):
         slots[live + i] = last
@@ -232,16 +262,29 @@
         return carry
 
     lax.fori_loop(0, groups, gather, 0)
-    sample_phase(groups, state, rows_p, rows_v, cells, scaled_cells, sampled_p, sampled_v)
-    bubble_phase(chunks, state, sampled_p, sampled_v, source, void)
+    sample_phase(
+        groups, lambda here: state[here, 2, :], rows_p, rows_v, cells, scaled_cells, sampled_p, sampled_v
+    )
+    bubble_phase(
+        chunks, lambda c, here: state[here, c, :], state, sampled_p, sampled_v, source, void
+    )
+    arrived[...] = jnp.zeros_like(arrived)
 
     def put(group, carry):
         base = pl.multiple_of(group * GROUP, GROUP)
         for i in range(GROUP):
-            bubbles_out[slots[base + i]] = state[base + i, 0:COMPS, :]
+            arrived[slots[base + i]] = state[base + i]
         return carry
 
     lax.fori_loop(0, groups, put, 0)
+
+    def store(group, carry):
+        here = pl.ds(pl.multiple_of(group * GROUP, GROUP), GROUP)
+        for c in range(COMPS):
+            bubbles_out[c, here, :] = arrived[here, c, :]
+        return carry
+
+    lax.fori_loop(0, NBLK // GROUP, store, 0)
     spread_phase(
         groups, live, lambda j: tiles[slots[j]], state, [source, void], cells, scaled_cells,
         [source_grid, void_grid],
@@ -249,8 +292,10 @@
 
 
 def fluid_kernel(
-    flow, source, stream_before, stream_after, azim_before, azim_after, new, *faces
+    flow, flow_before, flow_after, source, stream_before, stream_after, azim_before, azim_after, new, *faces
 ):
+    step = pl.program_id(0)
+    first, final = step == 0, step == pl.num_programs(0) - 1
     streams = flow.shape[1]
     azims = flow.shape[2]
     shape = (azims, CR)
@@ -263,7 +308,6 @@
     def plane(s, down, up):
         sums = []
         values = []
-        advected = []
         stream_slope = []
         azim_slope = {}
         radial_slope = {}
@@ -275,10 +319,9 @@
             right = jnp.where(last_row, azim_after[c, pl.ds(s, 1), :], pltpu.roll(f, azims - 1, 0))
             inner = jnp.where(first_lane, 0.0, pltpu.roll(f, 1, 1))
             outer = jnp.where(last_lane, 0.0, pltpu.roll(f, CR - 1, 1))
-            slope = after - before
             values.append(f)
             sums.append(((before + after) + (left + right)) + (inner + outer))
-            stream_slope.append(slope)
+            stream_slope.append(after - before)
             if c in (0, 2):
                 azim_slope[c] = right - left
             if c in (0, 3):
@@ -298,17 +341,21 @@
                 faces[2][c, pl.ds(s, 1), :] = value[0:1]
                 faces[3][c, pl.ds(s, 1), :] = value[azims - 1 : azims]
 
-    plane(0, lambda c: stream_before[c], lambda c: flow[c, 1])
-
-    def body(s, carry):
-        plane(s, lambda c: flow[c, s - 1], lambda c: flow[c, s + 1])
-        return carry
-
-    lax.fori_loop(1, streams - 1, body, 0)
-    plane(streams - 1, lambda c: flow[c, streams - 2], lambda c: stream_after[c])
+    for s in range(streams):
+        plane(
+            s,
+            (lambda c: jnp.where(first, stream_before[c], flow_before[c, 0])) if s == 0 else (lambda c: flow[c, s - 1]),
+            (lambda c: jnp.where(final, stream_after[c], flow_after[c, 0])) if s == streams - 1 else (lambda c: flow[c, s + 1]),
+        )
     if faces:
-        faces[0][...] = new[:, 0]
-        faces[1][...] = new[:, streams - 1]
+
+        @pl.when(first)
+        def _():
+            faces[0][...] = new[:, 0]
+
+        @pl.when(final)
+        def _():
+            faces[1][...] = new[:, streams - 1]
 
 
 F32 = jnp.float32
@@ -323,8 +370,8 @@
     return pl.BlockSpec((1, tiles, CR), lambda *_: (c, 0, 0), memory_space=VMEM)
 
 
-def params(mib):
-    return pltpu.CompilerParams(vmem_limit_bytes=mib << 20)
+def params():
+    return pltpu.CompilerParams(vmem_limit_bytes=VMEM_MIB << 20)
 
 
 def bubble_scratch(amounts):
@@ -339,32 +386,37 @@
         first_bubbles_kernel,
         grid=(1,),
         in_specs=[pl.BlockSpec(memory_space=SMEM)] * 3
-        + [whole((NBLK, COMPS, BB)), component(0, ntile), component(3, ntile)],
+        + [whole((COMPS, NBLK, BB)), component(0, ntile), component(3, ntile)],
         out_specs=[whole((peers, PACK, BB)), whole((ntile, CR))],
         out_shape=[SHAPE((peers, PACK, BB), F32), SHAPE((ntile, CR), F32)],
         scratch_shapes=bubble_scratch(1),
-        compiler_params=params(24),
-        cost_estimate=pl.CostEstimate(flops=10**9, bytes_accessed=40 * 10**6, transcendentals=10**7),
+        compiler_params=params(),
+        cost_estimate=pl.CostEstimate(flops=10**9, bytes_accessed=10**8, transcendentals=10**7),
         name="first_bubbles",
     )(counts, order, tiles, bubbles, flow_rows, flow_rows)
 
 
-def second_bubbles(alive, tiles, packed, flow_rows):
+def second_bubbles(tiles, packed, flow_rows):
     ntile = flow_rows.shape[1]
     peers = NBLK // CAP
     return pl.pallas_call(
         second_bubbles_kernel,
         grid=(1,),
-        in_specs=[pl.BlockSpec(memory_space=SMEM)] * 2
+        in_specs=[pl.BlockSpec(memory_space=SMEM)]
         + [whole((peers, PACK, BB)), component(0, ntile), component(3, ntile)],
-        out_specs=[whole((NBLK, COMPS, BB)), whole((ntile, CR)), whole((ntile, CR))],
-        out_shape=[SHAPE((NBLK, COMPS, BB), F32), SHAPE((ntile, CR), F32), SHAPE((ntile, CR), F32)],
-        scratch_shapes=[SMEM((NBLK + 2 * GROUP,), jnp.int32), VMEM((NBLK, 8, BB), F32)]
+        out_specs=[whole((COMPS, NBLK, BB)), whole((ntile, CR)), whole((ntile, CR))],
+        out_shape=[SHAPE((COMPS, NBLK, BB), F32), SHAPE((ntile, CR), F32), SHAPE((ntile, CR), F32)],
+        scratch_shapes=[
+            SMEM((NBLK + 2 * GROUP,), jnp.int32),
+            SMEM((peers, BB), F32),
+            pltpu.SemaphoreType.DMA,
+            VMEM((NBLK, 8, BB), F32),
+        ]
         + bubble_scratch(2),
-        compiler_params=params(24),
-        cost_estimate=pl.CostEstimate(flops=10**9, bytes_accessed=40 * 10**6, transcendentals=10**7),
+        compiler_params=params(),
+        cost_estimate=pl.CostEstimate(flops=10**9, bytes_accessed=10**8, transcendentals=10**7),
         name="second_bubbles",
-    )(alive, tiles, packed, flow_rows, flow_rows)
+    )(tiles, packed, flow_rows, flow_rows)
 
 
 def fluid_update(flow, source, halos, with_faces):
@@ -372,18 +424,29 @@
     out_shape = [SHAPE(flow.shape, F32)]
     if with_faces:
         out_shape += [SHAPE((4, azims, CR), F32)] * 2 + [SHAPE((4, streams, CR), F32)] * 2
+    slab = STREAM_BLOCK
+    moving = pl.BlockSpec((4, slab, azims, CR), lambda i: (0, i, 0, 0))
+    along = pl.BlockSpec((4, slab, CR), lambda i: (0, i, 0))
+    fixed = pl.BlockSpec((4, azims, CR), lambda i: (0, 0, 0))
     return pl.pallas_call(
         fluid_kernel,
-        grid=(1,),
-        in_specs=[whole(flow.shape), whole((streams, azims, CR))]
-        + [whole((4, azims, CR))] * 2
-        + [whole((4, streams, CR))] * 2,
-        out_specs=[whole(s.shape) for s in out_shape],
+        grid=(streams // slab,),
+        in_specs=[
+            moving,
+            pl.BlockSpec((4, 1, azims, CR), lambda i: (0, jnp.maximum(i * slab - 1, 0), 0, 0)),
+            pl.BlockSpec((4, 1, azims, CR), lambda i: (0, jnp.minimum((i + 1) * slab, streams - 1), 0, 0)),
+            pl.BlockSpec((slab, azims, CR), lambda i: (i, 0, 0)),
+            fixed,
+            fixed,
+            along,
+            along,
+        ],
+        out_specs=[moving, fixed, fixed, along, along] if with_faces else [moving],
         out_shape=out_shape,
-        compiler_params=params(28),
-        cost_estimate=pl.CostEstimate(flops=10**8, bytes_accessed=10**7, transcendentals=0),
+        compiler_params=params(),
+        cost_estimate=pl.CostEstimate(flops=10**8, bytes_accessed=3 * 10**7, transcendentals=0),
         name="fluid",
-    )(flow, source.reshape(streams, azims, CR), *halos)
+    )(flow, flow, flow, source.reshape(streams, azims, CR), *halos)
 
 
 def exchange(head_stream, tail_stream, head_azim, tail_azim):
@@ -401,15 +464,15 @@
     halos = exchange(fluid[:, 0], fluid[:, -1], fluid[:, :, 0], fluid[:, :, -1])
     rows = fluid.reshape(4, -1, CR)
     packed, source = first_bubbles(
-        counts, outgoing_block_order, tiles_first_update, bubbles, rows
-    )
+        counts, outgoing_block_order, tiles_first_update, bubbles.transpose(1, 0, 2), rows
+    )
+    packed, halos = lax.optimization_barrier((packed, halos))
     arrived = lax.all_to_all(packed, ("stream", "azim"), split_axis=0, concat_axis=0, tiled=True)
     flow, *faces = fluid_update(fluid, source, halos, True)
     halos = exchange(*faces)
-    alive = (arrived[:, COMPS * CAP :, 0] > 0.5).astype(jnp.int32).reshape(-1)
-    moved, source, void = second_bubbles(alive, tiles_after, arrived, flow.reshape(4, -1, CR))
+    moved, source, void = second_bubbles(tiles_after, arrived, flow.reshape(4, -1, CR))
     (flow,) = fluid_update(flow, source, halos, False)
-    return flow, moved, void.reshape(fluid.shape[1:])
+    return flow, moved.transpose(1, 0, 2), void.reshape(fluid.shape[1:])
 
 
 def solution(mesh):

time: 160 us -> 142 us (0.89); the launches traced: 159 us -> 140 us
  Pallas kernels: 96.5 us -> 83.2 us
  starting transfers between devices: 32.8 us -> 45.4 us
  local copies, waits for them, and re-layouts: 14.7 us -> 4.48 us
  waiting for transfers between devices: 11.6 us -> 4.98 us
  other arithmetic: 2.23 us -> 0 us
    pallas_call x1, Pallas kernels: 48.5 us -> 30.1 us  [first_bubbles(): pl.pallas_call(first_bubbles_kernel, grid=(1,), in_specs=[pl.BlockSpec(me...]
    all_to_all x1, starting transfers between devices: 10.8 us -> 21.3 us  [on_device(): lax.all_to_all(packed, ('stream', 'azim'), split_axis=0, concat_axis=0, t...]
    unnamed x18, local copies, waits for them, and re-layouts: 12 us -> 1.86 us
    ppermute x2, waiting for transfers between devices: 9 us -> 0.01 us  [exchange(): lax.ppermute(tail_azim, 'azim', [(i, (i + 1) % azims) for i in range(azim...]
    all_to_all x1, waiting for transfers between devices: 0.01 us -> 4.96 us  [on_device(): lax.all_to_all(packed, ('stream', 'azim'), split_axis=0, concat_axis=0, t...]
    pallas_call x1, Pallas kernels: 32.1 us -> 36.2 us  [second_bubbles(): pl.pallas_call(second_bubbles_kernel, grid=(1,), in_specs=[pl.BlockSpec(m...]
    ppermute x2, waiting for transfers between devices: 2.6 us -> 0.01 us  [exchange(): lax.ppermute(head_stream, 'stream', [(i + 1, i) for i in range(streams -...]
    convert_element_type x1 -> x0, other arithmetic: 2.23 us -> none  [on_device(): alive = (arrived[:, COMPS * CAP:, 0] > 0.5).astype(jnp.int32).reshape(-1)]
  transfers between devices with their start and end apart: 9 -> 9, of which waited for: 2 -> 1; matrix products, arithmetic and copies ran while one was open for 4% -> 1% of each run, Pallas kernels for 25% -> 54%
where the time goes in v2:
time: 142 us; the launch traced here: 140 us
  Pallas kernels  83.2 us (59%)
  starting transfers between devices  45.4 us (32%)
  waiting for transfers between devices  4.98 us (4%)
  local copies, waits for them, and re-layouts  4.48 us (3%)
  between operations  1.48 us (1%)
    pallas_call x1, Pallas kernels, second_bubbles(): pl.pallas_call(second_bubbles_kernel, grid=(1,), in_specs=[pl.BlockSpec(m...  36.2 us
    pallas_call x1, Pallas kernels, first_bubbles(): pl.pallas_call(first_bubbles_kernel, grid=(1,), in_specs=[pl.BlockSpec(me...  30.1 us
    all_to_all x1, starting transfers between devices, on_device(): lax.all_to_all(packed, ('stream', 'azim'), split_axis=0, concat_axis=0, t...  21.3 us
    pallas_call x2, Pallas kernels, fluid_update(): pl.pallas_call(fluid_kernel, grid=(streams // slab,), in_specs=[moving, p...  16.9 us
    ppermute x2, starting transfers between devices, exchange(): lax.ppermute(head_azim, 'azim', [((i + 1) % azims, i) for i in range(azim...  8.93 us
    ppermute x2, starting transfers between devices, exchange(): lax.ppermute(tail_stream, 'stream', [(i, i + 1) for i in range(streams -...  6.77 us
    all_to_all x1, waiting for transfers between devices, on_device(): lax.all_to_all(packed, ('stream', 'azim'), split_axis=0, concat_axis=0, t...  4.96 us
    ppermute x2, starting transfers between devices, exchange(): lax.ppermute(head_stream, 'stream', [(i + 1, i) for i in range(streams -...  4.78 us
  transfers between devices with their start and end apart: 9, of which 1 were waited for; matrix products, arithmetic and copies ran while one was open for 1% of the time, Pallas kernels for 54%

profile of v2, /device:TPU:1, one launch (start us, length us, event | category | flops | bytes accessed | tf_op | source)
XLA Modules:
  0.0 139.5 jit_solution(9884227542766714028)
XLA Ops:
  0.6 1.7 %fusion = (f32[4,64,1,128]{3,2,1,0:T(1,128)S(1)}, f32[4,64,1,128]{3,2,1,0:T(1,128)S(1)}) fusion(f32[4,64,32,128]{3,2,1,0:T(8,128)} %flow_after.1), kind=kLoop, calls=%fused_computation.2 | loop fusion | bytes 524288 | tf_op jit(solution)/shard_map/slice | solution.py:464
  2.4 2.1 %collective-permute-start.2 = (f32[4,64,128]{2,1,0:T(8,128)S(1)}, f32[4,64,128]{2,1,0:T(8,128)S(1)}, u32[]{:S(2)}, u32[]{:S(2)}) collective-permute-start(f32[4,64,128]{2,1,0:T(8,128)S(1)} %bitcast.28), channel_id=1, source_target_pairs={{0,1},{1,2},{2,3},{3,4},{4,5},{5,6},{6,7},{7,8},{8,9},{9,10},{10,1... | collective-permute-start | bytes 393224 | tf_op jit(solution)/shard_map/ppermute | solution.py:458
  4.5 4.8 %collective-permute-start.3 = (f32[4,64,128]{2,1,0:T(8,128)S(1)}, f32[4,64,128]{2,1,0:T(8,128)S(1)}, u32[]{:S(2)}, u32[]{:S(2)}) collective-permute-start(f32[4,64,128]{2,1,0:T(8,128)S(1)} %bitcast.27), channel_id=1, source_target_pairs={{1,0},{2,1},{3,2},{4,3},{5,4},{6,5},{7,6},{8,7},{9,8},{10,9},{11,1... | collective-permute-start | bytes 393224 | tf_op jit(solution)/shard_map/ppermute | solution.py:459
  9.3 0.9 slice_bitcast_fusion
  10.2 2.9 %collective-permute-start.1 = (f32[4,32,128]{2,1,0:T(8,128)S(1)}, f32[4,32,128]{2,1,0:T(8,128)S(1)}, u32[]{:S(2)}, u32[]{:S(2)}) collective-permute-start(f32[4,32,128]{2,1,0:T(8,128)S(1)} %get-tuple-element.35), channel_id=1, source_target_pairs={{16,0},{32,16},{48,32},{64,48},{80,64},{96,80},{112,96},{17,1},{33... | collective-permute-start | bytes 196616 | tf_op jit(solution)/shard_map/ppermute | solution.py:457
  13.1 3.1 %collective-permute-start = (f32[4,32,128]{2,1,0:T(8,128)S(1)}, f32[4,32,128]{2,1,0:T(8,128)S(1)}, u32[]{:S(2)}, u32[]{:S(2)}) collective-permute-start(f32[4,32,128]{2,1,0:T(8,128)S(1)} %get-tuple-element.36), channel_id=1, source_target_pairs={{0,16},{16,32},{32,48},{48,64},{64,80},{80,96},{96,112},{1,17},{17... | collective-permute-start | bytes 196616 | tf_op jit(solution)/shard_map/ppermute | solution.py:456
  16.8 30.1 %first_bubbles.1 = (f32[128,24,128]{2,1,0:T(8,128)}, f32[2048,128]{1,0:T(8,128)}) custom-call(s32[1]{0:T(128)S(6)} %copy.17.counts, s32[512]{0:T(512)} %order.1, s32[512]{0:T(512)} %tiles.2, f32[5,512,128]{2,1,0:T(8,128)} %bitcast.29, f32[4,2048,128]{2,1,0:T(8,128)} %bitcast.21, f32[4,2048,128]{2,1,0:T(8,128)} %bitcast.22), custom_call_target="tpu_custom_call" | custom-call | flops 1000000000 | bytes 100000000 | tf_op jit(solution)/shard_map/first_bubbles/pallas_call | solution.py:385
  46.9 0.0 collective-permute-done.1.stream_after
  46.9 0.0 collective-permute-done.stream_before
  47.0 0.0 copy-start.6
  47.0 0.0 collective-permute-done.2.azim_before
  47.0 0.0 copy-start.1
  47.0 0.0 collective-permute-done.3.azim_after
  47.0 0.0 copy-start.2
  47.0 21.3 %all-to-all-start = ((f32[128,24,128]{2,1,0:T(8,128)}), f32[128,24,128]{2,1,0:T(8,128)S(1)}, u32[]{:S(2)}, u32[]{:S(2)}) async-start(f32[128,24,128]{2,1,0:T(8,128)} %get-tuple-element.25), calls=%async_computation | async-start | bytes 3145728 | tf_op jit(solution)/shard_map/all_to_all | solution.py:470
  68.4 8.6 %fluid.2 = (f32[4,64,32,128]{3,2,1,0:T(8,128)}, f32[4,32,128]{2,1,0:T(8,128)}, f32[4,32,128]{2,1,0:T(8,128)}, f32[4,64,128]{2,1,0:T(8,128)}, f32[4,64,128]{2,1,0:T(8,128)}) custom-call(f32[4,64,32,128]{3,2,1,0:T(8,128)} %flow_after.1, f32[4,64,32,128]{3,2,1,0:T(8,128)} %flow_after.1, f32[4,64,32,128]{3,2,1,0:T(8,128)} %flow_after.1, ...), custom_call_target="tpu_custom_call" | custom-call | flops 100000000 | bytes 30000000 | tf_op jit(solution)/shard_map/fluid/pallas_call | solution.py:431
  76.9 1.4 %collective-permute-start.6 = (f32[4,64,128]{2,1,0:T(8,128)}, f32[4,64,128]{2,1,0:T(8,128)S(1)}, u32[]{:S(2)}, u32[]{:S(2)}) collective-permute-start(f32[4,64,128]{2,1,0:T(8,128)} %get-tuple-element.29), channel_id=1, source_target_pairs={{0,1},{1,2},{2,3},{3,4},{4,5},{5,6},{6,7},{7,8},{8,9},{9,10},{10,1... | collective-permute-start | bytes 393224 | tf_op jit(solution)/shard_map/ppermute | solution.py:458
  78.4 4.1 %collective-permute-start.7 = (f32[4,64,128]{2,1,0:T(8,128)}, f32[4,64,128]{2,1,0:T(8,128)S(1)}, u32[]{:S(2)}, u32[]{:S(2)}) collective-permute-start(f32[4,64,128]{2,1,0:T(8,128)} %get-tuple-element.30), channel_id=1, source_target_pairs={{1,0},{2,1},{3,2},{4,3},{5,4},{6,5},{7,6},{8,7},{9,8},{10,9},{11,1... | collective-permute-start | bytes 393224 | tf_op jit(solution)/shard_map/ppermute | solution.py:459
  82.5 3.7 %collective-permute-start.4 = (f32[4,32,128]{2,1,0:T(8,128)}, f32[4,32,128]{2,1,0:T(8,128)S(1)}, u32[]{:S(2)}, u32[]{:S(2)}) collective-permute-start(f32[4,32,128]{2,1,0:T(8,128)} %get-tuple-element.27), channel_id=1, source_target_pairs={{0,16},{16,32},{32,48},{48,64},{64,80},{80,96},{96,112},{1,17},{17... | collective-permute-start | bytes 196616 | tf_op jit(solution)/shard_map/ppermute | solution.py:456
  86.2 1.9 %collective-permute-start.5 = (f32[4,32,128]{2,1,0:T(8,128)}, f32[4,32,128]{2,1,0:T(8,128)S(1)}, u32[]{:S(2)}, u32[]{:S(2)}) collective-permute-start(f32[4,32,128]{2,1,0:T(8,128)} %get-tuple-element.28), channel_id=1, source_target_pairs={{16,0},{32,16},{48,32},{64,48},{80,64},{96,80},{112,96},{17,1},{33... | collective-permute-start | bytes 196616 | tf_op jit(solution)/shard_map/ppermute | solution.py:457
  88.1 5.0 %all-to-all-done.packed = f32[128,24,128]{2,1,0:T(8,128)S(1)} async-done(((f32[128,24,128]{2,1,0:T(8,128)}), f32[128,24,128]{2,1,0:T(8,128)S(1)}, u32[]{:S(2)}, u32[]{:S(2)}) %all-to-all-start) | async-done | bytes 1572896 | tf_op jit(solution)/shard_map/all_to_all | solution.py:470
  93.1 1.1 copy-done
  94.2 36.2 %second_bubbles.1 = (f32[5,512,128]{2,1,0:T(8,128)}, f32[2048,128]{1,0:T(8,128)}, f32[2048,128]{1,0:T(8,128)}) custom-call(s32[512]{0:T(512)} %tiles.3, f32[128,24,128]{2,1,0:T(8,128)} %copy-done, f32[4,2048,128]{2,1,0:T(8,128)} %bitcast.23, f32[4,2048,128]{2,1,0:T(8,128)} %bitcast.24), custom_call_target="tpu_custom_call" | custom-call | flops 1000000000 | bytes 100000000 | tf_op jit(solution)/shard_map/second_bubbles/pallas_call | solution.py:402
  130.4 0.0 collective-permute-done.4.stream_before
  130.4 0.0 collective-permute-done.5.stream_after
  130.5 0.0 collective-permute-done.6.azim_before
  130.5 0.0 collective-permute-done.7.azim_after
  130.5 0.5 copy-done.7
  131.1 0.0 copy-done.8
  131.1 0.0 copy-done.3
  131.1 0.1 copy-done.4
  131.2 8.3 %fluid.3 = f32[4,64,32,128]{3,2,1,0:T(8,128)} custom-call(f32[4,64,32,128]{3,2,1,0:T(8,128)} %get-tuple-element.24.flow.flow_before.flow_after, f32[4,64,32,128]{3,2,1,0:T(8,128)} %get-tuple-element.24.flow.flow_before.flow_after, f32[4,64,32,128]{3,2,1,0:T(8,128)} %get-tuple-element.24.flow.flow_before.flow_after, f32[64,32,128]{2,1,0:T(8,128)} %bitcast.25, ...), custom_call_target="tpu_custom_call" | custom-call | flops 100000000 | bytes 30000000 | tf_op jit(solution)/shard_map/fluid/pallas_call | solution.py:431
  (10 shorter events, 0.0 us)
Async XLA Ops:
  2.4 44.6 %collective-permute-start.2 = (f32[4,64,128]{2,1,0:T(8,128)S(1)}, f32[4,64,128]{2,1,0:T(8,128)S(1)}, u32[]{:S(2)}, u32[]{:S(2)}) collective-permute-start(f32[4,64,128]{2,1,0:T(8,128)S(1)} %bitcast.28), channel_id=1, source_target_pairs={{0,1},{1,2},{2,3},{3,4},{4,5},{5,6},{6,7},{7,8},{8,9},{9,10},{10,1... | collective-permute-start | bytes 393224 | tf_op jit(solution)/shard_map/ppermute | solution.py:458
  4.5 42.5 %collective-permute-start.3 = (f32[4,64,128]{2,1,0:T(8,128)S(1)}, f32[4,64,128]{2,1,0:T(8,128)S(1)}, u32[]{:S(2)}, u32[]{:S(2)}) collective-permute-start(f32[4,64,128]{2,1,0:T(8,128)S(1)} %bitcast.27), channel_id=1, source_target_pairs={{1,0},{2,1},{3,2},{4,3},{5,4},{6,5},{7,6},{8,7},{9,8},{10,9},{11,1... | collective-permute-start | bytes 393224 | tf_op jit(solution)/shard_map/ppermute | solution.py:459
  10.2 36.8 %collective-permute-start.1 = (f32[4,32,128]{2,1,0:T(8,128)S(1)}, f32[4,32,128]{2,1,0:T(8,128)S(1)}, u32[]{:S(2)}, u32[]{:S(2)}) collective-permute-start(f32[4,32,128]{2,1,0:T(8,128)S(1)} %get-tuple-element.35), channel_id=1, source_target_pairs={{16,0},{32,16},{48,32},{64,48},{80,64},{96,80},{112,96},{17,1},{33... | collective-permute-start | bytes 196616 | tf_op jit(solution)/shard_map/ppermute | solution.py:457
  13.1 33.9 %collective-permute-start = (f32[4,32,128]{2,1,0:T(8,128)S(1)}, f32[4,32,128]{2,1,0:T(8,128)S(1)}, u32[]{:S(2)}, u32[]{:S(2)}) collective-permute-start(f32[4,32,128]{2,1,0:T(8,128)S(1)} %get-tuple-element.36), channel_id=1, source_target_pairs={{0,16},{16,32},{32,48},{48,64},{64,80},{80,96},{96,112},{1,17},{17... | collective-permute-start | bytes 196616 | tf_op jit(solution)/shard_map/ppermute | solution.py:456
  46.9 21.4 %copy-start.5 = (f32[4,32,128]{2,1,0:T(8,128)}, f32[4,32,128]{2,1,0:T(8,128)S(1)}, u32[]{:S(2)}) copy-start(f32[4,32,128]{2,1,0:T(8,128)S(1)} %collective-permute-done.1.stream_after) | copy-start | bytes 196612
  47.0 21.4 %copy-start.6 = (f32[4,32,128]{2,1,0:T(8,128)}, f32[4,32,128]{2,1,0:T(8,128)S(1)}, u32[]{:S(2)}) copy-start(f32[4,32,128]{2,1,0:T(8,128)S(1)} %collective-permute-done.stream_before) | copy-start | bytes 196612
  47.0 21.4 %copy-start.1 = (f32[4,64,128]{2,1,0:T(8,128)}, f32[4,64,128]{2,1,0:T(8,128)S(1)}, u32[]{:S(2)}) copy-start(f32[4,64,128]{2,1,0:T(8,128)S(1)} %collective-permute-done.2.azim_before) | copy-start | bytes 393220
  47.0 21.4 %copy-start.2 = (f32[4,64,128]{2,1,0:T(8,128)}, f32[4,64,128]{2,1,0:T(8,128)S(1)}, u32[]{:S(2)}) copy-start(f32[4,64,128]{2,1,0:T(8,128)S(1)} %collective-permute-done.3.azim_after) | copy-start | bytes 393220
  47.0 46.1 %all-to-all-start = ((f32[128,24,128]{2,1,0:T(8,128)}), f32[128,24,128]{2,1,0:T(8,128)S(1)}, u32[]{:S(2)}, u32[]{:S(2)}) async-start(f32[128,24,128]{2,1,0:T(8,128)} %get-tuple-element.25), calls=%async_computation | async-start | bytes 3145728 | tf_op jit(solution)/shard_map/all_to_all | solution.py:470
  76.9 53.5 %collective-permute-start.6 = (f32[4,64,128]{2,1,0:T(8,128)}, f32[4,64,128]{2,1,0:T(8,128)S(1)}, u32[]{:S(2)}, u32[]{:S(2)}) collective-permute-start(f32[4,64,128]{2,1,0:T(8,128)} %get-tuple-element.29), channel_id=1, source_target_pairs={{0,1},{1,2},{2,3},{3,4},{4,5},{5,6},{6,7},{7,8},{8,9},{9,10},{10,1... | collective-permute-start | bytes 393224 | tf_op jit(solution)/shard_map/ppermute | solution.py:458
  78.4 52.1 %collective-permute-start.7 = (f32[4,64,128]{2,1,0:T(8,128)}, f32[4,64,128]{2,1,0:T(8,128)S(1)}, u32[]{:S(2)}, u32[]{:S(2)}) collective-permute-start(f32[4,64,128]{2,1,0:T(8,128)} %get-tuple-element.30), channel_id=1, source_target_pairs={{1,0},{2,1},{3,2},{4,3},{5,4},{6,5},{7,6},{8,7},{9,8},{10,9},{11,1... | collective-permute-start | bytes 393224 | tf_op jit(solution)/shard_map/ppermute | solution.py:459
  82.5 47.9 %collective-permute-start.4 = (f32[4,32,128]{2,1,0:T(8,128)}, f32[4,32,128]{2,1,0:T(8,128)S(1)}, u32[]{:S(2)}, u32[]{:S(2)}) collective-permute-start(f32[4,32,128]{2,1,0:T(8,128)} %get-tuple-element.27), channel_id=1, source_target_pairs={{0,16},{16,32},{32,48},{48,64},{64,80},{80,96},{96,112},{1,17},{17... | collective-permute-start | bytes 196616 | tf_op jit(solution)/shard_map/ppermute | solution.py:456
  86.2 44.3 %collective-permute-start.5 = (f32[4,32,128]{2,1,0:T(8,128)}, f32[4,32,128]{2,1,0:T(8,128)S(1)}, u32[]{:S(2)}, u32[]{:S(2)}) collective-permute-start(f32[4,32,128]{2,1,0:T(8,128)} %get-tuple-element.28), channel_id=1, source_target_pairs={{16,0},{32,16},{48,32},{64,48},{80,64},{96,80},{112,96},{17,1},{33... | collective-permute-start | bytes 196616 | tf_op jit(solution)/shard_map/ppermute | solution.py:457
  93.1 1.1 copy-start
  130.4 0.6 copy-start.7
  130.5 0.6 copy-start.8
  130.5 0.7 copy-start.3
  130.5 0.7 copy-start.4

commit v3 on v2

--- a/solution.py
+++ b/solution.py
@@ -29,8 +29,10 @@
 CAP = 4
 PACK = 24
 GROUP = 8
-STREAM_BLOCK = 8
+STREAM_BLOCK = 32
 VMEM_MIB = 58
+FIRST_BATCH = 64
+SECOND_BATCH = 32
 CHUNK = 64
 SHARP = 0.5 / (KERNEL_WIDTH * KERNEL_WIDTH) * LOG2_E
 VMEM = pltpu.VMEM
@@ -58,12 +60,11 @@
     scaled_cells[...] = index * SHARP
 
 
-def sample_phase(groups, positions, rows_p, rows_v, cells, scaled_cells, sampled_p, sampled_v):
+def sample_phase(size, batches, positions, tile_of, flow_p, flow_v, rows_p, rows_v, cells, scaled_cells, sampled_p, sampled_v):
     sublane = lax.broadcasted_iota(jnp.int32, (GROUP, BB), 0)
     ones = jnp.ones((16, CR), jnp.bfloat16)
 
-    def body(group, carry):
-        base = pl.multiple_of(group * GROUP, GROUP)
+    def one(base):
         here = pl.ds(base, GROUP)
         near, far = centre_terms(positions(here))
         rows = jnp.concatenate([rows_p[here, :], rows_v[here, :]], axis=0)
@@ -91,9 +92,21 @@
                 acc_n = jnp.where(mine, out[32:40], acc_n)
         sampled_p[here, :] = acc_p / acc_n
         sampled_v[here, :] = acc_v / acc_n
+
+    def gather(base):
+        for i in range(size):
+            tile = tile_of(base + i)
+            rows_p[pl.ds(base + i, 1), :] = flow_p[0, pl.ds(tile, 1), :]
+            rows_v[pl.ds(base + i, 1), :] = flow_v[0, pl.ds(tile, 1), :]
+
+    def body(batch, carry):
+        for sub in range(size // GROUP):
+            one(pl.multiple_of(batch * size + sub * GROUP, GROUP))
+        gather(jnp.minimum(batch + 1, batches - 1) * size)
         return carry
 
-    lax.fori_loop(0, groups, body, 0)
+    gather(0)
+    lax.fori_loop(0, batches, body, 0)
 
 
 def bubble_phase(chunks, component, state, sampled_p, sampled_v, source, void):
@@ -130,12 +143,11 @@
     lax.fori_loop(0, chunks, body, 0)
 
 
-def spread_phase(groups, live_blocks, tile_of, state, amounts, cells, scaled_cells, grids):
+def spread_phase(size, batches, live_blocks, tile_of, state, amounts, cells, scaled_cells, grids, beside):
     sublane = lax.broadcasted_iota(jnp.int32, (GROUP, BB), 0)
     kinds = len(amounts)
 
-    def body(group, carry):
-        base = pl.multiple_of(group * GROUP, GROUP)
+    def one(base):
         here = pl.ds(base, GROUP)
         near, far = centre_terms(state[here, 2, :])
         whole = jnp.concatenate([a[here, :] for a in amounts], axis=0)
@@ -165,129 +177,112 @@
                     )
         alive = sublane + base < live_blocks
         accs = [jnp.where(alive, acc, 0.0) for acc in accs]
-        for i in range(GROUP):
-            tile = tile_of(base + i)
-            for grid, acc in zip(grids, accs):
-                grid[pl.ds(tile, 1), :] = grid[pl.ds(tile, 1), :] + acc[i : i + 1]
+        return base, accs
+
+    def body(batch, carry):
+        done = [one(pl.multiple_of(batch * size + sub * GROUP, GROUP)) for sub in range(size // GROUP)]
+        for base, accs in done:
+            for i in range(GROUP):
+                tile = tile_of(base + i)
+                for grid, acc in zip(grids, accs):
+                    grid[pl.ds(tile, 1), :] = grid[pl.ds(tile, 1), :] + acc[i : i + 1]
+        beside(batch)
         return carry
 
-    lax.fori_loop(0, groups, body, 0)
+    lax.fori_loop(0, batches, body, 0)
 
 
 def first_bubbles_kernel(
     counts, order, tiles, bubbles, flow_p, flow_v, packed, source_grid,
     state, rows_p, rows_v, sampled_p, sampled_v, source, cells, scaled_cells,
 ):
+    size = FIRST_BATCH
     live = counts[0]
-    groups = (live + GROUP - 1) // GROUP
+    batches = (live + size - 1) // size
     chunks = (live + CHUNK - 1) // CHUNK
     fill_cells(cells, scaled_cells)
     source_grid[...] = jnp.zeros_like(source_grid)
 
-    def gather(group, carry):
-        base = pl.multiple_of(group * GROUP, GROUP)
-        for i in range(GROUP):
-            tile = tiles[base + i]
-            rows_p[pl.ds(base + i, 1), :] = flow_p[0, pl.ds(tile, 1), :]
-            rows_v[pl.ds(base + i, 1), :] = flow_v[0, pl.ds(tile, 1), :]
-        return carry
-
-    lax.fori_loop(0, groups, gather, 0)
     sample_phase(
-        groups, lambda here: bubbles[2, here, :], rows_p, rows_v, cells, scaled_cells, sampled_p, sampled_v
+        size, batches, lambda here: bubbles[2, here, :], lambda j: tiles[j], flow_p, flow_v, rows_p, rows_v,
+        cells, scaled_cells, sampled_p, sampled_v,
     )
     bubble_phase(
         chunks, lambda c, here: bubbles[c, here, :], state, sampled_p, sampled_v, source, None
     )
+    lane = lax.broadcasted_iota(jnp.int32, (PACK - COMPS * CAP, BB), 1)
+
+    def pack(batch):
+        for i in range(size // CAP):
+            peer = batch * (size // CAP) + i
+            flags = jnp.zeros((PACK - COMPS * CAP, BB), jnp.float32)
+            for k in range(CAP):
+                block = order[peer * CAP + k]
+                alive = block < live
+                packed[peer, COMPS * k : COMPS * (k + 1), :] = jnp.where(
+                    alive, state[block, 0:COMPS, :], 0.0
+                )
+                flags = jnp.where((lane == k) & alive, 1.0, flags)
+            packed[peer, COMPS * CAP : PACK, :] = flags
+
+    def pack_rest(batch, carry):
+        pack(batch)
+        return carry
+
     spread_phase(
-        groups, live, lambda j: tiles[j], state, [source], cells, scaled_cells, [source_grid]
-    )
-
-    lane = lax.broadcasted_iota(jnp.int32, (PACK - COMPS * CAP, BB), 1)
-
-    def pack(peer, carry):
-        flags = jnp.zeros((PACK - COMPS * CAP, BB), jnp.float32)
-        for k in range(CAP):
-            block = order[peer * CAP + k]
-            alive = block < live
-            packed[peer, COMPS * k : COMPS * (k + 1), :] = jnp.where(
-                alive, state[block, 0:COMPS, :], 0.0
-            )
-            flags = jnp.where((lane == k) & alive, 1.0, flags)
-        packed[peer, COMPS * CAP : PACK, :] = flags
-        return carry
-
-    lax.fori_loop(0, NBLK // CAP, pack, 0)
+        size, batches, live, lambda j: tiles[j], state, [source], cells, scaled_cells, [source_grid], pack
+    )
+    lax.fori_loop(batches, NBLK // size, pack_rest, 0)
 
 
 def second_bubbles_kernel(
     tiles, packed, flow_p, flow_v, bubbles_out, source_grid, void_grid,
-    slots, flags, flag_sem, arrived, state, rows_p, rows_v, sampled_p, sampled_v, source, void, cells, scaled_cells,
+    slots, flags, flag_sem, state, rows_p, rows_v, sampled_p, sampled_v, source, void, cells, scaled_cells,
 ):
+    size = SECOND_BATCH
     copy = pltpu.make_async_copy(packed.at[:, COMPS * CAP, :], flags, flag_sem)
     copy.start()
     fill_cells(cells, scaled_cells)
     source_grid[...] = jnp.zeros_like(source_grid)
     void_grid[...] = jnp.zeros_like(void_grid)
 
-    def unpack(peer, carry):
+    bubbles_out[...] = jnp.zeros_like(bubbles_out)
+    copy.wait()
+
+    def unpack(peer, live):
         for k in range(CAP):
-            arrived[peer * CAP + k, 0:COMPS, :] = packed[peer, COMPS * k : COMPS * (k + 1), :]
-        return carry
-
-    lax.fori_loop(0, NBLK // CAP, unpack, 0, unroll=4)
-    copy.wait()
-
-    def compact(peer, live):
-        for k in range(CAP):
-            slots[live] = peer * CAP + k
+            slot = peer * CAP + k
+            state[live, 0:COMPS, :] = packed[peer, COMPS * k : COMPS * (k + 1), :]
+            slots[live] = slot
             live = live + jnp.where(flags[peer, k] > 0.5, 1, 0)
         return live
 
-    live = lax.fori_loop(0, NBLK // CAP, compact, jnp.int32(0), unroll=4)
+    live = lax.fori_loop(0, NBLK // CAP, unpack, jnp.int32(0), unroll=4)
     last = slots[jnp.maximum(live - 1, 0)]
-    for i in range(GROUP):
+    for i in range(size):
         slots[live + i] = last
-    groups = (live + GROUP - 1) // GROUP
+        state[jnp.minimum(live + i, NBLK - 1), 0:COMPS, :] = state[jnp.maximum(live - 1, 0), 0:COMPS, :]
+    batches = (live + size - 1) // size
     chunks = (live + CHUNK - 1) // CHUNK
 
-    def gather(group, carry):
-        base = pl.multiple_of(group * GROUP, GROUP)
-        for i in range(GROUP):
-            slot = slots[base + i]
-            tile = tiles[slot]
-            rows_p[pl.ds(base + i, 1), :] = flow_p[0, pl.ds(tile, 1), :]
-            rows_v[pl.ds(base + i, 1), :] = flow_v[0, pl.ds(tile, 1), :]
-            state[base + i, 0:COMPS, :] = arrived[slot, 0:COMPS, :]
-        return carry
-
-    lax.fori_loop(0, groups, gather, 0)
     sample_phase(
-        groups, lambda here: state[here, 2, :], rows_p, rows_v, cells, scaled_cells, sampled_p, sampled_v
+        size, batches, lambda here: state[here, 2, :], lambda j: tiles[slots[j]], flow_p, flow_v, rows_p, rows_v,
+        cells, scaled_cells, sampled_p, sampled_v,
     )
     bubble_phase(
         chunks, lambda c, here: state[here, c, :], state, sampled_p, sampled_v, source, void
     )
-    arrived[...] = jnp.zeros_like(arrived)
-
-    def put(group, carry):
-        base = pl.multiple_of(group * GROUP, GROUP)
-        for i in range(GROUP):
-            arrived[slots[base + i]] = state[base + i]
-        return carry
-
-    lax.fori_loop(0, groups, put, 0)
-
-    def store(group, carry):
-        here = pl.ds(pl.multiple_of(group * GROUP, GROUP), GROUP)
-        for c in range(COMPS):
-            bubbles_out[c, here, :] = arrived[here, c, :]
-        return carry
-
-    lax.fori_loop(0, NBLK // GROUP, store, 0)
+
+    def put(batch):
+        for i in range(size):
+            j = batch * size + i
+            slot = slots[j]
+            for c in range(COMPS):
+                bubbles_out[c, pl.ds(slot, 1), :] = state[j, c : c + 1, :]
+
     spread_phase(
-        groups, live, lambda j: tiles[slots[j]], state, [source, void], cells, scaled_cells,
-        [source_grid, void_grid],
+        size, batches, live, lambda j: tiles[slots[j]], state, [source, void], cells, scaled_cells,
+        [source_grid, void_grid], put,
     )
 
 
@@ -407,10 +402,9 @@
         out_specs=[whole((COMPS, NBLK, BB)), whole((ntile, CR)), whole((ntile, CR))],
         out_shape=[SHAPE((COMPS, NBLK, BB), F32), SHAPE((ntile, CR), F32), SHAPE((ntile, CR), F32)],
         scratch_shapes=[
-            SMEM((NBLK + 2 * GROUP,), jnp.int32),
+            SMEM((NBLK + SECOND_BATCH,), jnp.int32),
             SMEM((peers, BB), F32),
             pltpu.SemaphoreType.DMA,
-            VMEM((NBLK, 8, BB), F32),
         ]
         + bubble_scratch(2),
         compiler_params=params(),

time: 142 us -> 113 us (0.80)
  Pallas kernels: 83.2 us -> 52.2 us
  waiting for transfers between devices: 4.98 us -> 6.87 us
  starting transfers between devices: 45.4 us -> 46.9 us
    pallas_call x1, Pallas kernels: 30.1 us -> 10.6 us  [first_bubbles(): pl.pallas_call(first_bubbles_kernel, grid=(1,), in_specs=[pl.BlockSpec(me...]
    pallas_call x1, Pallas kernels: 36.2 us -> 28.4 us  [second_bubbles(): pl.pallas_call(second_bubbles_kernel, grid=(1,), in_specs=[pl.BlockSpec(m...]
    pallas_call x2, Pallas kernels: 16.9 us -> 13.2 us  [fluid_update(): pl.pallas_call(fluid_kernel, grid=(streams // slab,), in_specs=[moving, p...]
    all_to_all x1, waiting for transfers between devices: 4.96 us -> 6.84 us  [on_device(): lax.all_to_all(packed, ('stream', 'azim'), split_axis=0, concat_axis=0, t...]
    all_to_all x1, starting transfers between devices: 21.3 us -> 22.8 us  [on_device(): lax.all_to_all(packed, ('stream', 'azim'), split_axis=0, concat_axis=0, t...]
  transfers between devices with their start and end apart: 9 -> 9, of which waited for: 1 -> 1; matrix products, arithmetic and copies ran while one was open for 1% -> 1% of each run, Pallas kernels for 54% -> 41%
where the time goes in v3:
time: 113 us; the launch traced here: 112 us
  Pallas kernels  52.2 us (46%)
  starting transfers between devices  46.9 us (42%)
  waiting for transfers between devices  6.87 us (6%)
  local copies, waits for them, and re-layouts  4.48 us (4%)
  between operations  1.47 us (1%)
    pallas_call x1, Pallas kernels, second_bubbles(): pl.pallas_call(second_bubbles_kernel, grid=(1,), in_specs=[pl.BlockSpec(m...  28.4 us
    all_to_all x1, starting transfers between devices, on_device(): lax.all_to_all(packed, ('stream', 'azim'), split_axis=0, concat_axis=0, t...  22.8 us
    pallas_call x2, Pallas kernels, fluid_update(): pl.pallas_call(fluid_kernel, grid=(streams // slab,), in_specs=[moving, p...  13.2 us
    pallas_call x1, Pallas kernels, first_bubbles(): pl.pallas_call(first_bubbles_kernel, grid=(1,), in_specs=[pl.BlockSpec(me...  10.6 us
    ppermute x2, starting transfers between devices, exchange(): lax.ppermute(head_azim, 'azim', [((i + 1) % azims, i) for i in range(azim...  8.93 us
    all_to_all x1, waiting for transfers between devices, on_device(): lax.all_to_all(packed, ('stream', 'azim'), split_axis=0, concat_axis=0, t...  6.84 us
    ppermute x2, starting transfers between devices, exchange(): lax.ppermute(tail_stream, 'stream', [(i, i + 1) for i in range(streams -...  6.77 us
    ppermute x2, starting transfers between devices, exchange(): lax.ppermute(head_stream, 'stream', [(i + 1, i) for i in range(streams -...  4.78 us
  transfers between devices with their start and end apart: 9, of which 1 were waited for; matrix products, arithmetic and copies ran while one was open for 1% of the time, Pallas kernels for 41%

profile of v3, /device:TPU:1, one launch (start us, length us, event | category | flops | bytes accessed | tf_op | source)
XLA Modules:
  0.0 111.8 jit_solution(4608114160483105435)
XLA Ops:
  0.6 1.7 %fusion = (f32[4,64,1,128]{3,2,1,0:T(1,128)S(1)}, f32[4,64,1,128]{3,2,1,0:T(1,128)S(1)}) fusion(f32[4,64,32,128]{3,2,1,0:T(8,128)} %flow_after.1), kind=kLoop, calls=%fused_computation.2 | loop fusion | bytes 524288 | tf_op jit(solution)/shard_map/slice | solution.py:458
  2.4 2.1 %collective-permute-start.2 = (f32[4,64,128]{2,1,0:T(8,128)S(1)}, f32[4,64,128]{2,1,0:T(8,128)S(1)}, u32[]{:S(2)}, u32[]{:S(2)}) collective-permute-start(f32[4,64,128]{2,1,0:T(8,128)S(1)} %bitcast.28), channel_id=1, source_target_pairs={{0,1},{1,2},{2,3},{3,4},{4,5},{5,6},{6,7},{7,8},{8,9},{9,10},{10,1... | collective-permute-start | bytes 393224 | tf_op jit(solution)/shard_map/ppermute | solution.py:452
  4.5 4.8 %collective-permute-start.3 = (f32[4,64,128]{2,1,0:T(8,128)S(1)}, f32[4,64,128]{2,1,0:T(8,128)S(1)}, u32[]{:S(2)}, u32[]{:S(2)}) collective-permute-start(f32[4,64,128]{2,1,0:T(8,128)S(1)} %bitcast.27), channel_id=1, source_target_pairs={{1,0},{2,1},{3,2},{4,3},{5,4},{6,5},{7,6},{8,7},{9,8},{10,9},{11,1... | collective-permute-start | bytes 393224 | tf_op jit(solution)/shard_map/ppermute | solution.py:453
  9.3 0.9 slice_bitcast_fusion
  10.2 2.9 %collective-permute-start.1 = (f32[4,32,128]{2,1,0:T(8,128)S(1)}, f32[4,32,128]{2,1,0:T(8,128)S(1)}, u32[]{:S(2)}, u32[]{:S(2)}) collective-permute-start(f32[4,32,128]{2,1,0:T(8,128)S(1)} %get-tuple-element.35), channel_id=1, source_target_pairs={{16,0},{32,16},{48,32},{64,48},{80,64},{96,80},{112,96},{17,1},{33... | collective-permute-start | bytes 196616 | tf_op jit(solution)/shard_map/ppermute | solution.py:451
  13.1 3.1 %collective-permute-start = (f32[4,32,128]{2,1,0:T(8,128)S(1)}, f32[4,32,128]{2,1,0:T(8,128)S(1)}, u32[]{:S(2)}, u32[]{:S(2)}) collective-permute-start(f32[4,32,128]{2,1,0:T(8,128)S(1)} %get-tuple-element.36), channel_id=1, source_target_pairs={{0,16},{16,32},{32,48},{48,64},{64,80},{80,96},{96,112},{1,17},{17... | collective-permute-start | bytes 196616 | tf_op jit(solution)/shard_map/ppermute | solution.py:450
  16.8 10.6 %first_bubbles.1 = (f32[128,24,128]{2,1,0:T(8,128)}, f32[2048,128]{1,0:T(8,128)}) custom-call(s32[1]{0:T(128)S(6)} %copy.17.counts, s32[512]{0:T(512)} %order.1, s32[512]{0:T(512)} %tiles.2, f32[5,512,128]{2,1,0:T(8,128)} %bitcast.29, f32[4,2048,128]{2,1,0:T(8,128)} %bitcast.21, f32[4,2048,128]{2,1,0:T(8,128)} %bitcast.22), custom_call_target="tpu_custom_call" | custom-call | flops 1000000000 | bytes 100000000 | tf_op jit(solution)/shard_map/first_bubbles/pallas_call | solution.py:380
  27.4 0.0 collective-permute-done.1.stream_after
  27.4 0.0 collective-permute-done.stream_before
  27.4 0.0 copy-start.6
  27.4 0.0 collective-permute-done.2.azim_before
  27.4 0.0 copy-start.1
  27.4 0.0 collective-permute-done.3.azim_after
  27.4 0.0 copy-start.2
  27.5 22.8 %all-to-all-start = ((f32[128,24,128]{2,1,0:T(8,128)}), f32[128,24,128]{2,1,0:T(8,128)S(1)}, u32[]{:S(2)}, u32[]{:S(2)}) async-start(f32[128,24,128]{2,1,0:T(8,128)} %get-tuple-element.25), calls=%async_computation | async-start | bytes 3145728 | tf_op jit(solution)/shard_map/all_to_all | solution.py:464
  50.3 6.7 %fluid.2 = (f32[4,64,32,128]{3,2,1,0:T(8,128)}, f32[4,32,128]{2,1,0:T(8,128)}, f32[4,32,128]{2,1,0:T(8,128)}, f32[4,64,128]{2,1,0:T(8,128)}, f32[4,64,128]{2,1,0:T(8,128)}) custom-call(f32[4,64,32,128]{3,2,1,0:T(8,128)} %flow_after.1, f32[4,64,32,128]{3,2,1,0:T(8,128)} %flow_after.1, f32[4,64,32,128]{3,2,1,0:T(8,128)} %flow_after.1, ...), custom_call_target="tpu_custom_call" | custom-call | flops 100000000 | bytes 30000000 | tf_op jit(solution)/shard_map/fluid/pallas_call | solution.py:425
  57.0 1.4 %collective-permute-start.6 = (f32[4,64,128]{2,1,0:T(8,128)}, f32[4,64,128]{2,1,0:T(8,128)S(1)}, u32[]{:S(2)}, u32[]{:S(2)}) collective-permute-start(f32[4,64,128]{2,1,0:T(8,128)} %get-tuple-element.29), channel_id=1, source_target_pairs={{0,1},{1,2},{2,3},{3,4},{4,5},{5,6},{6,7},{7,8},{8,9},{9,10},{10,1... | collective-permute-start | bytes 393224 | tf_op jit(solution)/shard_map/ppermute | solution.py:452
  58.4 4.1 %collective-permute-start.7 = (f32[4,64,128]{2,1,0:T(8,128)}, f32[4,64,128]{2,1,0:T(8,128)S(1)}, u32[]{:S(2)}, u32[]{:S(2)}) collective-permute-start(f32[4,64,128]{2,1,0:T(8,128)} %get-tuple-element.30), channel_id=1, source_target_pairs={{1,0},{2,1},{3,2},{4,3},{5,4},{6,5},{7,6},{8,7},{9,8},{10,9},{11,1... | collective-permute-start | bytes 393224 | tf_op jit(solution)/shard_map/ppermute | solution.py:453
  62.5 3.7 %collective-permute-start.4 = (f32[4,32,128]{2,1,0:T(8,128)}, f32[4,32,128]{2,1,0:T(8,128)S(1)}, u32[]{:S(2)}, u32[]{:S(2)}) collective-permute-start(f32[4,32,128]{2,1,0:T(8,128)} %get-tuple-element.27), channel_id=1, source_target_pairs={{0,16},{16,32},{32,48},{48,64},{64,80},{80,96},{96,112},{1,17},{17... | collective-permute-start | bytes 196616 | tf_op jit(solution)/shard_map/ppermute | solution.py:450
  66.2 1.9 %collective-permute-start.5 = (f32[4,32,128]{2,1,0:T(8,128)}, f32[4,32,128]{2,1,0:T(8,128)S(1)}, u32[]{:S(2)}, u32[]{:S(2)}) collective-permute-start(f32[4,32,128]{2,1,0:T(8,128)} %get-tuple-element.28), channel_id=1, source_target_pairs={{16,0},{32,16},{48,32},{64,48},{80,64},{96,80},{112,96},{17,1},{33... | collective-permute-start | bytes 196616 | tf_op jit(solution)/shard_map/ppermute | solution.py:451
  68.2 6.8 %all-to-all-done.packed = f32[128,24,128]{2,1,0:T(8,128)S(1)} async-done(((f32[128,24,128]{2,1,0:T(8,128)}), f32[128,24,128]{2,1,0:T(8,128)S(1)}, u32[]{:S(2)}, u32[]{:S(2)}) %all-to-all-start) | async-done | bytes 1572896 | tf_op jit(solution)/shard_map/all_to_all | solution.py:464
  75.0 1.1 %copy-done = f32[128,24,128]{2,1,0:T(8,128)} copy-done((f32[128,24,128]{2,1,0:T(8,128)}, f32[128,24,128]{2,1,0:T(8,128)S(1)}, u32[]{:S(2)}) %copy-start) | copy-done | bytes 1572888
  76.1 28.4 %second_bubbles.1 = (f32[5,512,128]{2,1,0:T(8,128)}, f32[2048,128]{1,0:T(8,128)}, f32[2048,128]{1,0:T(8,128)}) custom-call(s32[512]{0:T(512)} %tiles.3, f32[128,24,128]{2,1,0:T(8,128)} %copy-done, f32[4,2048,128]{2,1,0:T(8,128)} %bitcast.23, f32[4,2048,128]{2,1,0:T(8,128)} %bitcast.24), custom_call_target="tpu_custom_call" | custom-call | flops 1000000000 | bytes 100000000 | tf_op jit(solution)/shard_map/second_bubbles/pallas_call | solution.py:397
  104.6 0.0 collective-permute-done.4.stream_before
  104.6 0.0 collective-permute-done.5.stream_after
  104.6 0.0 collective-permute-done.6.azim_before
  104.6 0.0 collective-permute-done.7.azim_after
  104.7 0.5 copy-done.7
  105.2 0.0 copy-done.8
  105.2 0.0 copy-done.3
  105.3 0.1 copy-done.4
  105.3 6.5 %fluid.3 = f32[4,64,32,128]{3,2,1,0:T(8,128)} custom-call(f32[4,64,32,128]{3,2,1,0:T(8,128)} %get-tuple-element.24.flow.flow_before.flow_after, f32[4,64,32,128]{3,2,1,0:T(8,128)} %get-tuple-element.24.flow.flow_before.flow_after, f32[4,64,32,128]{3,2,1,0:T(8,128)} %get-tuple-element.24.flow.flow_before.flow_after, f32[64,32,128]{2,1,0:T(8,128)} %bitcast.25, ...), custom_call_target="tpu_custom_call" | custom-call | flops 100000000 | bytes 30000000 | tf_op jit(solution)/shard_map/fluid/pallas_call | solution.py:425
  (10 shorter events, 0.0 us)
Async XLA Ops:
  2.4 25.0 %collective-permute-start.2 = (f32[4,64,128]{2,1,0:T(8,128)S(1)}, f32[4,64,128]{2,1,0:T(8,128)S(1)}, u32[]{:S(2)}, u32[]{:S(2)}) collective-permute-start(f32[4,64,128]{2,1,0:T(8,128)S(1)} %bitcast.28), channel_id=1, source_target_pairs={{0,1},{1,2},{2,3},{3,4},{4,5},{5,6},{6,7},{7,8},{8,9},{9,10},{10,1... | collective-permute-start | bytes 393224 | tf_op jit(solution)/shard_map/ppermute | solution.py:452
  4.5 23.0 %collective-permute-start.3 = (f32[4,64,128]{2,1,0:T(8,128)S(1)}, f32[4,64,128]{2,1,0:T(8,128)S(1)}, u32[]{:S(2)}, u32[]{:S(2)}) collective-permute-start(f32[4,64,128]{2,1,0:T(8,128)S(1)} %bitcast.27), channel_id=1, source_target_pairs={{1,0},{2,1},{3,2},{4,3},{5,4},{6,5},{7,6},{8,7},{9,8},{10,9},{11,1... | collective-permute-start | bytes 393224 | tf_op jit(solution)/shard_map/ppermute | solution.py:453
  10.2 17.2 %collective-permute-start.1 = (f32[4,32,128]{2,1,0:T(8,128)S(1)}, f32[4,32,128]{2,1,0:T(8,128)S(1)}, u32[]{:S(2)}, u32[]{:S(2)}) collective-permute-start(f32[4,32,128]{2,1,0:T(8,128)S(1)} %get-tuple-element.35), channel_id=1, source_target_pairs={{16,0},{32,16},{48,32},{64,48},{80,64},{96,80},{112,96},{17,1},{33... | collective-permute-start | bytes 196616 | tf_op jit(solution)/shard_map/ppermute | solution.py:451
  13.1 14.3 %collective-permute-start = (f32[4,32,128]{2,1,0:T(8,128)S(1)}, f32[4,32,128]{2,1,0:T(8,128)S(1)}, u32[]{:S(2)}, u32[]{:S(2)}) collective-permute-start(f32[4,32,128]{2,1,0:T(8,128)S(1)} %get-tuple-element.36), channel_id=1, source_target_pairs={{0,16},{16,32},{32,48},{48,64},{64,80},{80,96},{96,112},{1,17},{17... | collective-permute-start | bytes 196616 | tf_op jit(solution)/shard_map/ppermute | solution.py:450
  27.4 22.9 %copy-start.5 = (f32[4,32,128]{2,1,0:T(8,128)}, f32[4,32,128]{2,1,0:T(8,128)S(1)}, u32[]{:S(2)}) copy-start(f32[4,32,128]{2,1,0:T(8,128)S(1)} %collective-permute-done.1.stream_after) | copy-start | bytes 196612
  27.4 22.9 %copy-start.6 = (f32[4,32,128]{2,1,0:T(8,128)}, f32[4,32,128]{2,1,0:T(8,128)S(1)}, u32[]{:S(2)}) copy-start(f32[4,32,128]{2,1,0:T(8,128)S(1)} %collective-permute-done.stream_before) | copy-start | bytes 196612
  27.4 22.9 %copy-start.1 = (f32[4,64,128]{2,1,0:T(8,128)}, f32[4,64,128]{2,1,0:T(8,128)S(1)}, u32[]{:S(2)}) copy-start(f32[4,64,128]{2,1,0:T(8,128)S(1)} %collective-permute-done.2.azim_before) | copy-start | bytes 393220
  27.4 22.9 %copy-start.2 = (f32[4,64,128]{2,1,0:T(8,128)}, f32[4,64,128]{2,1,0:T(8,128)S(1)}, u32[]{:S(2)}) copy-start(f32[4,64,128]{2,1,0:T(8,128)S(1)} %collective-permute-done.3.azim_after) | copy-start | bytes 393220
  27.5 47.5 %all-to-all-start = ((f32[128,24,128]{2,1,0:T(8,128)}), f32[128,24,128]{2,1,0:T(8,128)S(1)}, u32[]{:S(2)}, u32[]{:S(2)}) async-start(f32[128,24,128]{2,1,0:T(8,128)} %get-tuple-element.25), calls=%async_computation | async-start | bytes 3145728 | tf_op jit(solution)/shard_map/all_to_all | solution.py:464
  57.0 47.6 %collective-permute-start.6 = (f32[4,64,128]{2,1,0:T(8,128)}, f32[4,64,128]{2,1,0:T(8,128)S(1)}, u32[]{:S(2)}, u32[]{:S(2)}) collective-permute-start(f32[4,64,128]{2,1,0:T(8,128)} %get-tuple-element.29), channel_id=1, source_target_pairs={{0,1},{1,2},{2,3},{3,4},{4,5},{5,6},{6,7},{7,8},{8,9},{9,10},{10,1... | collective-permute-start | bytes 393224 | tf_op jit(solution)/shard_map/ppermute | solution.py:452
  58.4 46.2 %collective-permute-start.7 = (f32[4,64,128]{2,1,0:T(8,128)}, f32[4,64,128]{2,1,0:T(8,128)S(1)}, u32[]{:S(2)}, u32[]{:S(2)}) collective-permute-start(f32[4,64,128]{2,1,0:T(8,128)} %get-tuple-element.30), channel_id=1, source_target_pairs={{1,0},{2,1},{3,2},{4,3},{5,4},{6,5},{7,6},{8,7},{9,8},{10,9},{11,1... | collective-permute-start | bytes 393224 | tf_op jit(solution)/shard_map/ppermute | solution.py:453
  62.5 42.0 %collective-permute-start.4 = (f32[4,32,128]{2,1,0:T(8,128)}, f32[4,32,128]{2,1,0:T(8,128)S(1)}, u32[]{:S(2)}, u32[]{:S(2)}) collective-permute-start(f32[4,32,128]{2,1,0:T(8,128)} %get-tuple-element.27), channel_id=1, source_target_pairs={{0,16},{16,32},{32,48},{48,64},{64,80},{80,96},{96,112},{1,17},{17... | collective-permute-start | bytes 196616 | tf_op jit(solution)/shard_map/ppermute | solution.py:450
  66.2 38.4 %collective-permute-start.5 = (f32[4,32,128]{2,1,0:T(8,128)}, f32[4,32,128]{2,1,0:T(8,128)S(1)}, u32[]{:S(2)}, u32[]{:S(2)}) collective-permute-start(f32[4,32,128]{2,1,0:T(8,128)} %get-tuple-element.28), channel_id=1, source_target_pairs={{16,0},{32,16},{48,32},{64,48},{80,64},{96,80},{112,96},{17,1},{33... | collective-permute-start | bytes 196616 | tf_op jit(solution)/shard_map/ppermute | solution.py:451
  75.0 1.1 %copy-start = (f32[128,24,128]{2,1,0:T(8,128)}, f32[128,24,128]{2,1,0:T(8,128)S(1)}, u32[]{:S(2)}) copy-start(f32[128,24,128]{2,1,0:T(8,128)S(1)} %all-to-all-done.packed) | copy-start | bytes 4718596
  104.6 0.6 copy-start.7
  104.6 0.6 copy-start.8
  104.6 0.7 copy-start.3
  104.6 0.7 copy-start.4

commit v4 on v3

--- a/solution.py
+++ b/solution.py
@@ -109,7 +109,7 @@
     lax.fori_loop(0, batches, body, 0)
 
 
-def bubble_phase(chunks, component, state, sampled_p, sampled_v, source, void):
+def bubble_phase(chunks, component, state, sampled_p, sampled_v, places, source, void):
     h = TIME_STEP / SUBSTEPS
 
     def body(chunk, carry):
@@ -134,6 +134,7 @@
         state[here, 2, :] = position
         state[here, 3, :] = speed
         state[here, 4, :] = component(4, here)
+        places[here, :] = position
         area = radius * radius
         source[here, :] = (SOURCE_GAIN * FOUR_PI) * area * growth
         if void is not None:
@@ -143,13 +144,13 @@
     lax.fori_loop(0, chunks, body, 0)
 
 
-def spread_phase(size, batches, live_blocks, tile_of, state, amounts, cells, scaled_cells, grids, beside):
+def spread_phase(size, batches, live_blocks, tile_of, places, amounts, cells, scaled_cells, grids, beside):
     sublane = lax.broadcasted_iota(jnp.int32, (GROUP, BB), 0)
     kinds = len(amounts)
 
     def one(base):
         here = pl.ds(base, GROUP)
-        near, far = centre_terms(state[here, 2, :])
+        near, far = centre_terms(places[here, :])
         whole = jnp.concatenate([a[here, :] for a in amounts], axis=0)
         accs = [jnp.zeros((GROUP, CR), jnp.float32) for _ in amounts]
         for i in range(0, GROUP, 2):
@@ -186,58 +187,96 @@
                 tile = tile_of(base + i)
                 for grid, acc in zip(grids, accs):
                     grid[pl.ds(tile, 1), :] = grid[pl.ds(tile, 1), :] + acc[i : i + 1]
-        beside(batch)
+        if beside is not None:
+            beside(batch)
         return carry
 
     lax.fori_loop(0, batches, body, 0)
 
 
 def first_bubbles_kernel(
-    counts, order, tiles, bubbles, flow_p, flow_v, packed, source_grid,
-    state, rows_p, rows_v, sampled_p, sampled_v, source, cells, scaled_cells,
+    counts, order, tiles, bubbles, flow_p, flow_v, packed, places, source,
+    state, rows_p, rows_v, sampled_p, sampled_v, cells, scaled_cells,
 ):
     size = FIRST_BATCH
     live = counts[0]
     batches = (live + size - 1) // size
     chunks = (live + CHUNK - 1) // CHUNK
     fill_cells(cells, scaled_cells)
-    source_grid[...] = jnp.zeros_like(source_grid)
-
     sample_phase(
         size, batches, lambda here: bubbles[2, here, :], lambda j: tiles[j], flow_p, flow_v, rows_p, rows_v,
         cells, scaled_cells, sampled_p, sampled_v,
     )
     bubble_phase(
-        chunks, lambda c, here: bubbles[c, here, :], state, sampled_p, sampled_v, source, None
+        chunks, lambda c, here: bubbles[c, here, :], state, sampled_p, sampled_v, places, source, None
     )
     lane = lax.broadcasted_iota(jnp.int32, (PACK - COMPS * CAP, BB), 1)
 
-    def pack(batch):
-        for i in range(size // CAP):
-            peer = batch * (size // CAP) + i
-            flags = jnp.zeros((PACK - COMPS * CAP, BB), jnp.float32)
-            for k in range(CAP):
-                block = order[peer * CAP + k]
-                alive = block < live
-                packed[peer, COMPS * k : COMPS * (k + 1), :] = jnp.where(
-                    alive, state[block, 0:COMPS, :], 0.0
-                )
-                flags = jnp.where((lane == k) & alive, 1.0, flags)
-            packed[peer, COMPS * CAP : PACK, :] = flags
-
-    def pack_rest(batch, carry):
-        pack(batch)
+    def pack(peer, carry):
+        flags = jnp.zeros((PACK - COMPS * CAP, BB), jnp.float32)
+        for k in range(CAP):
+            block = order[peer * CAP + k]
+            alive = block < live
+            packed[peer, COMPS * k : COMPS * (k + 1), :] = jnp.where(
+                alive, state[block, 0:COMPS, :], 0.0
+            )
+            flags = jnp.where((lane == k) & alive, 1.0, flags)
+        packed[peer, COMPS * CAP : PACK, :] = flags
         return carry
 
-    spread_phase(
-        size, batches, live, lambda j: tiles[j], state, [source], cells, scaled_cells, [source_grid], pack
-    )
-    lax.fori_loop(batches, NBLK // size, pack_rest, 0)
-
-
-def second_bubbles_kernel(
-    tiles, packed, flow_p, flow_v, bubbles_out, source_grid, void_grid,
-    slots, flags, flag_sem, state, rows_p, rows_v, sampled_p, sampled_v, source, void, cells, scaled_cells,
+    lax.fori_loop(0, NBLK // CAP, pack, 0, unroll=8)
+
+
+def first_flow_kernel(
+    counts, tiles, places, source, flow, flow_before, flow_after, stream_before, stream_after, azim_before,
+    azim_after, new, face_0, face_1, face_2, face_3, source_grid, cells, scaled_cells,
+):
+    step = pl.program_id(0)
+
+    @pl.when(step == 0)
+    def _():
+        size = FIRST_BATCH
+        live = counts[0]
+        fill_cells(cells, scaled_cells)
+        source_grid[...] = jnp.zeros_like(source_grid)
+        spread_phase(
+            size, (live + size - 1) // size, live, lambda j: tiles[j], places, [source], cells, scaled_cells,
+            [source_grid], None,
+        )
+
+    @pl.when(step > 0)
+    def _():
+        flow_slab(
+            step - 1, pl.num_programs(0) - 1, flow, flow_before, flow_after, source_grid, stream_before,
+            stream_after, azim_before, azim_after, new, face_0, face_1, face_2, face_3,
+        )
+
+
+def second_kernel(
+    tiles, packed, flow_p, flow_v, flow, flow_before, flow_after, stream_before, stream_after, azim_before,
+    azim_after, new, bubbles_out, void_grid, slots, flags, flag_sem, source_grid, places, source, void,
+    *scratch,
+):
+    step = pl.program_id(0)
+
+    @pl.when(step == 0)
+    def _():
+        second_bubbles(
+            tiles, packed, flow_p, flow_v, bubbles_out, source_grid, void_grid, slots, flags, flag_sem,
+            places, source, void, *scratch,
+        )
+
+    @pl.when(step > 0)
+    def _():
+        flow_slab(
+            step - 1, pl.num_programs(0) - 1, flow, flow_before, flow_after, source_grid, stream_before,
+            stream_after, azim_before, azim_after, new,
+        )
+
+
+def second_bubbles(
+    tiles, packed, flow_p, flow_v, bubbles_out, source_grid, void_grid, slots, flags, flag_sem,
+    places, source, void, state, rows_p, rows_v, sampled_p, sampled_v, cells, scaled_cells,
 ):
     size = SECOND_BATCH
     copy = pltpu.make_async_copy(packed.at[:, COMPS * CAP, :], flags, flag_sem)
@@ -270,7 +309,7 @@
         cells, scaled_cells, sampled_p, sampled_v,
     )
     bubble_phase(
-        chunks, lambda c, here: state[here, c, :], state, sampled_p, sampled_v, source, void
+        chunks, lambda c, here: state[here, c, :], state, sampled_p, sampled_v, places, source, void
     )
 
     def put(batch):
@@ -281,16 +320,16 @@
                 bubbles_out[c, pl.ds(slot, 1), :] = state[j, c : c + 1, :]
 
     spread_phase(
-        size, batches, live, lambda j: tiles[slots[j]], state, [source, void], cells, scaled_cells,
+        size, batches, live, lambda j: tiles[slots[j]], places, [source, void], cells, scaled_cells,
         [source_grid, void_grid], put,
     )
 
 
-def fluid_kernel(
-    flow, flow_before, flow_after, source, stream_before, stream_after, azim_before, azim_after, new, *faces
+def flow_slab(
+    index, slabs, flow, flow_before, flow_after, source, stream_before, stream_after, azim_before,
+    azim_after, new, *faces,
 ):
-    step = pl.program_id(0)
-    first, final = step == 0, step == pl.num_programs(0) - 1
+    first, final = index == 0, index == slabs - 1
     streams = flow.shape[1]
     azims = flow.shape[2]
     shape = (azims, CR)
@@ -330,7 +369,7 @@
         for c in range(4):
             value = (1.0 - 6.0 * DIFFUSION) * values[c] + DIFFUSION * sums[c] - a * rates[c]
             if c == 0:
-                value = value - TIME_STEP * source[s]
+                value = value - TIME_STEP * source[pl.ds(pl.multiple_of((index * streams + s) * azims, azims), azims), :]
             new[c, s] = value
             if faces:
                 faces[2][c, pl.ds(s, 1), :] = value[0:1]
@@ -369,9 +408,8 @@
     return pltpu.CompilerParams(vmem_limit_bytes=VMEM_MIB << 20)
 
 
-def bubble_scratch(amounts):
-    wide = [VMEM((NBLK, BB), F32)] * (4 + amounts)
-    return [VMEM((NBLK, 8, BB), F32)] + wide + [VMEM((CR, BB), F32)] * 2
+def bubble_scratch():
+    return [VMEM((NBLK, 8, BB), F32)] + [VMEM((NBLK, BB), F32)] * 4 + [VMEM((CR, BB), F32)] * 2
 
 
 def first_bubbles(counts, order, tiles, bubbles, flow_rows):
@@ -382,65 +420,71 @@
         grid=(1,),
         in_specs=[pl.BlockSpec(memory_space=SMEM)] * 3
         + [whole((COMPS, NBLK, BB)), component(0, ntile), component(3, ntile)],
-        out_specs=[whole((peers, PACK, BB)), whole((ntile, CR))],
-        out_shape=[SHAPE((peers, PACK, BB), F32), SHAPE((ntile, CR), F32)],
-        scratch_shapes=bubble_scratch(1),
+        out_specs=[whole((peers, PACK, BB))] + [whole((NBLK, BB))] * 2,
+        out_shape=[SHAPE((peers, PACK, BB), F32)] + [SHAPE((NBLK, BB), F32)] * 2,
+        scratch_shapes=bubble_scratch(),
         compiler_params=params(),
         cost_estimate=pl.CostEstimate(flops=10**9, bytes_accessed=10**8, transcendentals=10**7),
         name="first_bubbles",
     )(counts, order, tiles, bubbles, flow_rows, flow_rows)
 
 
-def second_bubbles(tiles, packed, flow_rows):
-    ntile = flow_rows.shape[1]
+def slab_specs(streams, azims):
+    slab = STREAM_BLOCK
+    moving = pl.BlockSpec((4, slab, azims, CR), lambda i: (0, jnp.maximum(i - 1, 0), 0, 0))
+    before = pl.BlockSpec((4, 1, azims, CR), lambda i: (0, jnp.maximum((i - 1) * slab - 1, 0), 0, 0))
+    after = pl.BlockSpec(
+        (4, 1, azims, CR), lambda i: (0, jnp.minimum(jnp.maximum(i, 1) * slab, streams - 1), 0, 0)
+    )
+    along = pl.BlockSpec((4, slab, CR), lambda i: (0, jnp.maximum(i - 1, 0), 0))
+    fixed = whole((4, azims, CR))
+    return (1 + streams // slab,), [moving, before, after, fixed, fixed, along, along], moving, along, fixed
+
+
+def first_flow(counts, tiles, places, source, flow, halos):
+    streams, azims = flow.shape[1:3]
+    grid, slabs, moving, along, fixed = slab_specs(streams, azims)
+    return pl.pallas_call(
+        first_flow_kernel,
+        grid=grid,
+        in_specs=[pl.BlockSpec(memory_space=SMEM)] * 2 + [whole((NBLK, BB))] * 2 + slabs,
+        out_specs=[moving, fixed, fixed, along, along],
+        out_shape=[SHAPE(flow.shape, F32)]
+        + [SHAPE((4, azims, CR), F32)] * 2
+        + [SHAPE((4, streams, CR), F32)] * 2,
+        scratch_shapes=[VMEM((streams * azims, CR), F32)] + [VMEM((CR, BB), F32)] * 2,
+        compiler_params=params(),
+        cost_estimate=pl.CostEstimate(flops=10**9, bytes_accessed=8 * 10**7, transcendentals=10**7),
+        name="first_flow",
+    )(counts, tiles, places, source, flow, flow, flow, *halos)
+
+
+def second_update(tiles, packed, flow, halos):
+    streams, azims = flow.shape[1:3]
+    grid, slabs, moving, along, fixed = slab_specs(streams, azims)
+    ntile = streams * azims
     peers = NBLK // CAP
+    rows = flow.reshape(4, ntile, CR)
     return pl.pallas_call(
-        second_bubbles_kernel,
-        grid=(1,),
+        second_kernel,
+        grid=grid,
         in_specs=[pl.BlockSpec(memory_space=SMEM)]
-        + [whole((peers, PACK, BB)), component(0, ntile), component(3, ntile)],
-        out_specs=[whole((COMPS, NBLK, BB)), whole((ntile, CR)), whole((ntile, CR))],
-        out_shape=[SHAPE((COMPS, NBLK, BB), F32), SHAPE((ntile, CR), F32), SHAPE((ntile, CR), F32)],
+        + [whole((peers, PACK, BB)), component(0, ntile), component(3, ntile)]
+        + slabs,
+        out_specs=[moving, whole((COMPS, NBLK, BB)), whole((ntile, CR))],
+        out_shape=[SHAPE(flow.shape, F32), SHAPE((COMPS, NBLK, BB), F32), SHAPE((ntile, CR), F32)],
         scratch_shapes=[
             SMEM((NBLK + SECOND_BATCH,), jnp.int32),
             SMEM((peers, BB), F32),
             pltpu.SemaphoreType.DMA,
+            VMEM((ntile, CR), F32),
         ]
-        + bubble_scratch(2),
+        + [VMEM((NBLK, BB), F32)] * 3
+        + bubble_scratch(),
         compiler_params=params(),
         cost_estimate=pl.CostEstimate(flops=10**9, bytes_accessed=10**8, transcendentals=10**7),
-        name="second_bubbles",
-    )(tiles, packed, flow_rows, flow_rows)
-
-
-def fluid_update(flow, source, halos, with_faces):
-    streams, azims = flow.shape[1:3]
-    out_shape = [SHAPE(flow.shape, F32)]
-    if with_faces:
-        out_shape += [SHAPE((4, azims, CR), F32)] * 2 + [SHAPE((4, streams, CR), F32)] * 2
-    slab = STREAM_BLOCK
-    moving = pl.BlockSpec((4, slab, azims, CR), lambda i: (0, i, 0, 0))
-    along = pl.BlockSpec((4, slab, CR), lambda i: (0, i, 0))
-    fixed = pl.BlockSpec((4, azims, CR), lambda i: (0, 0, 0))
-    return pl.pallas_call(
-        fluid_kernel,
-        grid=(streams // slab,),
-        in_specs=[
-            moving,
-            pl.BlockSpec((4, 1, azims, CR), lambda i: (0, jnp.maximum(i * slab - 1, 0), 0, 0)),
-            pl.BlockSpec((4, 1, azims, CR), lambda i: (0, jnp.minimum((i + 1) * slab, streams - 1), 0, 0)),
-            pl.BlockSpec((slab, azims, CR), lambda i: (i, 0, 0)),
-            fixed,
-            fixed,
-            along,
-            along,
-        ],
-        out_specs=[moving, fixed, fixed, along, along] if with_faces else [moving],
-        out_shape=out_shape,
-        compiler_params=params(),
-        cost_estimate=pl.CostEstimate(flops=10**8, bytes_accessed=3 * 10**7, transcendentals=0),
-        name="fluid",
-    )(flow, flow, flow, source.reshape(streams, azims, CR), *halos)
+        name="second_update",
+    )(tiles, packed, rows, rows, flow, flow, flow, *halos)
 
 
 def exchange(head_stream, tail_stream, head_azim, tail_azim):
@@ -457,15 +501,13 @@
 def on_device(fluid, bubbles, counts, outgoing_block_order, tiles_first_update, tiles_after):
     halos = exchange(fluid[:, 0], fluid[:, -1], fluid[:, :, 0], fluid[:, :, -1])
     rows = fluid.reshape(4, -1, CR)
-    packed, source = first_bubbles(
+    packed, places, source = first_bubbles(
         counts, outgoing_block_order, tiles_first_update, bubbles.transpose(1, 0, 2), rows
     )
     packed, halos = lax.optimization_barrier((packed, halos))
     arrived = lax.all_to_all(packed, ("stream", "azim"), split_axis=0, concat_axis=0, tiled=True)
-    flow, *faces = fluid_update(fluid, source, halos, True)
-    halos = exchange(*faces)
-    moved, source, void = second_bubbles(tiles_after, arrived, flow.reshape(4, -1, CR))
-    (flow,) = fluid_update(flow, source, halos, False)
+    flow, *faces = first_flow(counts, tiles_first_update, places, source, fluid, halos)
+    flow, moved, void = second_update(tiles_after, arrived, flow, exchange(*faces))
     return flow, moved.transpose(1, 0, 2), void.reshape(fluid.shape[1:])
 
 

time: 113 us -> 107 us (0.947); the launches traced: 112 us -> 107 us
  starting transfers between devices: 46.9 us -> 32.4 us
  Pallas kernels: 52.2 us -> 65.6 us
  waiting for transfers between devices: 6.87 us -> 3.69 us
    all_to_all x1, starting transfers between devices: 22.8 us -> 6.77 us  [on_device(): lax.all_to_all(packed, ('stream', 'azim'), split_axis=0, concat_axis=0, t...]
    pallas_call x3 -> x2, Pallas kernels: 41.6 us -> 50.2 us  [the longest x1 33 us: second_update(): pl.pallas_call(second_kernel, grid=grid, in_specs=[pl.BlockSpec(memory_sp...]
    all_to_all x1, waiting for transfers between devices: 6.84 us -> 0.01 us  [on_device(): lax.all_to_all(packed, ('stream', 'azim'), split_axis=0, concat_axis=0, t...]
    pallas_call x1, Pallas kernels: 10.6 us -> 15.4 us  [first_bubbles(): pl.pallas_call(first_bubbles_kernel, grid=(1,), in_specs=[pl.BlockSpec(me...]
    ppermute x2, waiting for transfers between devices: 0.01 us -> 3.67 us  [exchange(): lax.ppermute(head_stream, 'stream', [(i + 1, i) for i in range(streams -...]
    ppermute x2, starting transfers between devices: 6.77 us -> 8.93 us  [exchange(): lax.ppermute(tail_stream, 'stream', [(i, i + 1) for i in range(streams -...]
    ppermute x2, starting transfers between devices: 3.56 us -> 2.18 us  [exchange(): lax.ppermute(tail_azim, 'azim', [(i, (i + 1) % azims) for i in range(azim...]
  transfers between devices with their start and end apart: 9 -> 9, of which waited for: 1 -> 1; matrix products, arithmetic and copies ran while one was open for 1% -> 1% of each run, Pallas kernels for 41% -> 30%
where the time goes in v4:
time: 107 us
  Pallas kernels  65.6 us (61%)
  starting transfers between devices  32.4 us (30%)
  local copies, waits for them, and re-layouts  3.88 us (4%)
  waiting for transfers between devices  3.69 us (3%)
  between operations  1.62 us (2%)
    pallas_call x1, Pallas kernels, second_update(): pl.pallas_call(second_kernel, grid=grid, in_specs=[pl.BlockSpec(memory_sp...  33 us
    pallas_call x1, Pallas kernels, first_flow(): pl.pallas_call(first_flow_kernel, grid=grid, in_specs=[pl.BlockSpec(memor...  17.2 us
    pallas_call x1, Pallas kernels, first_bubbles(): pl.pallas_call(first_bubbles_kernel, grid=(1,), in_specs=[pl.BlockSpec(me...  15.4 us
    ppermute x2, starting transfers between devices, exchange(): lax.ppermute(head_azim, 'azim', [((i + 1) % azims, i) for i in range(azim...  9.6 us
    ppermute x2, starting transfers between devices, exchange(): lax.ppermute(tail_stream, 'stream', [(i, i + 1) for i in range(streams -...  8.93 us
    all_to_all x1, starting transfers between devices, on_device(): lax.all_to_all(packed, ('stream', 'azim'), split_axis=0, concat_axis=0, t...  6.77 us
    ppermute x2, starting transfers between devices, exchange(): lax.ppermute(head_stream, 'stream', [(i + 1, i) for i in range(streams -...  4.96 us
    ppermute x2, waiting for transfers between devices, exchange(): lax.ppermute(head_stream, 'stream', [(i + 1, i) for i in range(streams -...  3.67 us
  transfers between devices with their start and end apart: 9, of which 1 were waited for; matrix products, arithmetic and copies ran while one was open for 1% of the time, Pallas kernels for 30%

profile of v4, /device:TPU:1, one launch (start us, length us, event | category | flops | bytes accessed | tf_op | source)
XLA Modules:
  0.0 107.2 jit_solution(9086684977115904407)
XLA Ops:
  0.6 1.7 %fusion = (f32[4,64,1,128]{3,2,1,0:T(1,128)S(1)}, f32[4,64,1,128]{3,2,1,0:T(1,128)S(1)}) fusion(f32[4,64,32,128]{3,2,1,0:T(8,128)} %flow_after.1), kind=kLoop, calls=%fused_computation.2 | loop fusion | bytes 524288 | tf_op jit(solution)/shard_map/slice | solution.py:502
  2.4 2.1 %collective-permute-start.2 = (f32[4,64,128]{2,1,0:T(8,128)S(1)}, f32[4,64,128]{2,1,0:T(8,128)S(1)}, u32[]{:S(2)}, u32[]{:S(2)}) collective-permute-start(f32[4,64,128]{2,1,0:T(8,128)S(1)} %bitcast.22), channel_id=1, source_target_pairs={{0,1},{1,2},{2,3},{3,4},{4,5},{5,6},{6,7},{7,8},{8,9},{9,10},{10,1... | collective-permute-start | bytes 393224 | tf_op jit(solution)/shard_map/ppermute | solution.py:496
  4.5 4.8 %collective-permute-start.3 = (f32[4,64,128]{2,1,0:T(8,128)S(1)}, f32[4,64,128]{2,1,0:T(8,128)S(1)}, u32[]{:S(2)}, u32[]{:S(2)}) collective-permute-start(f32[4,64,128]{2,1,0:T(8,128)S(1)} %bitcast.21), channel_id=1, source_target_pairs={{1,0},{2,1},{3,2},{4,3},{5,4},{6,5},{7,6},{8,7},{9,8},{10,9},{11,1... | collective-permute-start | bytes 393224 | tf_op jit(solution)/shard_map/ppermute | solution.py:497
  9.3 0.9 slice_bitcast_fusion
  10.2 2.9 %collective-permute-start.1 = (f32[4,32,128]{2,1,0:T(8,128)S(1)}, f32[4,32,128]{2,1,0:T(8,128)S(1)}, u32[]{:S(2)}, u32[]{:S(2)}) collective-permute-start(f32[4,32,128]{2,1,0:T(8,128)S(1)} %get-tuple-element.37), channel_id=1, source_target_pairs={{16,0},{32,16},{48,32},{64,48},{80,64},{96,80},{112,96},{17,1},{33... | collective-permute-start | bytes 196616 | tf_op jit(solution)/shard_map/ppermute | solution.py:495
  13.1 3.1 %collective-permute-start = (f32[4,32,128]{2,1,0:T(8,128)S(1)}, f32[4,32,128]{2,1,0:T(8,128)S(1)}, u32[]{:S(2)}, u32[]{:S(2)}) collective-permute-start(f32[4,32,128]{2,1,0:T(8,128)S(1)} %get-tuple-element.38), channel_id=1, source_target_pairs={{0,16},{16,32},{32,48},{48,64},{64,80},{80,96},{96,112},{1,17},{17... | collective-permute-start | bytes 196616 | tf_op jit(solution)/shard_map/ppermute | solution.py:494
  16.8 15.4 %first_bubbles.1 = (f32[128,24,128]{2,1,0:T(8,128)}, f32[512,128]{1,0:T(8,128)}, f32[512,128]{1,0:T(8,128)}) custom-call(s32[1]{0:T(128)S(6)} %copy.17.counts, s32[512]{0:T(512)} %order.1, s32[512]{0:T(512)} %tiles.4, f32[5,512,128]{2,1,0:T(8,128)} %bitcast.25, f32[4,2048,128]{2,1,0:T(8,128)} %bitcast.23, f32[4,2048,128]{2,1,0:T(8,128)} %bitcast.24), custom_call_target="tpu_custom_call" | custom-call | flops 1000000000 | bytes 100000000 | tf_op jit(solution)/shard_map/first_bubbles/pallas_call | solution.py:418
  32.3 0.0 collective-permute-done.1.stream_after
  32.3 0.0 collective-permute-done.stream_before
  32.3 0.0 copy-start.8
  32.3 0.0 collective-permute-done.2.azim_before
  32.3 0.0 copy-start.5
  32.3 0.0 collective-permute-done.3.azim_after
  32.3 0.0 copy-start.6
  32.3 6.8 %all-to-all-start = ((f32[128,24,128]{2,1,0:T(8,128)}), f32[128,24,128]{2,1,0:T(8,128)S(1)}, u32[]{:S(2)}, u32[]{:S(2)}) async-start(f32[128,24,128]{2,1,0:T(8,128)} %get-tuple-element.20), calls=%async_computation | async-start | bytes 3145728 | tf_op jit(solution)/shard_map/all_to_all | solution.py:508
  39.1 17.2 %first_flow.1 = (f32[4,64,32,128]{3,2,1,0:T(8,128)}, f32[4,32,128]{2,1,0:T(8,128)}, f32[4,32,128]{2,1,0:T(8,128)}, f32[4,64,128]{2,1,0:T(8,128)}, f32[4,64,128]{2,1,0:T(8,128)}) custom-call(s32[1]{0:T(128)S(6)} %copy.17.counts, s32[512]{0:T(512)} %tiles.4, f32[512,128]{1,0:T(8,128)} %get-tuple-element.21.places, f32[512,128]{1,0:T(8,128)} %get-tuple-element.22.source, ...), custom_call_target="tpu_custom_call" | custom-call | flops 1000000000 | bytes 80000000 | tf_op jit(solution)/shard_map/first_flow/pallas_call | solution.py:447
  56.3 0.1 collective-permute-start.6
  56.4 4.8 %collective-permute-start.7 = (f32[4,64,128]{2,1,0:T(8,128)}, f32[4,64,128]{2,1,0:T(8,128)S(1)}, u32[]{:S(2)}, u32[]{:S(2)}) collective-permute-start(f32[4,64,128]{2,1,0:T(8,128)} %get-tuple-element.31), channel_id=1, source_target_pairs={{1,0},{2,1},{3,2},{4,3},{5,4},{6,5},{7,6},{8,7},{9,8},{10,9},{11,1... | collective-permute-start | bytes 393224 | tf_op jit(solution)/shard_map/ppermute | solution.py:497
  61.1 5.8 %collective-permute-start.4 = (f32[4,32,128]{2,1,0:T(8,128)}, f32[4,32,128]{2,1,0:T(8,128)S(1)}, u32[]{:S(2)}, u32[]{:S(2)}) collective-permute-start(f32[4,32,128]{2,1,0:T(8,128)} %get-tuple-element.28), channel_id=1, source_target_pairs={{0,16},{16,32},{32,48},{48,64},{64,80},{80,96},{96,112},{1,17},{17... | collective-permute-start | bytes 196616 | tf_op jit(solution)/shard_map/ppermute | solution.py:494
  67.0 2.1 %collective-permute-start.5 = (f32[4,32,128]{2,1,0:T(8,128)}, f32[4,32,128]{2,1,0:T(8,128)S(1)}, u32[]{:S(2)}, u32[]{:S(2)}) collective-permute-start(f32[4,32,128]{2,1,0:T(8,128)} %get-tuple-element.29), channel_id=1, source_target_pairs={{16,0},{32,16},{48,32},{64,48},{80,64},{96,80},{112,96},{17,1},{33... | collective-permute-start | bytes 196616 | tf_op jit(solution)/shard_map/ppermute | solution.py:495
  69.1 0.0 collective-permute-done.4.stream_before
  69.1 0.0 copy-start.3
  69.1 3.7 %collective-permute-done.5.stream_after = f32[4,32,128]{2,1,0:T(8,128)S(1)} collective-permute-done((f32[4,32,128]{2,1,0:T(8,128)}, f32[4,32,128]{2,1,0:T(8,128)S(1)}, u32[]{:S(2)}, u32[]{:S(2)}) %collective-permute-start.5) | collective-permute-done | bytes 65568 | tf_op jit(solution)/shard_map/ppermute | solution.py:495
  72.8 0.0 collective-permute-done.6.azim_before
  72.8 0.0 collective-permute-done.7.azim_after
  72.8 0.0 copy-start.2
  72.8 0.0 all-to-all-done.packed
  72.8 0.6 copy-done.4
  73.4 0.1 copy-done.1
  73.4 0.0 copy-done.2
  73.5 0.6 copy-done
  74.1 33.0 %second_update.1 = (f32[4,64,32,128]{3,2,1,0:T(8,128)}, f32[5,512,128]{2,1,0:T(8,128)}, f32[2048,128]{1,0:T(8,128)}) custom-call(s32[512]{0:T(512)} %tiles.5, f32[128,24,128]{2,1,0:T(8,128)} %copy-done, f32[4,2048,128]{2,1,0:T(8,128)} %bitcast.19, f32[4,2048,128]{2,1,0:T(8,128)} %bitcast.20, ...), custom_call_target="tpu_custom_call" | custom-call | flops 1000000000 | bytes 100000000 | tf_op jit(solution)/shard_map/second_update/pallas_call | solution.py:468
  (9 shorter events, 0.0 us)
Async XLA Ops:
  2.4 29.9 %collective-permute-start.2 = (f32[4,64,128]{2,1,0:T(8,128)S(1)}, f32[4,64,128]{2,1,0:T(8,128)S(1)}, u32[]{:S(2)}, u32[]{:S(2)}) collective-permute-start(f32[4,64,128]{2,1,0:T(8,128)S(1)} %bitcast.22), channel_id=1, source_target_pairs={{0,1},{1,2},{2,3},{3,4},{4,5},{5,6},{6,7},{7,8},{8,9},{9,10},{10,1... | collective-permute-start | bytes 393224 | tf_op jit(solution)/shard_map/ppermute | solution.py:496
  4.5 27.8 %collective-permute-start.3 = (f32[4,64,128]{2,1,0:T(8,128)S(1)}, f32[4,64,128]{2,1,0:T(8,128)S(1)}, u32[]{:S(2)}, u32[]{:S(2)}) collective-permute-start(f32[4,64,128]{2,1,0:T(8,128)S(1)} %bitcast.21), channel_id=1, source_target_pairs={{1,0},{2,1},{3,2},{4,3},{5,4},{6,5},{7,6},{8,7},{9,8},{10,9},{11,1... | collective-permute-start | bytes 393224 | tf_op jit(solution)/shard_map/ppermute | solution.py:497
  10.2 22.1 %collective-permute-start.1 = (f32[4,32,128]{2,1,0:T(8,128)S(1)}, f32[4,32,128]{2,1,0:T(8,128)S(1)}, u32[]{:S(2)}, u32[]{:S(2)}) collective-permute-start(f32[4,32,128]{2,1,0:T(8,128)S(1)} %get-tuple-element.37), channel_id=1, source_target_pairs={{16,0},{32,16},{48,32},{64,48},{80,64},{96,80},{112,96},{17,1},{33... | collective-permute-start | bytes 196616 | tf_op jit(solution)/shard_map/ppermute | solution.py:495
  13.1 19.2 %collective-permute-start = (f32[4,32,128]{2,1,0:T(8,128)S(1)}, f32[4,32,128]{2,1,0:T(8,128)S(1)}, u32[]{:S(2)}, u32[]{:S(2)}) collective-permute-start(f32[4,32,128]{2,1,0:T(8,128)S(1)} %get-tuple-element.38), channel_id=1, source_target_pairs={{0,16},{16,32},{32,48},{48,64},{64,80},{80,96},{96,112},{1,17},{17... | collective-permute-start | bytes 196616 | tf_op jit(solution)/shard_map/ppermute | solution.py:494
  32.3 6.8 %copy-start.7 = (f32[4,32,128]{2,1,0:T(8,128)}, f32[4,32,128]{2,1,0:T(8,128)S(1)}, u32[]{:S(2)}) copy-start(f32[4,32,128]{2,1,0:T(8,128)S(1)} %collective-permute-done.1.stream_after) | copy-start | bytes 196612
  32.3 6.8 %copy-start.8 = (f32[4,32,128]{2,1,0:T(8,128)}, f32[4,32,128]{2,1,0:T(8,128)S(1)}, u32[]{:S(2)}) copy-start(f32[4,32,128]{2,1,0:T(8,128)S(1)} %collective-permute-done.stream_before) | copy-start | bytes 196612
  32.3 6.8 %copy-start.5 = (f32[4,64,128]{2,1,0:T(8,128)}, f32[4,64,128]{2,1,0:T(8,128)S(1)}, u32[]{:S(2)}) copy-start(f32[4,64,128]{2,1,0:T(8,128)S(1)} %collective-permute-done.2.azim_before) | copy-start | bytes 393220
  32.3 6.8 %copy-start.6 = (f32[4,64,128]{2,1,0:T(8,128)}, f32[4,64,128]{2,1,0:T(8,128)S(1)}, u32[]{:S(2)}) copy-start(f32[4,64,128]{2,1,0:T(8,128)S(1)} %collective-permute-done.3.azim_after) | copy-start | bytes 393220
  32.3 40.5 %all-to-all-start = ((f32[128,24,128]{2,1,0:T(8,128)}), f32[128,24,128]{2,1,0:T(8,128)S(1)}, u32[]{:S(2)}, u32[]{:S(2)}) async-start(f32[128,24,128]{2,1,0:T(8,128)} %get-tuple-element.20), calls=%async_computation | async-start | bytes 3145728 | tf_op jit(solution)/shard_map/all_to_all | solution.py:508
  56.3 16.5 %collective-permute-start.6 = (f32[4,64,128]{2,1,0:T(8,128)}, f32[4,64,128]{2,1,0:T(8,128)S(1)}, u32[]{:S(2)}, u32[]{:S(2)}) collective-permute-start(f32[4,64,128]{2,1,0:T(8,128)} %get-tuple-element.30), channel_id=1, source_target_pairs={{0,1},{1,2},{2,3},{3,4},{4,5},{5,6},{6,7},{7,8},{8,9},{9,10},{10,1... | collective-permute-start | bytes 393224 | tf_op jit(solution)/shard_map/ppermute | solution.py:496
  56.4 16.4 %collective-permute-start.7 = (f32[4,64,128]{2,1,0:T(8,128)}, f32[4,64,128]{2,1,0:T(8,128)S(1)}, u32[]{:S(2)}, u32[]{:S(2)}) collective-permute-start(f32[4,64,128]{2,1,0:T(8,128)} %get-tuple-element.31), channel_id=1, source_target_pairs={{1,0},{2,1},{3,2},{4,3},{5,4},{6,5},{7,6},{8,7},{9,8},{10,9},{11,1... | collective-permute-start | bytes 393224 | tf_op jit(solution)/shard_map/ppermute | solution.py:497
  61.1 7.9 %collective-permute-start.4 = (f32[4,32,128]{2,1,0:T(8,128)}, f32[4,32,128]{2,1,0:T(8,128)S(1)}, u32[]{:S(2)}, u32[]{:S(2)}) collective-permute-start(f32[4,32,128]{2,1,0:T(8,128)} %get-tuple-element.28), channel_id=1, source_target_pairs={{0,16},{16,32},{32,48},{48,64},{64,80},{80,96},{96,112},{1,17},{17... | collective-permute-start | bytes 196616 | tf_op jit(solution)/shard_map/ppermute | solution.py:494
  67.0 5.8 %collective-permute-start.5 = (f32[4,32,128]{2,1,0:T(8,128)}, f32[4,32,128]{2,1,0:T(8,128)S(1)}, u32[]{:S(2)}, u32[]{:S(2)}) collective-permute-start(f32[4,32,128]{2,1,0:T(8,128)} %get-tuple-element.29), channel_id=1, source_target_pairs={{16,0},{32,16},{48,32},{64,48},{80,64},{96,80},{112,96},{17,1},{33... | collective-permute-start | bytes 196616 | tf_op jit(solution)/shard_map/ppermute | solution.py:495
  69.1 3.7 %copy-start.3 = (f32[4,32,128]{2,1,0:T(8,128)}, f32[4,32,128]{2,1,0:T(8,128)S(1)}, u32[]{:S(2)}) copy-start(f32[4,32,128]{2,1,0:T(8,128)S(1)} %collective-permute-done.4.stream_before) | copy-start | bytes 196612
  72.8 0.6 copy-start.4
  72.8 0.7 copy-start.1
  72.8 0.7 copy-start.2
  72.8 1.2 %copy-start = (f32[128,24,128]{2,1,0:T(8,128)}, f32[128,24,128]{2,1,0:T(8,128)S(1)}, u32[]{:S(2)}) copy-start(f32[128,24,128]{2,1,0:T(8,128)S(1)} %all-to-all-done.packed) | copy-start | bytes 4718596

commit v5 on v4

--- a/solution.py
+++ b/solution.py
@@ -29,7 +29,8 @@
 CAP = 4
 PACK = 24
 GROUP = 8
-STREAM_BLOCK = 32
+AZIMS = 32
+SLAB = 8
 VMEM_MIB = 58
 FIRST_BATCH = 64
 SECOND_BATCH = 32
@@ -37,6 +38,7 @@
 SHARP = 0.5 / (KERNEL_WIDTH * KERNEL_WIDTH) * LOG2_E
 VMEM = pltpu.VMEM
 SMEM = pltpu.SMEM
+ANY = pl.BlockSpec(memory_space=pl.ANY)
 
 
 def split(values):
@@ -60,7 +62,7 @@
     scaled_cells[...] = index * SHARP
 
 
-def sample_phase(size, batches, positions, tile_of, flow_p, flow_v, rows_p, rows_v, cells, scaled_cells, sampled_p, sampled_v):
+def sample_phase(size, batches, positions, tile_of, row_of, rows_p, rows_v, cells, scaled_cells, sampled_p, sampled_v):
     sublane = lax.broadcasted_iota(jnp.int32, (GROUP, BB), 0)
     ones = jnp.ones((16, CR), jnp.bfloat16)
 
@@ -96,8 +98,8 @@
     def gather(base):
         for i in range(size):
             tile = tile_of(base + i)
-            rows_p[pl.ds(base + i, 1), :] = flow_p[0, pl.ds(tile, 1), :]
-            rows_v[pl.ds(base + i, 1), :] = flow_v[0, pl.ds(tile, 1), :]
+            rows_p[pl.ds(base + i, 1), :] = row_of(0, tile)
+            rows_v[pl.ds(base + i, 1), :] = row_of(3, tile)
 
     def body(batch, carry):
         for sub in range(size // GROUP):
@@ -204,7 +206,8 @@
     chunks = (live + CHUNK - 1) // CHUNK
     fill_cells(cells, scaled_cells)
     sample_phase(
-        size, batches, lambda here: bubbles[2, here, :], lambda j: tiles[j], flow_p, flow_v, rows_p, rows_v,
+        size, batches, lambda here: bubbles[2, here, :], lambda j: tiles[j],
+        lambda c, tile: (flow_v if c else flow_p)[0, pl.ds(tile, 1), :], rows_p, rows_v,
         cells, scaled_cells, sampled_p, sampled_v,
     )
     bubble_phase(
@@ -228,56 +231,39 @@
 
 
 def first_flow_kernel(
-    counts, tiles, places, source, flow, flow_before, flow_after, stream_before, stream_after, azim_before,
-    azim_after, new, face_0, face_1, face_2, face_3, source_grid, cells, scaled_cells,
+    counts, tiles, places, source, flow_in, stream_before, stream_after, azim_before, azim_after,
+    new_out, face_0, face_1, face_2, face_3, flow, new, in_sems, out_sems, source_grid, cells, scaled_cells,
 ):
-    step = pl.program_id(0)
-
-    @pl.when(step == 0)
-    def _():
-        size = FIRST_BATCH
-        live = counts[0]
-        fill_cells(cells, scaled_cells)
-        source_grid[...] = jnp.zeros_like(source_grid)
-        spread_phase(
-            size, (live + size - 1) // size, live, lambda j: tiles[j], places, [source], cells, scaled_cells,
-            [source_grid], None,
-        )
-
-    @pl.when(step > 0)
-    def _():
-        flow_slab(
-            step - 1, pl.num_programs(0) - 1, flow, flow_before, flow_after, source_grid, stream_before,
-            stream_after, azim_before, azim_after, new, face_0, face_1, face_2, face_3,
-        )
+    copies = flow_copies(flow_in, stream_before, stream_after, flow, in_sems)
+    for copy in copies:
+        copy.start()
+    size = FIRST_BATCH
+    live = counts[0]
+    fill_cells(cells, scaled_cells)
+    source_grid[...] = jnp.zeros_like(source_grid)
+    spread_phase(
+        size, (live + size - 1) // size, live, lambda j: tiles[j], places, [source], cells, scaled_cells,
+        [source_grid], None,
+    )
+    for copy in copies:
+        copy.wait()
+    flow_update(flow, source_grid, azim_before, azim_after, new, new_out, out_sems, face_2, face_3)
+    streams = new.shape[1] // AZIMS
+    face_0[...] = new[:, 0:AZIMS, :]
+    face_1[...] = new[:, (streams - 1) * AZIMS :, :]
+    flow_stored(new, new_out, out_sems)
 
 
 def second_kernel(
-    tiles, packed, flow_p, flow_v, flow, flow_before, flow_after, stream_before, stream_after, azim_before,
-    azim_after, new, bubbles_out, void_grid, slots, flags, flag_sem, source_grid, places, source, void,
-    *scratch,
+    tiles, packed, flow_in, stream_before, stream_after, azim_before, azim_after,
+    new_out, moved_out, void_out,
+    flow, new, in_sems, out_sems, source_grid, void_grid, bubbles_out, moved_sem, void_sem,
+    slots, flags, flag_sem, places, source, void,
+    state, rows_p, rows_v, sampled_p, sampled_v, cells, scaled_cells,
 ):
-    step = pl.program_id(0)
-
-    @pl.when(step == 0)
-    def _():
-        second_bubbles(
-            tiles, packed, flow_p, flow_v, bubbles_out, source_grid, void_grid, slots, flags, flag_sem,
-            places, source, void, *scratch,
-        )
-
-    @pl.when(step > 0)
-    def _():
-        flow_slab(
-            step - 1, pl.num_programs(0) - 1, flow, flow_before, flow_after, source_grid, stream_before,
-            stream_after, azim_before, azim_after, new,
-        )
-
-
-def second_bubbles(
-    tiles, packed, flow_p, flow_v, bubbles_out, source_grid, void_grid, slots, flags, flag_sem,
-    places, source, void, state, rows_p, rows_v, sampled_p, sampled_v, cells, scaled_cells,
-):
+    copies = flow_copies(flow_in, stream_before, stream_after, flow, in_sems)
+    for copy in copies:
+        copy.start()
     size = SECOND_BATCH
     copy = pltpu.make_async_copy(packed.at[:, COMPS * CAP, :], flags, flag_sem)
     copy.start()
@@ -303,9 +289,11 @@
         state[jnp.minimum(live + i, NBLK - 1), 0:COMPS, :] = state[jnp.maximum(live - 1, 0), 0:COMPS, :]
     batches = (live + size - 1) // size
     chunks = (live + CHUNK - 1) // CHUNK
-
+    for copy in copies[:2]:
+        copy.wait()
     sample_phase(
-        size, batches, lambda here: state[here, 2, :], lambda j: tiles[slots[j]], flow_p, flow_v, rows_p, rows_v,
+        size, batches, lambda here: state[here, 2, :], lambda j: tiles[slots[j]],
+        lambda c, tile: flow[c, pl.ds(tile + AZIMS, 1), :], rows_p, rows_v,
         cells, scaled_cells, sampled_p, sampled_v,
     )
     bubble_phase(
@@ -323,34 +311,58 @@
         size, batches, live, lambda j: tiles[slots[j]], places, [source, void], cells, scaled_cells,
         [source_grid, void_grid], put,
     )
-
-
-def flow_slab(
-    index, slabs, flow, flow_before, flow_after, source, stream_before, stream_after, azim_before,
-    azim_after, new, *faces,
-):
-    first, final = index == 0, index == slabs - 1
-    streams = flow.shape[1]
-    azims = flow.shape[2]
-    shape = (azims, CR)
+    moved_copy = pltpu.make_async_copy(bubbles_out, moved_out, moved_sem)
+    void_copy = pltpu.make_async_copy(void_grid, void_out, void_sem)
+    moved_copy.start()
+    void_copy.start()
+    for copy in copies[2:]:
+        copy.wait()
+    flow_update(flow, source_grid, azim_before, azim_after, new, new_out, out_sems)
+    moved_copy.wait()
+    void_copy.wait()
+    flow_stored(new, new_out, out_sems)
+
+
+def flow_copies(flow_in, stream_before, stream_after, flow, sems):
+    tiles = flow_in.shape[1]
+    parts = [(flow_in.at[c], flow.at[c, AZIMS : AZIMS + tiles]) for c in (0, 3, 1, 2)]
+    parts.append((stream_before, flow.at[:, 0:AZIMS]))
+    parts.append((stream_after, flow.at[:, AZIMS + tiles : AZIMS + tiles + AZIMS]))
+    return [pltpu.make_async_copy(src, dst, sems.at[i]) for i, (src, dst) in enumerate(parts)]
+
+
+def slab_copy(slab, new, new_out, sems):
+    here = pl.ds(pl.multiple_of(slab * SLAB * AZIMS, SLAB * AZIMS), SLAB * AZIMS)
+    return pltpu.make_async_copy(new.at[:, here], new_out.at[:, here], sems.at[slab])
+
+
+def flow_stored(new, new_out, sems):
+    for slab in range(new.shape[1] // AZIMS // SLAB):
+        slab_copy(slab, new, new_out, sems).wait()
+
+
+def flow_update(flow, source, azim_before, azim_after, new, new_out, sems, *faces):
+    shape = (AZIMS, CR)
     lane = lax.broadcasted_iota(jnp.int32, shape, 1)
     row = lax.broadcasted_iota(jnp.int32, shape, 0)
     first_lane, last_lane = lane == 0, lane == CR - 1
-    first_row, last_row = row == 0, row == azims - 1
+    first_row, last_row = row == 0, row == AZIMS - 1
     a = 0.5 * TIME_STEP
 
-    def plane(s, down, up):
+    def plane(s):
+        start = pl.multiple_of(s * AZIMS, AZIMS)
+        here = pl.ds(start, AZIMS)
         sums = []
         values = []
         stream_slope = []
         azim_slope = {}
         radial_slope = {}
         for c in range(4):
-            f = flow[c, s]
-            before = down(c)
-            after = up(c)
+            before = flow[c, here, :]
+            f = flow[c, pl.ds(start + AZIMS, AZIMS), :]
+            after = flow[c, pl.ds(start + 2 * AZIMS, AZIMS), :]
             left = jnp.where(first_row, azim_before[c, pl.ds(s, 1), :], pltpu.roll(f, 1, 0))
-            right = jnp.where(last_row, azim_after[c, pl.ds(s, 1), :], pltpu.roll(f, azims - 1, 0))
+            right = jnp.where(last_row, azim_after[c, pl.ds(s, 1), :], pltpu.roll(f, AZIMS - 1, 0))
             inner = jnp.where(first_lane, 0.0, pltpu.roll(f, 1, 1))
             outer = jnp.where(last_lane, 0.0, pltpu.roll(f, CR - 1, 1))
             values.append(f)
@@ -369,27 +381,19 @@
         for c in range(4):
             value = (1.0 - 6.0 * DIFFUSION) * values[c] + DIFFUSION * sums[c] - a * rates[c]
             if c == 0:
-                value = value - TIME_STEP * source[pl.ds(pl.multiple_of((index * streams + s) * azims, azims), azims), :]
-            new[c, s] = value
+                value = value - TIME_STEP * source[here, :]
+            new[c, here, :] = value
             if faces:
-                faces[2][c, pl.ds(s, 1), :] = value[0:1]
-                faces[3][c, pl.ds(s, 1), :] = value[azims - 1 : azims]
-
-    for s in range(streams):
-        plane(
-            s,
-            (lambda c: jnp.where(first, stream_before[c], flow_before[c, 0])) if s == 0 else (lambda c: flow[c, s - 1]),
-            (lambda c: jnp.where(final, stream_after[c], flow_after[c, 0])) if s == streams - 1 else (lambda c: flow[c, s + 1]),
-        )
-    if faces:
-
-        @pl.when(first)
-        def _():
-            faces[0][...] = new[:, 0]
-
-        @pl.when(final)
-        def _():
-            faces[1][...] = new[:, streams - 1]
+                faces[0][c, pl.ds(s, 1), :] = value[0:1]
+                faces[1][c, pl.ds(s, 1), :] = value[AZIMS - 1 : AZIMS]
+
+    def body(slab, carry):
+        for i in range(SLAB):
+            plane(slab * SLAB + i)
+        slab_copy(slab, new, new_out, sems).start()
+        return carry
+
+    lax.fori_loop(0, new.shape[1] // AZIMS // SLAB, body, 0)
 
 
 F32 = jnp.float32
@@ -429,62 +433,63 @@
     )(counts, order, tiles, bubbles, flow_rows, flow_rows)
 
 
-def slab_specs(streams, azims):
-    slab = STREAM_BLOCK
-    moving = pl.BlockSpec((4, slab, azims, CR), lambda i: (0, jnp.maximum(i - 1, 0), 0, 0))
-    before = pl.BlockSpec((4, 1, azims, CR), lambda i: (0, jnp.maximum((i - 1) * slab - 1, 0), 0, 0))
-    after = pl.BlockSpec(
-        (4, 1, azims, CR), lambda i: (0, jnp.minimum(jnp.maximum(i, 1) * slab, streams - 1), 0, 0)
-    )
-    along = pl.BlockSpec((4, slab, CR), lambda i: (0, jnp.maximum(i - 1, 0), 0))
-    fixed = whole((4, azims, CR))
-    return (1 + streams // slab,), [moving, before, after, fixed, fixed, along, along], moving, along, fixed
+def flow_scratch(streams):
+    return [
+        VMEM((4, (streams + 2) * AZIMS, CR), F32),
+        VMEM((4, streams * AZIMS, CR), F32),
+        pltpu.SemaphoreType.DMA((6,)),
+        pltpu.SemaphoreType.DMA((streams // SLAB,)),
+        VMEM((streams * AZIMS, CR), F32),
+    ]
+
+
+def flow_specs(streams):
+    return [ANY] * 3 + [whole((4, streams, CR))] * 2
 
 
 def first_flow(counts, tiles, places, source, flow, halos):
-    streams, azims = flow.shape[1:3]
-    grid, slabs, moving, along, fixed = slab_specs(streams, azims)
+    streams = flow.shape[1] // AZIMS
     return pl.pallas_call(
         first_flow_kernel,
-        grid=grid,
-        in_specs=[pl.BlockSpec(memory_space=SMEM)] * 2 + [whole((NBLK, BB))] * 2 + slabs,
-        out_specs=[moving, fixed, fixed, along, along],
+        grid=(1,),
+        in_specs=[pl.BlockSpec(memory_space=SMEM)] * 2 + [whole((NBLK, BB))] * 2 + flow_specs(streams),
+        out_specs=[ANY] + [whole((4, AZIMS, CR))] * 2 + [whole((4, streams, CR))] * 2,
         out_shape=[SHAPE(flow.shape, F32)]
-        + [SHAPE((4, azims, CR), F32)] * 2
+        + [SHAPE((4, AZIMS, CR), F32)] * 2
         + [SHAPE((4, streams, CR), F32)] * 2,
-        scratch_shapes=[VMEM((streams * azims, CR), F32)] + [VMEM((CR, BB), F32)] * 2,
+        scratch_shapes=flow_scratch(streams) + [VMEM((CR, BB), F32)] * 2,
         compiler_params=params(),
         cost_estimate=pl.CostEstimate(flops=10**9, bytes_accessed=8 * 10**7, transcendentals=10**7),
         name="first_flow",
-    )(counts, tiles, places, source, flow, flow, flow, *halos)
+    )(counts, tiles, places, source, flow, *halos)
 
 
 def second_update(tiles, packed, flow, halos):
-    streams, azims = flow.shape[1:3]
-    grid, slabs, moving, along, fixed = slab_specs(streams, azims)
-    ntile = streams * azims
+    ntile = flow.shape[1]
+    streams = ntile // AZIMS
     peers = NBLK // CAP
-    rows = flow.reshape(4, ntile, CR)
     return pl.pallas_call(
         second_kernel,
-        grid=grid,
-        in_specs=[pl.BlockSpec(memory_space=SMEM)]
-        + [whole((peers, PACK, BB)), component(0, ntile), component(3, ntile)]
-        + slabs,
-        out_specs=[moving, whole((COMPS, NBLK, BB)), whole((ntile, CR))],
+        grid=(1,),
+        in_specs=[pl.BlockSpec(memory_space=SMEM), whole((peers, PACK, BB))] + flow_specs(streams),
+        out_specs=[ANY] * 3,
         out_shape=[SHAPE(flow.shape, F32), SHAPE((COMPS, NBLK, BB), F32), SHAPE((ntile, CR), F32)],
-        scratch_shapes=[
+        scratch_shapes=flow_scratch(streams)
+        + [
+            VMEM((ntile, CR), F32),
+            VMEM((COMPS, NBLK, BB), F32),
+            pltpu.SemaphoreType.DMA,
+            pltpu.SemaphoreType.DMA,
             SMEM((NBLK + SECOND_BATCH,), jnp.int32),
             SMEM((peers, BB), F32),
             pltpu.SemaphoreType.DMA,
-            VMEM((ntile, CR), F32),
         ]
         + [VMEM((NBLK, BB), F32)] * 3
         + bubble_scratch(),
         compiler_params=params(),
         cost_estimate=pl.CostEstimate(flops=10**9, bytes_accessed=10**8, transcendentals=10**7),
         name="second_update",
-    )(tiles, packed, rows, rows, flow, flow, flow, *halos)
+    )(tiles, packed, flow, *halos)
 
 
 def exchange(head_stream, tail_stream, head_azim, tail_azim):
@@ -506,9 +511,9 @@
     )
     packed, halos = lax.optimization_barrier((packed, halos))
     arrived = lax.all_to_all(packed, ("stream", "azim"), split_axis=0, concat_axis=0, tiled=True)
-    flow, *faces = first_flow(counts, tiles_first_update, places, source, fluid, halos)
+    flow, *faces = first_flow(counts, tiles_first_update, places, source, rows, halos)
     flow, moved, void = second_update(tiles_after, arrived, flow, exchange(*faces))
-    return flow, moved.transpose(1, 0, 2), void.reshape(fluid.shape[1:])
+    return flow.reshape(fluid.shape), moved.transpose(1, 0, 2), void.reshape(fluid.shape[1:])
 
 
 def solution(mesh):

time: 107 us -> 101 us (0.944)
  starting transfers between devices: 32.4 us -> 27.4 us
    ppermute x2, starting transfers between devices: 8.93 us -> 5.01 us  [exchange(): lax.ppermute(tail_stream, 'stream', [(i, i + 1) for i in range(streams -...]
    pallas_call x2, Pallas kernels: 50.2 us -> 48.2 us  [the longest x1 30.4 us: second_update(): pl.pallas_call(second_kernel, grid=(1,), in_specs=[pl.BlockSpec(memory_sp...]
    all_to_all x1, starting transfers between devices: 6.77 us -> 4.87 us  [on_device(): lax.all_to_all(packed, ('stream', 'azim'), split_axis=0, concat_axis=0, t...]
    pallas_call x1, Pallas kernels: 15.4 us -> 17 us  [first_bubbles(): pl.pallas_call(first_bubbles_kernel, grid=(1,), in_specs=[pl.BlockSpec(me...]
  transfers between devices with their start and end apart: 9 -> 9, of which waited for: 1 -> 1; matrix products, arithmetic and copies ran while one was open for 1% -> 1% of each run, Pallas kernels for 30% -> 35%
where the time goes in v5:
time: 101 us
  Pallas kernels  65.2 us (65%)
  starting transfers between devices  27.4 us (27%)
  local copies, waits for them, and re-layouts  3.88 us (4%)
  waiting for transfers between devices  2.87 us (3%)
  between operations  1.47 us (1%)
    pallas_call x1, Pallas kernels, second_update(): pl.pallas_call(second_kernel, grid=(1,), in_specs=[pl.BlockSpec(memory_sp...  30.4 us
    pallas_call x1, Pallas kernels, first_flow(): pl.pallas_call(first_flow_kernel, grid=(1,), in_specs=[pl.BlockSpec(memor...  17.8 us
    pallas_call x1, Pallas kernels, first_bubbles(): pl.pallas_call(first_bubbles_kernel, grid=(1,), in_specs=[pl.BlockSpec(me...  17 us
    ppermute x2, starting transfers between devices, exchange(): lax.ppermute(head_azim, 'azim', [((i + 1) % azims, i) for i in range(azim...  9.6 us
    ppermute x2, starting transfers between devices, exchange(): lax.ppermute(head_stream, 'stream', [(i + 1, i) for i in range(streams -...  5.78 us
    ppermute x2, starting transfers between devices, exchange(): lax.ppermute(tail_stream, 'stream', [(i, i + 1) for i in range(streams -...  5.01 us
    all_to_all x1, starting transfers between devices, on_device(): lax.all_to_all(packed, ('stream', 'azim'), split_axis=0, concat_axis=0, t...  4.87 us
    ppermute x2, waiting for transfers between devices, exchange(): lax.ppermute(head_stream, 'stream', [(i + 1, i) for i in range(streams -...  2.86 us
  transfers between devices with their start and end apart: 9, of which 1 were waited for; matrix products, arithmetic and copies ran while one was open for 1% of the time, Pallas kernels for 35%

profile of v5, /device:TPU:1, one launch (start us, length us, event | category | flops | bytes accessed | tf_op | source)
XLA Modules:
  0.0 100.9 jit_solution(4486478354567504211)
XLA Ops:
  0.6 1.7 %fusion = (f32[4,64,1,128]{3,2,1,0:T(1,128)S(1)}, f32[4,64,1,128]{3,2,1,0:T(1,128)S(1)}) fusion(f32[4,64,32,128]{3,2,1,0:T(8,128)} %param.6), kind=kLoop, calls=%fused_computation.2 | loop fusion | bytes 524288 | tf_op jit(solution)/shard_map/slice | solution.py:507
  2.4 2.1 %collective-permute-start.2 = (f32[4,64,128]{2,1,0:T(8,128)S(1)}, f32[4,64,128]{2,1,0:T(8,128)S(1)}, u32[]{:S(2)}, u32[]{:S(2)}) collective-permute-start(f32[4,64,128]{2,1,0:T(8,128)S(1)} %bitcast.20), channel_id=1, source_target_pairs={{0,1},{1,2},{2,3},{3,4},{4,5},{5,6},{6,7},{7,8},{8,9},{9,10},{10,1... | collective-permute-start | bytes 393224 | tf_op jit(solution)/shard_map/ppermute | solution.py:501
  4.5 4.8 %collective-permute-start.3 = (f32[4,64,128]{2,1,0:T(8,128)S(1)}, f32[4,64,128]{2,1,0:T(8,128)S(1)}, u32[]{:S(2)}, u32[]{:S(2)}) collective-permute-start(f32[4,64,128]{2,1,0:T(8,128)S(1)} %bitcast.19), channel_id=1, source_target_pairs={{1,0},{2,1},{3,2},{4,3},{5,4},{6,5},{7,6},{8,7},{9,8},{10,9},{11,1... | collective-permute-start | bytes 393224 | tf_op jit(solution)/shard_map/ppermute | solution.py:502
  9.3 0.9 slice_bitcast_fusion
  10.2 2.9 %collective-permute-start.1 = (f32[4,32,128]{2,1,0:T(8,128)S(1)}, f32[4,32,128]{2,1,0:T(8,128)S(1)}, u32[]{:S(2)}, u32[]{:S(2)}) collective-permute-start(f32[4,32,128]{2,1,0:T(8,128)S(1)} %get-tuple-element.37), channel_id=1, source_target_pairs={{16,0},{32,16},{48,32},{64,48},{80,64},{96,80},{112,96},{17,1},{33... | collective-permute-start | bytes 196616 | tf_op jit(solution)/shard_map/ppermute | solution.py:500
  13.1 3.1 %collective-permute-start = (f32[4,32,128]{2,1,0:T(8,128)S(1)}, f32[4,32,128]{2,1,0:T(8,128)S(1)}, u32[]{:S(2)}, u32[]{:S(2)}) collective-permute-start(f32[4,32,128]{2,1,0:T(8,128)S(1)} %get-tuple-element.38), channel_id=1, source_target_pairs={{0,16},{16,32},{32,48},{48,64},{64,80},{80,96},{96,112},{1,17},{17... | collective-permute-start | bytes 196616 | tf_op jit(solution)/shard_map/ppermute | solution.py:499
  16.8 17.0 %first_bubbles.1 = (f32[128,24,128]{2,1,0:T(8,128)}, f32[512,128]{1,0:T(8,128)}, f32[512,128]{1,0:T(8,128)}) custom-call(s32[1]{0:T(128)S(6)} %copy.17.counts, s32[512]{0:T(512)} %order.1, s32[512]{0:T(512)} %tiles.4, f32[5,512,128]{2,1,0:T(8,128)} %bitcast.24, f32[4,2048,128]{2,1,0:T(8,128)} %bitcast.21, f32[4,2048,128]{2,1,0:T(8,128)} %bitcast.22), custom_call_target="tpu_custom_call" | custom-call | flops 1000000000 | bytes 100000000 | tf_op jit(solution)/shard_map/first_bubbles/pallas_call | solution.py:422
  33.8 0.0 collective-permute-done.1.stream_after
  33.8 0.0 collective-permute-done.stream_before
  33.9 0.0 collective-permute-done.2.azim_before
  33.9 0.0 copy-start.1
  33.9 0.0 collective-permute-done.3.azim_after
  33.9 4.9 %all-to-all-start = ((f32[128,24,128]{2,1,0:T(8,128)}), f32[128,24,128]{2,1,0:T(8,128)S(1)}, u32[]{:S(2)}, u32[]{:S(2)}) async-start(f32[128,24,128]{2,1,0:T(8,128)} %get-tuple-element.20), calls=%async_computation | async-start | bytes 3145728 | tf_op jit(solution)/shard_map/all_to_all | solution.py:513
  38.8 0.0 copy-done.5
  38.8 0.0 copy-done.6
  38.8 0.0 copy-done.1
  38.8 0.0 copy-done.2
  38.8 17.8 %first_flow.1 = (f32[4,2048,128]{2,1,0:T(8,128)}, f32[4,32,128]{2,1,0:T(8,128)}, f32[4,32,128]{2,1,0:T(8,128)}, f32[4,64,128]{2,1,0:T(8,128)}, f32[4,64,128]{2,1,0:T(8,128)}) custom-call(s32[1]{0:T(128)S(6)} %copy.17.counts, s32[512]{0:T(512)} %tiles.4, f32[512,128]{1,0:T(8,128)} %get-tuple-element.21.places, f32[512,128]{1,0:T(8,128)} %get-tuple-element.22.source, ...), custom_call_target="tpu_custom_call" | custom-call | flops 1000000000 | bytes 80000000 | tf_op jit(solution)/shard_map/first_flow/pallas_call | solution.py:452
  56.6 0.1 collective-permute-start.6
  56.7 4.8 %collective-permute-start.7 = (f32[4,64,128]{2,1,0:T(8,128)}, f32[4,64,128]{2,1,0:T(8,128)S(1)}, u32[]{:S(2)}, u32[]{:S(2)}) collective-permute-start(f32[4,64,128]{2,1,0:T(8,128)} %get-tuple-element.31), channel_id=1, source_target_pairs={{1,0},{2,1},{3,2},{4,3},{5,4},{6,5},{7,6},{8,7},{9,8},{10,9},{11,1... | collective-permute-start | bytes 393224 | tf_op jit(solution)/shard_map/ppermute | solution.py:502
  61.5 1.9 %collective-permute-start.4 = (f32[4,32,128]{2,1,0:T(8,128)}, f32[4,32,128]{2,1,0:T(8,128)S(1)}, u32[]{:S(2)}, u32[]{:S(2)}) collective-permute-start(f32[4,32,128]{2,1,0:T(8,128)} %get-tuple-element.28), channel_id=1, source_target_pairs={{0,16},{16,32},{32,48},{48,64},{64,80},{80,96},{96,112},{1,17},{17... | collective-permute-start | bytes 196616 | tf_op jit(solution)/shard_map/ppermute | solution.py:499
  63.4 2.9 %collective-permute-start.5 = (f32[4,32,128]{2,1,0:T(8,128)}, f32[4,32,128]{2,1,0:T(8,128)S(1)}, u32[]{:S(2)}, u32[]{:S(2)}) collective-permute-start(f32[4,32,128]{2,1,0:T(8,128)} %get-tuple-element.29), channel_id=1, source_target_pairs={{16,0},{32,16},{48,32},{64,48},{80,64},{96,80},{112,96},{17,1},{33... | collective-permute-start | bytes 196616 | tf_op jit(solution)/shard_map/ppermute | solution.py:500
  66.3 0.0 collective-permute-done.4.stream_before
  66.4 2.9 %collective-permute-done.5.stream_after = f32[4,32,128]{2,1,0:T(8,128)S(1)} collective-permute-done((f32[4,32,128]{2,1,0:T(8,128)}, f32[4,32,128]{2,1,0:T(8,128)S(1)}, u32[]{:S(2)}, u32[]{:S(2)}) %collective-permute-start.5) | collective-permute-done | bytes 65568 | tf_op jit(solution)/shard_map/ppermute | solution.py:500
  69.2 0.0 collective-permute-done.6.azim_before
  69.2 0.0 collective-permute-done.7.azim_after
  69.2 0.0 all-to-all-done.packed
  69.3 0.6 copy-done.8
  69.8 0.1 copy-done.3
  69.9 0.0 copy-done.4
  69.9 0.6 copy-done
  70.5 30.4 %second_update.1 = (f32[4,2048,128]{2,1,0:T(8,128)}, f32[5,512,128]{2,1,0:T(8,128)}, f32[2048,128]{1,0:T(8,128)}) custom-call(s32[512]{0:T(512)} %tiles.5, f32[128,24,128]{2,1,0:T(8,128)} %copy-done, f32[4,2048,128]{2,1,0:T(8,128)} %get-tuple-element.27.flow_in, f32[4,32,128]{2,1,0:T(8,128)} %copy-done.7, f32[4,32,128]{2,1,0:T(8,128)} %copy-done.8, ...), custom_call_target="tpu_custom_call" | custom-call | flops 1000000000 | bytes 100000000 | tf_op jit(solution)/shard_map/second_update/pallas_call | solution.py:471
  (9 shorter events, 0.0 us)
Async XLA Ops:
  2.4 31.5 %collective-permute-start.2 = (f32[4,64,128]{2,1,0:T(8,128)S(1)}, f32[4,64,128]{2,1,0:T(8,128)S(1)}, u32[]{:S(2)}, u32[]{:S(2)}) collective-permute-start(f32[4,64,128]{2,1,0:T(8,128)S(1)} %bitcast.20), channel_id=1, source_target_pairs={{0,1},{1,2},{2,3},{3,4},{4,5},{5,6},{6,7},{7,8},{8,9},{9,10},{10,1... | collective-permute-start | bytes 393224 | tf_op jit(solution)/shard_map/ppermute | solution.py:501
  4.5 29.4 %collective-permute-start.3 = (f32[4,64,128]{2,1,0:T(8,128)S(1)}, f32[4,64,128]{2,1,0:T(8,128)S(1)}, u32[]{:S(2)}, u32[]{:S(2)}) collective-permute-start(f32[4,64,128]{2,1,0:T(8,128)S(1)} %bitcast.19), channel_id=1, source_target_pairs={{1,0},{2,1},{3,2},{4,3},{5,4},{6,5},{7,6},{8,7},{9,8},{10,9},{11,1... | collective-permute-start | bytes 393224 | tf_op jit(solution)/shard_map/ppermute | solution.py:502
  10.2 23.6 %collective-permute-start.1 = (f32[4,32,128]{2,1,0:T(8,128)S(1)}, f32[4,32,128]{2,1,0:T(8,128)S(1)}, u32[]{:S(2)}, u32[]{:S(2)}) collective-permute-start(f32[4,32,128]{2,1,0:T(8,128)S(1)} %get-tuple-element.37), channel_id=1, source_target_pairs={{16,0},{32,16},{48,32},{64,48},{80,64},{96,80},{112,96},{17,1},{33... | collective-permute-start | bytes 196616 | tf_op jit(solution)/shard_map/ppermute | solution.py:500
  13.1 20.8 %collective-permute-start = (f32[4,32,128]{2,1,0:T(8,128)S(1)}, f32[4,32,128]{2,1,0:T(8,128)S(1)}, u32[]{:S(2)}, u32[]{:S(2)}) collective-permute-start(f32[4,32,128]{2,1,0:T(8,128)S(1)} %get-tuple-element.38), channel_id=1, source_target_pairs={{0,16},{16,32},{32,48},{48,64},{64,80},{80,96},{96,112},{1,17},{17... | collective-permute-start | bytes 196616 | tf_op jit(solution)/shard_map/ppermute | solution.py:499
  33.8 4.9 %copy-start.5 = (f32[4,32,128]{2,1,0:T(8,128)}, f32[4,32,128]{2,1,0:T(8,128)S(1)}, u32[]{:S(2)}) copy-start(f32[4,32,128]{2,1,0:T(8,128)S(1)} %collective-permute-done.1.stream_after) | copy-start | bytes 196612
  33.8 4.9 %copy-start.6 = (f32[4,32,128]{2,1,0:T(8,128)}, f32[4,32,128]{2,1,0:T(8,128)S(1)}, u32[]{:S(2)}) copy-start(f32[4,32,128]{2,1,0:T(8,128)S(1)} %collective-permute-done.stream_before) | copy-start | bytes 196612
  33.9 4.9 %copy-start.1 = (f32[4,64,128]{2,1,0:T(8,128)}, f32[4,64,128]{2,1,0:T(8,128)S(1)}, u32[]{:S(2)}) copy-start(f32[4,64,128]{2,1,0:T(8,128)S(1)} %collective-permute-done.2.azim_before) | copy-start | bytes 393220
  33.9 4.9 %copy-start.2 = (f32[4,64,128]{2,1,0:T(8,128)}, f32[4,64,128]{2,1,0:T(8,128)S(1)}, u32[]{:S(2)}) copy-start(f32[4,64,128]{2,1,0:T(8,128)S(1)} %collective-permute-done.3.azim_after) | copy-start | bytes 393220
  33.9 35.3 %all-to-all-start = ((f32[128,24,128]{2,1,0:T(8,128)}), f32[128,24,128]{2,1,0:T(8,128)S(1)}, u32[]{:S(2)}, u32[]{:S(2)}) async-start(f32[128,24,128]{2,1,0:T(8,128)} %get-tuple-element.20), calls=%async_computation | async-start | bytes 3145728 | tf_op jit(solution)/shard_map/all_to_all | solution.py:513
  56.6 12.6 %collective-permute-start.6 = (f32[4,64,128]{2,1,0:T(8,128)}, f32[4,64,128]{2,1,0:T(8,128)S(1)}, u32[]{:S(2)}, u32[]{:S(2)}) collective-permute-start(f32[4,64,128]{2,1,0:T(8,128)} %get-tuple-element.30), channel_id=1, source_target_pairs={{0,1},{1,2},{2,3},{3,4},{4,5},{5,6},{6,7},{7,8},{8,9},{9,10},{10,1... | collective-permute-start | bytes 393224 | tf_op jit(solution)/shard_map/ppermute | solution.py:501
  56.7 12.5 %collective-permute-start.7 = (f32[4,64,128]{2,1,0:T(8,128)}, f32[4,64,128]{2,1,0:T(8,128)S(1)}, u32[]{:S(2)}, u32[]{:S(2)}) collective-permute-start(f32[4,64,128]{2,1,0:T(8,128)} %get-tuple-element.31), channel_id=1, source_target_pairs={{1,0},{2,1},{3,2},{4,3},{5,4},{6,5},{7,6},{8,7},{9,8},{10,9},{11,1... | collective-permute-start | bytes 393224 | tf_op jit(solution)/shard_map/ppermute | solution.py:502
  61.5 4.8 %collective-permute-start.4 = (f32[4,32,128]{2,1,0:T(8,128)}, f32[4,32,128]{2,1,0:T(8,128)S(1)}, u32[]{:S(2)}, u32[]{:S(2)}) collective-permute-start(f32[4,32,128]{2,1,0:T(8,128)} %get-tuple-element.28), channel_id=1, source_target_pairs={{0,16},{16,32},{32,48},{48,64},{64,80},{80,96},{96,112},{1,17},{17... | collective-permute-start | bytes 196616 | tf_op jit(solution)/shard_map/ppermute | solution.py:499
  63.4 5.8 %collective-permute-start.5 = (f32[4,32,128]{2,1,0:T(8,128)}, f32[4,32,128]{2,1,0:T(8,128)S(1)}, u32[]{:S(2)}, u32[]{:S(2)}) collective-permute-start(f32[4,32,128]{2,1,0:T(8,128)} %get-tuple-element.29), channel_id=1, source_target_pairs={{16,0},{32,16},{48,32},{64,48},{80,64},{96,80},{112,96},{17,1},{33... | collective-permute-start | bytes 196616 | tf_op jit(solution)/shard_map/ppermute | solution.py:500
  66.3 2.9 %copy-start.7 = (f32[4,32,128]{2,1,0:T(8,128)}, f32[4,32,128]{2,1,0:T(8,128)S(1)}, u32[]{:S(2)}) copy-start(f32[4,32,128]{2,1,0:T(8,128)S(1)} %collective-permute-done.4.stream_before) | copy-start | bytes 196612
  69.2 0.6 copy-start.8
  69.2 0.7 copy-start.3
  69.2 0.7 copy-start.4
  69.2 1.2 %copy-start = (f32[128,24,128]{2,1,0:T(8,128)}, f32[128,24,128]{2,1,0:T(8,128)S(1)}, u32[]{:S(2)}) copy-start(f32[128,24,128]{2,1,0:T(8,128)S(1)} %all-to-all-done.packed) | copy-start | bytes 4718596

commit v6 on v5

--- a/solution.py
+++ b/solution.py
@@ -31,7 +31,8 @@
 GROUP = 8
 AZIMS = 32
 SLAB = 8
-VMEM_MIB = 58
+VMEM_MIB = 52
+WIDE_MIB = 58
 FIRST_BATCH = 64
 SECOND_BATCH = 32
 CHUNK = 64
@@ -39,6 +40,7 @@
 VMEM = pltpu.VMEM
 SMEM = pltpu.SMEM
 ANY = pl.BlockSpec(memory_space=pl.ANY)
+DIRECT = pl.BlockSpec(memory_space=pltpu.VMEM)
 
 
 def split(values):
@@ -408,8 +410,8 @@
     return pl.BlockSpec((1, tiles, CR), lambda *_: (c, 0, 0), memory_space=VMEM)
 
 
-def params():
-    return pltpu.CompilerParams(vmem_limit_bytes=VMEM_MIB << 20)
+def params(mib=VMEM_MIB):
+    return pltpu.CompilerParams(vmem_limit_bytes=mib << 20)
 
 
 def bubble_scratch():
@@ -427,10 +429,39 @@
         out_specs=[whole((peers, PACK, BB))] + [whole((NBLK, BB))] * 2,
         out_shape=[SHAPE((peers, PACK, BB), F32)] + [SHAPE((NBLK, BB), F32)] * 2,
         scratch_shapes=bubble_scratch(),
-        compiler_params=params(),
+        compiler_params=params(WIDE_MIB),
         cost_estimate=pl.CostEstimate(flops=10**9, bytes_accessed=10**8, transcendentals=10**7),
         name="first_bubbles",
     )(counts, order, tiles, bubbles, flow_rows, flow_rows)
+
+
+def faces_kernel(flow, face_0, face_1, face_2, face_3, sems):
+    streams, azims = flow.shape[1:3]
+    parts = [
+        (flow.at[:, :, 0], face_2),
+        (flow.at[:, :, azims - 1], face_3),
+        (flow.at[:, 0], face_0),
+        (flow.at[:, streams - 1], face_1),
+    ]
+    copies = [pltpu.make_async_copy(src, dst, sems.at[i]) for i, (src, dst) in enumerate(parts)]
+    for copy in copies:
+        copy.start()
+    for copy in copies:
+        copy.wait()
+
+
+def faces_of(flow):
+    streams, azims = flow.shape[1:3]
+    return pl.pallas_call(
+        faces_kernel,
+        in_specs=[ANY],
+        out_specs=[DIRECT] * 4,
+        out_shape=[SHAPE((4, azims, CR), F32)] * 2 + [SHAPE((4, streams, CR), F32)] * 2,
+        scratch_shapes=[pltpu.SemaphoreType.DMA((4,))],
+        compiler_params=params(WIDE_MIB),
+        cost_estimate=pl.CostEstimate(flops=1000, bytes_accessed=10**6, transcendentals=0),
+        name="faces",
+    )(flow)
 
 
 def flow_scratch(streams):
@@ -443,17 +474,16 @@
     ]
 
 
-def flow_specs(streams):
-    return [ANY] * 3 + [whole((4, streams, CR))] * 2
+def flow_specs():
+    return [ANY, DIRECT, DIRECT, DIRECT, DIRECT]
 
 
 def first_flow(counts, tiles, places, source, flow, halos):
     streams = flow.shape[1] // AZIMS
     return pl.pallas_call(
         first_flow_kernel,
-        grid=(1,),
-        in_specs=[pl.BlockSpec(memory_space=SMEM)] * 2 + [whole((NBLK, BB))] * 2 + flow_specs(streams),
-        out_specs=[ANY] + [whole((4, AZIMS, CR))] * 2 + [whole((4, streams, CR))] * 2,
+        in_specs=[pl.BlockSpec(memory_space=SMEM)] * 2 + [DIRECT] * 2 + flow_specs(),
+        out_specs=[ANY] + [DIRECT] * 4,
         out_shape=[SHAPE(flow.shape, F32)]
         + [SHAPE((4, AZIMS, CR), F32)] * 2
         + [SHAPE((4, streams, CR), F32)] * 2,
@@ -470,8 +500,7 @@
     peers = NBLK // CAP
     return pl.pallas_call(
         second_kernel,
-        grid=(1,),
-        in_specs=[pl.BlockSpec(memory_space=SMEM), whole((peers, PACK, BB))] + flow_specs(streams),
+        in_specs=[pl.BlockSpec(memory_space=SMEM), DIRECT] + flow_specs(),
         out_specs=[ANY] * 3,
         out_shape=[SHAPE(flow.shape, F32), SHAPE((COMPS, NBLK, BB), F32), SHAPE((ntile, CR), F32)],
         scratch_shapes=flow_scratch(streams)
@@ -504,7 +533,7 @@
 
 
 def on_device(fluid, bubbles, counts, outgoing_block_order, tiles_first_update, tiles_after):
-    halos = exchange(fluid[:, 0], fluid[:, -1], fluid[:, :, 0], fluid[:, :, -1])
+    halos = exchange(*faces_of(fluid))
     rows = fluid.reshape(4, -1, CR)
     packed, places, source = first_bubbles(
         counts, outgoing_block_order, tiles_first_update, bubbles.transpose(1, 0, 2), rows

time: 101 us -> 97.5 us (0.965)
  the two profiles are of different devices: /device:TPU:1 before, /device:TPU:17 now
where the time goes in v6:
time: 97.5 us; the launch traced here: 96.7 us
  Pallas kernels  55.8 us (57%)
  starting transfers between devices  33.9 us (35%)
  waiting for transfers between devices  5.54 us (6%)
  between operations  1.43 us (1%)
    pallas_call x1, Pallas kernels, second_update(): pl.pallas_call(second_kernel, in_specs=[pl.BlockSpec(memory_space=SMEM),...  29.5 us
    pallas_call x1, Pallas kernels, first_bubbles(): pl.pallas_call(first_bubbles_kernel, grid=(1,), in_specs=[pl.BlockSpec(me...  12.3 us
    pallas_call x1, Pallas kernels, first_flow(): pl.pallas_call(first_flow_kernel, in_specs=[pl.BlockSpec(memory_space=SME...  12.2 us
    all_to_all x1, starting transfers between devices, on_device(): lax.all_to_all(packed, ('stream', 'azim'), split_axis=0, concat_axis=0, t...  10.8 us
    ppermute x2, starting transfers between devices, exchange(): lax.ppermute(tail_azim, 'azim', [(i, (i + 1) % azims) for i in range(azim...  6.87 us
    ppermute x2, starting transfers between devices, exchange(): lax.ppermute(head_azim, 'azim', [((i + 1) % azims, i) for i in range(azim...  6.16 us
    ppermute x2, starting transfers between devices, exchange(): lax.ppermute(tail_stream, 'stream', [(i, i + 1) for i in range(streams -...  5.65 us
    ppermute x2, waiting for transfers between devices, exchange(): lax.ppermute(head_stream, 'stream', [(i + 1, i) for i in range(streams -...  5.52 us
  transfers between devices with their start and end apart: 9, of which 1 were waited for; matrix products, arithmetic and copies ran while one was open for 0% of the time, Pallas kernels for 25%

profile of v6, /device:TPU:17, one launch (start us, length us, event | category | flops | bytes accessed | tf_op | source)
XLA Modules:
  0.0 96.7 jit_solution(15992727498262030926)
XLA Ops:
  0.6 1.8 %faces.1 = (f32[4,32,128]{2,1,0:T(8,128)}, f32[4,32,128]{2,1,0:T(8,128)}, f32[4,64,128]{2,1,0:T(8,128)}, f32[4,64,128]{2,1,0:T(8,128)}) custom-call(f32[4,64,32,128]{3,2,1,0:T(8,128)} %flow.1), custom_call_target="tpu_custom_call" | custom-call | flops 1000 | bytes 1000000 | tf_op jit(solution)/shard_map/faces/pallas_call | solution.py:455
  2.4 1.3 %collective-permute-start.2 = (f32[4,64,128]{2,1,0:T(8,128)}, f32[4,64,128]{2,1,0:T(8,128)S(1)}, u32[]{:S(2)}, u32[]{:S(2)}) collective-permute-start(f32[4,64,128]{2,1,0:T(8,128)} %get-tuple-element.26), channel_id=1, source_target_pairs={{0,1},{1,2},{2,3},{3,4},{4,5},{5,6},{6,7},{7,8},{8,9},{9,10},{10,1... | collective-permute-start | bytes 393224 | tf_op jit(solution)/shard_map/ppermute | solution.py:530
  3.7 4.8 %collective-permute-start.3 = (f32[4,64,128]{2,1,0:T(8,128)}, f32[4,64,128]{2,1,0:T(8,128)S(1)}, u32[]{:S(2)}, u32[]{:S(2)}) collective-permute-start(f32[4,64,128]{2,1,0:T(8,128)} %get-tuple-element.27), channel_id=1, source_target_pairs={{1,0},{2,1},{3,2},{4,3},{5,4},{6,5},{7,6},{8,7},{9,8},{10,9},{11,1... | collective-permute-start | bytes 393224 | tf_op jit(solution)/shard_map/ppermute | solution.py:531
  8.6 3.7 %collective-permute-start = (f32[4,32,128]{2,1,0:T(8,128)}, f32[4,32,128]{2,1,0:T(8,128)S(1)}, u32[]{:S(2)}, u32[]{:S(2)}) collective-permute-start(f32[4,32,128]{2,1,0:T(8,128)} %get-tuple-element.24), channel_id=1, source_target_pairs={{0,16},{16,32},{32,48},{48,64},{64,80},{80,96},{96,112},{1,17},{17... | collective-permute-start | bytes 196616 | tf_op jit(solution)/shard_map/ppermute | solution.py:528
  12.3 1.9 %collective-permute-start.1 = (f32[4,32,128]{2,1,0:T(8,128)}, f32[4,32,128]{2,1,0:T(8,128)S(1)}, u32[]{:S(2)}, u32[]{:S(2)}) collective-permute-start(f32[4,32,128]{2,1,0:T(8,128)} %get-tuple-element.25), channel_id=1, source_target_pairs={{16,0},{32,16},{48,32},{64,48},{80,64},{96,80},{112,96},{17,1},{33... | collective-permute-start | bytes 196616 | tf_op jit(solution)/shard_map/ppermute | solution.py:529
  14.9 12.3 %first_bubbles.1 = (f32[128,24,128]{2,1,0:T(8,128)}, f32[512,128]{1,0:T(8,128)}, f32[512,128]{1,0:T(8,128)}) custom-call(s32[1]{0:T(128)S(6)} %copy.9.counts, s32[512]{0:T(512)} %order.1, s32[512]{0:T(512)} %tiles.4, f32[5,512,128]{2,1,0:T(8,128)} %bitcast.8, f32[4,2048,128]{2,1,0:T(8,128)} %bitcast.5, f32[4,2048,128]{2,1,0:T(8,128)} %bitcast.6), custom_call_target="tpu_custom_call" | custom-call | flops 1000000000 | bytes 100000000 | tf_op jit(solution)/shard_map/first_bubbles/pallas_call | solution.py:424
  27.2 0.0 collective-permute-done.stream_before
  27.2 0.0 collective-permute-done.1.stream_after
  27.2 0.0 collective-permute-done.2.azim_before
  27.2 0.0 collective-permute-done.3.azim_after
  27.2 0.0 copy-start
  27.2 0.0 copy-start.2
  27.2 0.0 copy-start.3
  27.2 10.8 %all-to-all-start = ((f32[128,24,128]{2,1,0:T(8,128)}), f32[128,24,128]{2,1,0:T(8,128)S(1)}, u32[]{:S(2)}, u32[]{:S(2)}) async-start(f32[128,24,128]{2,1,0:T(8,128)} %get-tuple-element.28), calls=%async_computation | async-start | bytes 3145728 | tf_op jit(solution)/shard_map/all_to_all | solution.py:542
  38.0 0.0 copy-done
  38.0 0.0 copy-done.2
  38.0 0.0 copy-done.3
  38.0 0.0 copy-start.1
  38.0 12.2 %first_flow.1 = (f32[4,2048,128]{2,1,0:T(8,128)}, f32[4,32,128]{2,1,0:T(8,128)S(1)}, f32[4,32,128]{2,1,0:T(8,128)S(1)}, f32[4,64,128]{2,1,0:T(8,128)S(1)}, f32[4,64,128]{2,1,0:T(8,128)S(1)}) custom-call(s32[1]{0:T(128)S(6)} %copy.9.counts, s32[512]{0:T(512)S(1)} %copy-done, f32[512,128]{1,0:T(8,128)S(1)} %copy-done.2, f32[512,128]{1,0:T(8,128)S(1)} %copy-done.3, ...), custom_call_target="tpu_custom_call" | custom-call | flops 1000000000 | bytes 80000000 | tf_op jit(solution)/shard_map/first_flow/pallas_call | solution.py:483
  50.2 5.6 %collective-permute-start.6 = (f32[4,64,128]{2,1,0:T(8,128)S(1)}, f32[4,64,128]{2,1,0:T(8,128)S(1)}, u32[]{:S(2)}, u32[]{:S(2)}) collective-permute-start(f32[4,64,128]{2,1,0:T(8,128)S(1)} %get-tuple-element.38), channel_id=1, source_target_pairs={{0,1},{1,2},{2,3},{3,4},{4,5},{5,6},{6,7},{7,8},{8,9},{9,10},{10,1... | collective-permute-start | bytes 393224 | tf_op jit(solution)/shard_map/ppermute | solution.py:530
  55.8 1.3 %collective-permute-start.7 = (f32[4,64,128]{2,1,0:T(8,128)S(1)}, f32[4,64,128]{2,1,0:T(8,128)S(1)}, u32[]{:S(2)}, u32[]{:S(2)}) collective-permute-start(f32[4,64,128]{2,1,0:T(8,128)S(1)} %get-tuple-element.39), channel_id=1, source_target_pairs={{1,0},{2,1},{3,2},{4,3},{5,4},{6,5},{7,6},{8,7},{9,8},{10,9},{11,1... | collective-permute-start | bytes 393224 | tf_op jit(solution)/shard_map/ppermute | solution.py:531
  57.2 1.9 %collective-permute-start.4 = (f32[4,32,128]{2,1,0:T(8,128)S(1)}, f32[4,32,128]{2,1,0:T(8,128)S(1)}, u32[]{:S(2)}, u32[]{:S(2)}) collective-permute-start(f32[4,32,128]{2,1,0:T(8,128)S(1)} %get-tuple-element.36), channel_id=1, source_target_pairs={{0,16},{16,32},{32,48},{48,64},{64,80},{80,96},{96,112},{1,17},{17... | collective-permute-start | bytes 196616 | tf_op jit(solution)/shard_map/ppermute | solution.py:528
  59.1 2.5 %collective-permute-start.5 = (f32[4,32,128]{2,1,0:T(8,128)S(1)}, f32[4,32,128]{2,1,0:T(8,128)S(1)}, u32[]{:S(2)}, u32[]{:S(2)}) collective-permute-start(f32[4,32,128]{2,1,0:T(8,128)S(1)} %get-tuple-element.37), channel_id=1, source_target_pairs={{16,0},{32,16},{48,32},{64,48},{80,64},{96,80},{112,96},{17,1},{33... | collective-permute-start | bytes 196616 | tf_op jit(solution)/shard_map/ppermute | solution.py:529
  61.7 0.0 collective-permute-done.4.stream_before
  61.7 5.5 %collective-permute-done.5.stream_after = f32[4,32,128]{2,1,0:T(8,128)S(1)} collective-permute-done((f32[4,32,128]{2,1,0:T(8,128)S(1)}, f32[4,32,128]{2,1,0:T(8,128)S(1)}, u32[]{:S(2)}, u32[]{:S(2)}) %collective-permute-start.5) | collective-permute-done | bytes 65568 | tf_op jit(solution)/shard_map/ppermute | solution.py:529
  67.2 0.0 collective-permute-done.6.azim_before
  67.2 0.0 collective-permute-done.7.azim_after
  67.2 0.0 all-to-all-done.packed
  67.2 0.0 copy-done.1
  67.2 29.5 %second_update.1 = (f32[4,2048,128]{2,1,0:T(8,128)}, f32[5,512,128]{2,1,0:T(8,128)}, f32[2048,128]{1,0:T(8,128)}) custom-call(s32[512]{0:T(512)S(1)} %copy-done.1, f32[128,24,128]{2,1,0:T(8,128)S(1)} %all-to-all-done.packed, f32[4,2048,128]{2,1,0:T(8,128)} %get-tuple-element.35.flow_in, f32[4,32,128]{2,1,0:T(8,128)S(1)} %collective-permute-done.4.stream_before, ...), custom_call_target="tpu_custom_call" | custom-call | flops 1000000000 | bytes 100000000 | tf_op jit(solution)/shard_map/second_update/pallas_call | solution.py:501
Async XLA Ops:
  2.4 24.7 %collective-permute-start.2 = (f32[4,64,128]{2,1,0:T(8,128)}, f32[4,64,128]{2,1,0:T(8,128)S(1)}, u32[]{:S(2)}, u32[]{:S(2)}) collective-permute-start(f32[4,64,128]{2,1,0:T(8,128)} %get-tuple-element.26), channel_id=1, source_target_pairs={{0,1},{1,2},{2,3},{3,4},{4,5},{5,6},{6,7},{7,8},{8,9},{9,10},{10,1... | collective-permute-start | bytes 393224 | tf_op jit(solution)/shard_map/ppermute | solution.py:530
  3.7 23.4 %collective-permute-start.3 = (f32[4,64,128]{2,1,0:T(8,128)}, f32[4,64,128]{2,1,0:T(8,128)S(1)}, u32[]{:S(2)}, u32[]{:S(2)}) collective-permute-start(f32[4,64,128]{2,1,0:T(8,128)} %get-tuple-element.27), channel_id=1, source_target_pairs={{1,0},{2,1},{3,2},{4,3},{5,4},{6,5},{7,6},{8,7},{9,8},{10,9},{11,1... | collective-permute-start | bytes 393224 | tf_op jit(solution)/shard_map/ppermute | solution.py:531
  8.6 18.6 %collective-permute-start = (f32[4,32,128]{2,1,0:T(8,128)}, f32[4,32,128]{2,1,0:T(8,128)S(1)}, u32[]{:S(2)}, u32[]{:S(2)}) collective-permute-start(f32[4,32,128]{2,1,0:T(8,128)} %get-tuple-element.24), channel_id=1, source_target_pairs={{0,16},{16,32},{32,48},{48,64},{64,80},{80,96},{96,112},{1,17},{17... | collective-permute-start | bytes 196616 | tf_op jit(solution)/shard_map/ppermute | solution.py:528
  12.3 14.9 %collective-permute-start.1 = (f32[4,32,128]{2,1,0:T(8,128)}, f32[4,32,128]{2,1,0:T(8,128)S(1)}, u32[]{:S(2)}, u32[]{:S(2)}) collective-permute-start(f32[4,32,128]{2,1,0:T(8,128)} %get-tuple-element.25), channel_id=1, source_target_pairs={{16,0},{32,16},{48,32},{64,48},{80,64},{96,80},{112,96},{17,1},{33... | collective-permute-start | bytes 196616 | tf_op jit(solution)/shard_map/ppermute | solution.py:529
  27.2 10.8 %copy-start = (s32[512]{0:T(512)S(1)}, s32[512]{0:T(512)}, u32[]{:S(2)}) copy-start(s32[512]{0:T(512)} %tiles.4) | copy-start | bytes 6148
  27.2 10.8 %copy-start.2 = (f32[512,128]{1,0:T(8,128)S(1)}, f32[512,128]{1,0:T(8,128)}, u32[]{:S(2)}) copy-start(f32[512,128]{1,0:T(8,128)} %get-tuple-element.29.places) | copy-start | bytes 786436
  27.2 10.8 %copy-start.3 = (f32[512,128]{1,0:T(8,128)S(1)}, f32[512,128]{1,0:T(8,128)}, u32[]{:S(2)}) copy-start(f32[512,128]{1,0:T(8,128)} %get-tuple-element.30.source) | copy-start | bytes 786436
  27.2 40.0 %all-to-all-start = ((f32[128,24,128]{2,1,0:T(8,128)}), f32[128,24,128]{2,1,0:T(8,128)S(1)}, u32[]{:S(2)}, u32[]{:S(2)}) async-start(f32[128,24,128]{2,1,0:T(8,128)} %get-tuple-element.28), calls=%async_computation | async-start | bytes 3145728 | tf_op jit(solution)/shard_map/all_to_all | solution.py:542
  38.0 29.2 %copy-start.1 = (s32[512]{0:T(512)S(1)}, s32[512]{0:T(512)}, u32[]{:S(2)}) copy-start(s32[512]{0:T(512)} %tiles.5) | copy-start | bytes 6148
  50.2 16.9 %collective-permute-start.6 = (f32[4,64,128]{2,1,0:T(8,128)S(1)}, f32[4,64,128]{2,1,0:T(8,128)S(1)}, u32[]{:S(2)}, u32[]{:S(2)}) collective-permute-start(f32[4,64,128]{2,1,0:T(8,128)S(1)} %get-tuple-element.38), channel_id=1, source_target_pairs={{0,1},{1,2},{2,3},{3,4},{4,5},{5,6},{6,7},{7,8},{8,9},{9,10},{10,1... | collective-permute-start | bytes 393224 | tf_op jit(solution)/shard_map/ppermute | solution.py:530
  55.8 11.4 %collective-permute-start.7 = (f32[4,64,128]{2,1,0:T(8,128)S(1)}, f32[4,64,128]{2,1,0:T(8,128)S(1)}, u32[]{:S(2)}, u32[]{:S(2)}) collective-permute-start(f32[4,64,128]{2,1,0:T(8,128)S(1)} %get-tuple-element.39), channel_id=1, source_target_pairs={{1,0},{2,1},{3,2},{4,3},{5,4},{6,5},{7,6},{8,7},{9,8},{10,9},{11,1... | collective-permute-start | bytes 393224 | tf_op jit(solution)/shard_map/ppermute | solution.py:531
  57.2 4.5 %collective-permute-start.4 = (f32[4,32,128]{2,1,0:T(8,128)S(1)}, f32[4,32,128]{2,1,0:T(8,128)S(1)}, u32[]{:S(2)}, u32[]{:S(2)}) collective-permute-start(f32[4,32,128]{2,1,0:T(8,128)S(1)} %get-tuple-element.36), channel_id=1, source_target_pairs={{0,16},{16,32},{32,48},{48,64},{64,80},{80,96},{96,112},{1,17},{17... | collective-permute-start | bytes 196616 | tf_op jit(solution)/shard_map/ppermute | solution.py:528
  59.1 8.1 %collective-permute-start.5 = (f32[4,32,128]{2,1,0:T(8,128)S(1)}, f32[4,32,128]{2,1,0:T(8,128)S(1)}, u32[]{:S(2)}, u32[]{:S(2)}) collective-permute-start(f32[4,32,128]{2,1,0:T(8,128)S(1)} %get-tuple-element.37), channel_id=1, source_target_pairs={{16,0},{32,16},{48,32},{64,48},{80,64},{96,80},{112,96},{17,1},{33... | collective-permute-start | bytes 196616 | tf_op jit(solution)/shard_map/ppermute | solution.py:529

commit v7 on v6

--- a/solution.py
+++ b/solution.py
@@ -34,6 +34,7 @@
 VMEM_MIB = 52
 WIDE_MIB = 58
 FIRST_BATCH = 64
+SPREAD_BATCH = 128
 SECOND_BATCH = 32
 CHUNK = 64
 SHARP = 0.5 / (KERNEL_WIDTH * KERNEL_WIDTH) * LOG2_E
@@ -239,7 +240,7 @@
     copies = flow_copies(flow_in, stream_before, stream_after, flow, in_sems)
     for copy in copies:
         copy.start()
-    size = FIRST_BATCH
+    size = SPREAD_BATCH
     live = counts[0]
     fill_cells(cells, scaled_cells)
     source_grid[...] = jnp.zeros_like(source_grid)

time: 97.5 us -> 98.5 us (1.010)
  the two profiles are of different devices: /device:TPU:17 before, /device:TPU:1 now
where the time goes in v7:
time: 98.5 us; the launch traced here: 96.9 us
  Pallas kernels  56.2 us (57%)
  starting transfers between devices  35.6 us (36%)
  waiting for transfers between devices  3.67 us (4%)
  between operations  1.44 us (1%)
    pallas_call x1, Pallas kernels, second_update(): pl.pallas_call(second_kernel, in_specs=[pl.BlockSpec(memory_space=SMEM),...  27.3 us
    pallas_call x1, Pallas kernels, first_bubbles(): pl.pallas_call(first_bubbles_kernel, grid=(1,), in_specs=[pl.BlockSpec(me...  13.8 us
    pallas_call x1, Pallas kernels, first_flow(): pl.pallas_call(first_flow_kernel, in_specs=[pl.BlockSpec(memory_space=SME...  13.2 us
    ppermute x2, starting transfers between devices, exchange(): lax.ppermute(head_azim, 'azim', [((i + 1) % azims, i) for i in range(azim...  13 us
    all_to_all x1, starting transfers between devices, on_device(): lax.all_to_all(packed, ('stream', 'azim'), split_axis=0, concat_axis=0, t...  9.09 us
    ppermute x2, starting transfers between devices, exchange(): lax.ppermute(tail_stream, 'stream', [(i, i + 1) for i in range(streams -...  7.41 us
    ppermute x2, starting transfers between devices, exchange(): lax.ppermute(head_stream, 'stream', [(i + 1, i) for i in range(streams -...  3.84 us
    ppermute x2, waiting for transfers between devices, exchange(): lax.ppermute(head_stream, 'stream', [(i + 1, i) for i in range(streams -...  3.65 us
  transfers between devices with their start and end apart: 9, of which 1 were waited for; matrix products, arithmetic and copies ran while one was open for 0% of the time, Pallas kernels for 28%

profile of v7, /device:TPU:1, one launch (start us, length us, event | category | flops | bytes accessed | tf_op | source)
XLA Modules:
  0.0 96.9 jit_solution(13139987404169244969)
XLA Ops:
  0.6 1.8 %faces.1 = (f32[4,32,128]{2,1,0:T(8,128)}, f32[4,32,128]{2,1,0:T(8,128)}, f32[4,64,128]{2,1,0:T(8,128)}, f32[4,64,128]{2,1,0:T(8,128)}) custom-call(f32[4,64,32,128]{3,2,1,0:T(8,128)} %flow.1), custom_call_target="tpu_custom_call" | custom-call | flops 1000 | bytes 1000000 | tf_op jit(solution)/shard_map/faces/pallas_call | solution.py:456
  2.4 2.1 %collective-permute-start.2 = (f32[4,64,128]{2,1,0:T(8,128)}, f32[4,64,128]{2,1,0:T(8,128)S(1)}, u32[]{:S(2)}, u32[]{:S(2)}) collective-permute-start(f32[4,64,128]{2,1,0:T(8,128)} %get-tuple-element.26), channel_id=1, source_target_pairs={{0,1},{1,2},{2,3},{3,4},{4,5},{5,6},{6,7},{7,8},{8,9},{9,10},{10,1... | collective-permute-start | bytes 393224 | tf_op jit(solution)/shard_map/ppermute | solution.py:531
  4.6 4.8 %collective-permute-start.3 = (f32[4,64,128]{2,1,0:T(8,128)}, f32[4,64,128]{2,1,0:T(8,128)S(1)}, u32[]{:S(2)}, u32[]{:S(2)}) collective-permute-start(f32[4,64,128]{2,1,0:T(8,128)} %get-tuple-element.27), channel_id=1, source_target_pairs={{1,0},{2,1},{3,2},{4,3},{5,4},{6,5},{7,6},{8,7},{9,8},{10,9},{11,1... | collective-permute-start | bytes 393224 | tf_op jit(solution)/shard_map/ppermute | solution.py:532
  9.4 4.0 %collective-permute-start = (f32[4,32,128]{2,1,0:T(8,128)}, f32[4,32,128]{2,1,0:T(8,128)S(1)}, u32[]{:S(2)}, u32[]{:S(2)}) collective-permute-start(f32[4,32,128]{2,1,0:T(8,128)} %get-tuple-element.24), channel_id=1, source_target_pairs={{0,16},{16,32},{32,48},{48,64},{64,80},{80,96},{96,112},{1,17},{17... | collective-permute-start | bytes 196616 | tf_op jit(solution)/shard_map/ppermute | solution.py:529
  13.4 1.9 %collective-permute-start.1 = (f32[4,32,128]{2,1,0:T(8,128)}, f32[4,32,128]{2,1,0:T(8,128)S(1)}, u32[]{:S(2)}, u32[]{:S(2)}) collective-permute-start(f32[4,32,128]{2,1,0:T(8,128)} %get-tuple-element.25), channel_id=1, source_target_pairs={{16,0},{32,16},{48,32},{64,48},{80,64},{96,80},{112,96},{17,1},{33... | collective-permute-start | bytes 196616 | tf_op jit(solution)/shard_map/ppermute | solution.py:530
  16.0 13.8 %first_bubbles.1 = (f32[128,24,128]{2,1,0:T(8,128)}, f32[512,128]{1,0:T(8,128)}, f32[512,128]{1,0:T(8,128)}) custom-call(s32[1]{0:T(128)S(6)} %copy.9.counts, s32[512]{0:T(512)} %order.1, s32[512]{0:T(512)} %tiles.4, f32[5,512,128]{2,1,0:T(8,128)} %bitcast.8, f32[4,2048,128]{2,1,0:T(8,128)} %bitcast.5, f32[4,2048,128]{2,1,0:T(8,128)} %bitcast.6), custom_call_target="tpu_custom_call" | custom-call | flops 1000000000 | bytes 100000000 | tf_op jit(solution)/shard_map/first_bubbles/pallas_call | solution.py:425
  29.8 0.0 collective-permute-done.stream_before
  29.8 0.0 collective-permute-done.1.stream_after
  29.9 0.0 collective-permute-done.2.azim_before
  29.9 0.0 collective-permute-done.3.azim_after
  29.9 0.0 copy-start
  29.9 0.0 copy-start.2
  29.9 0.0 copy-start.3
  29.9 9.1 %all-to-all-start = ((f32[128,24,128]{2,1,0:T(8,128)}), f32[128,24,128]{2,1,0:T(8,128)S(1)}, u32[]{:S(2)}, u32[]{:S(2)}) async-start(f32[128,24,128]{2,1,0:T(8,128)} %get-tuple-element.28), calls=%async_computation | async-start | bytes 3145728 | tf_op jit(solution)/shard_map/all_to_all | solution.py:543
  39.0 0.0 copy-done
  39.0 0.0 copy-done.2
  39.0 0.0 copy-done.3
  39.0 0.0 copy-start.1
  39.1 13.2 %first_flow.1 = (f32[4,2048,128]{2,1,0:T(8,128)}, f32[4,32,128]{2,1,0:T(8,128)S(1)}, f32[4,32,128]{2,1,0:T(8,128)S(1)}, f32[4,64,128]{2,1,0:T(8,128)S(1)}, f32[4,64,128]{2,1,0:T(8,128)S(1)}) custom-call(s32[1]{0:T(128)S(6)} %copy.9.counts, s32[512]{0:T(512)S(1)} %copy-done, f32[512,128]{1,0:T(8,128)S(1)} %copy-done.2, f32[512,128]{1,0:T(8,128)S(1)} %copy-done.3, ...), custom_call_target="tpu_custom_call" | custom-call | flops 1000000000 | bytes 80000000 | tf_op jit(solution)/shard_map/first_flow/pallas_call | solution.py:484
  52.3 0.1 collective-permute-start.6
  52.4 8.2 %collective-permute-start.7 = (f32[4,64,128]{2,1,0:T(8,128)S(1)}, f32[4,64,128]{2,1,0:T(8,128)S(1)}, u32[]{:S(2)}, u32[]{:S(2)}) collective-permute-start(f32[4,64,128]{2,1,0:T(8,128)S(1)} %get-tuple-element.39), channel_id=1, source_target_pairs={{1,0},{2,1},{3,2},{4,3},{5,4},{6,5},{7,6},{8,7},{9,8},{10,9},{11,1... | collective-permute-start | bytes 393224 | tf_op jit(solution)/shard_map/ppermute | solution.py:532
  60.6 3.4 %collective-permute-start.4 = (f32[4,32,128]{2,1,0:T(8,128)S(1)}, f32[4,32,128]{2,1,0:T(8,128)S(1)}, u32[]{:S(2)}, u32[]{:S(2)}) collective-permute-start(f32[4,32,128]{2,1,0:T(8,128)S(1)} %get-tuple-element.36), channel_id=1, source_target_pairs={{0,16},{16,32},{32,48},{48,64},{64,80},{80,96},{96,112},{1,17},{17... | collective-permute-start | bytes 196616 | tf_op jit(solution)/shard_map/ppermute | solution.py:529
  64.0 1.9 %collective-permute-start.5 = (f32[4,32,128]{2,1,0:T(8,128)S(1)}, f32[4,32,128]{2,1,0:T(8,128)S(1)}, u32[]{:S(2)}, u32[]{:S(2)}) collective-permute-start(f32[4,32,128]{2,1,0:T(8,128)S(1)} %get-tuple-element.37), channel_id=1, source_target_pairs={{16,0},{32,16},{48,32},{64,48},{80,64},{96,80},{112,96},{17,1},{33... | collective-permute-start | bytes 196616 | tf_op jit(solution)/shard_map/ppermute | solution.py:530
  65.9 0.0 collective-permute-done.4.stream_before
  65.9 3.6 %collective-permute-done.5.stream_after = f32[4,32,128]{2,1,0:T(8,128)S(1)} collective-permute-done((f32[4,32,128]{2,1,0:T(8,128)S(1)}, f32[4,32,128]{2,1,0:T(8,128)S(1)}, u32[]{:S(2)}, u32[]{:S(2)}) %collective-permute-start.5) | collective-permute-done | bytes 65568 | tf_op jit(solution)/shard_map/ppermute | solution.py:530
  69.6 0.0 collective-permute-done.6.azim_before
  69.6 0.0 collective-permute-done.7.azim_after
  69.6 0.0 all-to-all-done.packed
  69.6 0.0 copy-done.1
  69.6 27.3 %second_update.1 = (f32[4,2048,128]{2,1,0:T(8,128)}, f32[5,512,128]{2,1,0:T(8,128)}, f32[2048,128]{1,0:T(8,128)}) custom-call(s32[512]{0:T(512)S(1)} %copy-done.1, f32[128,24,128]{2,1,0:T(8,128)S(1)} %all-to-all-done.packed, f32[4,2048,128]{2,1,0:T(8,128)} %get-tuple-element.35.flow_in, f32[4,32,128]{2,1,0:T(8,128)S(1)} %collective-permute-done.4.stream_before, ...), custom_call_target="tpu_custom_call" | custom-call | flops 1000000000 | bytes 100000000 | tf_op jit(solution)/shard_map/second_update/pallas_call | solution.py:502
Async XLA Ops:
  2.4 27.4 %collective-permute-start.2 = (f32[4,64,128]{2,1,0:T(8,128)}, f32[4,64,128]{2,1,0:T(8,128)S(1)}, u32[]{:S(2)}, u32[]{:S(2)}) collective-permute-start(f32[4,64,128]{2,1,0:T(8,128)} %get-tuple-element.26), channel_id=1, source_target_pairs={{0,1},{1,2},{2,3},{3,4},{4,5},{5,6},{6,7},{7,8},{8,9},{9,10},{10,1... | collective-permute-start | bytes 393224 | tf_op jit(solution)/shard_map/ppermute | solution.py:531
  4.6 25.3 %collective-permute-start.3 = (f32[4,64,128]{2,1,0:T(8,128)}, f32[4,64,128]{2,1,0:T(8,128)S(1)}, u32[]{:S(2)}, u32[]{:S(2)}) collective-permute-start(f32[4,64,128]{2,1,0:T(8,128)} %get-tuple-element.27), channel_id=1, source_target_pairs={{1,0},{2,1},{3,2},{4,3},{5,4},{6,5},{7,6},{8,7},{9,8},{10,9},{11,1... | collective-permute-start | bytes 393224 | tf_op jit(solution)/shard_map/ppermute | solution.py:532
  9.4 20.5 %collective-permute-start = (f32[4,32,128]{2,1,0:T(8,128)}, f32[4,32,128]{2,1,0:T(8,128)S(1)}, u32[]{:S(2)}, u32[]{:S(2)}) collective-permute-start(f32[4,32,128]{2,1,0:T(8,128)} %get-tuple-element.24), channel_id=1, source_target_pairs={{0,16},{16,32},{32,48},{48,64},{64,80},{80,96},{96,112},{1,17},{17... | collective-permute-start | bytes 196616 | tf_op jit(solution)/shard_map/ppermute | solution.py:529
  13.4 16.4 %collective-permute-start.1 = (f32[4,32,128]{2,1,0:T(8,128)}, f32[4,32,128]{2,1,0:T(8,128)S(1)}, u32[]{:S(2)}, u32[]{:S(2)}) collective-permute-start(f32[4,32,128]{2,1,0:T(8,128)} %get-tuple-element.25), channel_id=1, source_target_pairs={{16,0},{32,16},{48,32},{64,48},{80,64},{96,80},{112,96},{17,1},{33... | collective-permute-start | bytes 196616 | tf_op jit(solution)/shard_map/ppermute | solution.py:530
  29.9 9.1 %copy-start = (s32[512]{0:T(512)S(1)}, s32[512]{0:T(512)}, u32[]{:S(2)}) copy-start(s32[512]{0:T(512)} %tiles.4) | copy-start | bytes 6148
  29.9 9.1 %copy-start.2 = (f32[512,128]{1,0:T(8,128)S(1)}, f32[512,128]{1,0:T(8,128)}, u32[]{:S(2)}) copy-start(f32[512,128]{1,0:T(8,128)} %get-tuple-element.29.places) | copy-start | bytes 786436
  29.9 9.1 %copy-start.3 = (f32[512,128]{1,0:T(8,128)S(1)}, f32[512,128]{1,0:T(8,128)}, u32[]{:S(2)}) copy-start(f32[512,128]{1,0:T(8,128)} %get-tuple-element.30.source) | copy-start | bytes 786436
  29.9 39.7 %all-to-all-start = ((f32[128,24,128]{2,1,0:T(8,128)}), f32[128,24,128]{2,1,0:T(8,128)S(1)}, u32[]{:S(2)}, u32[]{:S(2)}) async-start(f32[128,24,128]{2,1,0:T(8,128)} %get-tuple-element.28), calls=%async_computation | async-start | bytes 3145728 | tf_op jit(solution)/shard_map/all_to_all | solution.py:543
  39.0 30.5 %copy-start.1 = (s32[512]{0:T(512)S(1)}, s32[512]{0:T(512)}, u32[]{:S(2)}) copy-start(s32[512]{0:T(512)} %tiles.5) | copy-start | bytes 6148
  52.3 17.3 %collective-permute-start.6 = (f32[4,64,128]{2,1,0:T(8,128)S(1)}, f32[4,64,128]{2,1,0:T(8,128)S(1)}, u32[]{:S(2)}, u32[]{:S(2)}) collective-permute-start(f32[4,64,128]{2,1,0:T(8,128)S(1)} %get-tuple-element.38), channel_id=1, source_target_pairs={{0,1},{1,2},{2,3},{3,4},{4,5},{5,6},{6,7},{7,8},{8,9},{9,10},{10,1... | collective-permute-start | bytes 393224 | tf_op jit(solution)/shard_map/ppermute | solution.py:531
  52.4 17.2 %collective-permute-start.7 = (f32[4,64,128]{2,1,0:T(8,128)S(1)}, f32[4,64,128]{2,1,0:T(8,128)S(1)}, u32[]{:S(2)}, u32[]{:S(2)}) collective-permute-start(f32[4,64,128]{2,1,0:T(8,128)S(1)} %get-tuple-element.39), channel_id=1, source_target_pairs={{1,0},{2,1},{3,2},{4,3},{5,4},{6,5},{7,6},{8,7},{9,8},{10,9},{11,1... | collective-permute-start | bytes 393224 | tf_op jit(solution)/shard_map/ppermute | solution.py:532
  60.6 5.3 %collective-permute-start.4 = (f32[4,32,128]{2,1,0:T(8,128)S(1)}, f32[4,32,128]{2,1,0:T(8,128)S(1)}, u32[]{:S(2)}, u32[]{:S(2)}) collective-permute-start(f32[4,32,128]{2,1,0:T(8,128)S(1)} %get-tuple-element.36), channel_id=1, source_target_pairs={{0,16},{16,32},{32,48},{48,64},{64,80},{80,96},{96,112},{1,17},{17... | collective-permute-start | bytes 196616 | tf_op jit(solution)/shard_map/ppermute | solution.py:529
  64.0 5.6 %collective-permute-start.5 = (f32[4,32,128]{2,1,0:T(8,128)S(1)}, f32[4,32,128]{2,1,0:T(8,128)S(1)}, u32[]{:S(2)}, u32[]{:S(2)}) collective-permute-start(f32[4,32,128]{2,1,0:T(8,128)S(1)} %get-tuple-element.37), channel_id=1, source_target_pairs={{16,0},{32,16},{48,32},{64,48},{80,64},{96,80},{112,96},{17,1},{33... | collective-permute-start | bytes 196616 | tf_op jit(solution)/shard_map/ppermute | solution.py:530
